TPU v7x, 256 devices: a whole 4x4x8 slice. The times are simulated.
256 devices in a mesh: ctx: 16 (over x, y_hi, core), exp: 16 (over y_lo, z).
Axes of the slice: x: 4, y: 4 (y_hi: 2, y_lo: 2; y = y_hi * 2 + y_lo), z: 8, core: 2. Of those that a mesh axis runs over, the one named last changes fastest.
Arguments:
- query: bfloat16 [16, 2048, 12288], P('exp', 'ctx'), may hold values from -8 to 8
- out_grad: bfloat16 [16, 2048, 8192], P('exp', 'ctx'), may hold values from -6 to 6
- latent: bfloat16 [16, 2048, 512], P('exp', 'ctx'), may hold values from -6 to 6
- rope_key: bfloat16 [16, 2048, 64], P('exp', 'ctx'), may hold values from -8 to 8
- w_key: bfloat16 [512, 8192], P(None, 'ctx'), may hold values from -0.25 to 0.25
- w_value: bfloat16 [512, 8192], P(None, 'ctx'), may hold values from -0.25 to 0.25
- grad_stream: bfloat16 [16, 2048, 5120], P('exp', 'ctx'), may hold values from -6 to 6
- expert_ids: int32 [16, 2048, 6], P('exp', 'ctx'), may hold values from 0 to 159, all different within a row; in each aligned block of 128 rows (0 to 127, 128 to 255, ..., all dimensions but the last counted through in order) at most 6 rows name the same one
- gate_weights: bfloat16 [16, 2048, 6], P('exp', 'ctx'), may hold values from 0.049804688 to 0.5
- saved_hidden: bfloat16 [16, 16, 96, 1536], P('ctx', 'exp'), may hold values from -6 to 6
- w_down: bfloat16 [16, 1536, 5120], P('exp', None, 'ctx'), may hold values from -0.15625 to 0.15625
Outputs:
- query_grad: bfloat16 [16, 2048, 12288], P('exp', 'ctx')
- latent_grad: bfloat16 [16, 2048, 512], P('exp', 'ctx')
- rope_grad: bfloat16 [16, 2048, 64], P('exp', 'ctx')
- hidden_grad: bfloat16 [16, 16, 96, 1536], P('ctx', 'exp')
- gate_grad: float32 [16, 2048, 6], P('exp', 'ctx')
Inputs may be any that keep to these rules, and one draw needn't show every extreme that they name: `expert_ids`: each token names 6 distinct experts; within the 128 tokens of one device no expert is named by more than 6 tokens, a bound that some block reaches.
All inputs are finite; a program needn't handle non-finite values.
Results may differ from a plain program's by a relative error of at most 0.015.
Values may be sent and summed in bfloat16 or wider, within the bound.
No kernel may reach another device: no remote copies, remote signals or barrier semaphores. Data moves between devices by JAX's collectives and lax.ppermute only.
A program may use at most 192 MiB of HBM per device.

v0:
```python
import jax
import jax.numpy as jnp
from jax import lax
from jax.sharding import PartitionSpec as P

HEADS = 64
NOPE = 128
ROPE = 64
VDIM = 128
LATENT = 512
FFH = 1536
EXPERTS = 160
TOPK = 6
WIN = 32
CAP = 6


def from_behind(shard, axis, by):
    size = lax.axis_size(axis)
    pairs = [(i, i + by) for i in range(size) if 0 <= i + by < size]
    return lax.ppermute(shard, axis, pairs)


def route_plan(expert_ids, owners, capacity):
    share = EXPERTS // owners
    flat_ids = expert_ids.reshape(-1)
    active = flat_ids % share == 0
    owner_of = jnp.where(active, flat_ids // share, -1)
    owner_hot = (owner_of[:, None] == jnp.arange(owners, dtype=jnp.int32)[None, :]).astype(
        jnp.int32
    )
    earlier = jnp.cumsum(owner_hot, axis=0) - owner_hot
    slot_of = jnp.sum(earlier * owner_hot, axis=1)
    target = jnp.where(active, owner_of * capacity + slot_of, -1)
    slot_ids = jnp.arange(owners * capacity, dtype=jnp.int32)
    return (target[:, None] == slot_ids[None, :]).astype(jnp.float32)


def window_mask(block_index, rows):
    query_rel = jnp.arange(rows, dtype=jnp.int32)[:, None]
    key_rel = jnp.arange(2 * rows, dtype=jnp.int32)[None, :]
    inside = (key_rel > query_rel) & (key_rel <= query_rel + rows)
    return inside & ((block_index > 0) | (key_rel >= rows))


def window_grads(q_nope, q_rope, d_out, keys, values, rope_rows, key_cols, value_cols, allowed):
    score_scale = (NOPE + ROPE) ** (-0.5)
    raw_scores = jnp.einsum("ihd,jhd->hij", q_nope, keys, preferred_element_type=jnp.float32)
    raw_scores = raw_scores + jnp.einsum(
        "ihd,jd->hij", q_rope, rope_rows, preferred_element_type=jnp.float32
    )
    scores = jnp.where(allowed[None], score_scale * raw_scores, -jnp.inf)
    row_max = jnp.max(scores, axis=2, keepdims=True)
    shifted = jnp.exp(scores - row_max)
    probs = shifted / jnp.sum(shifted, axis=2, keepdims=True)
    prob_grad = jnp.einsum("ihd,jhd->hij", d_out, values, preferred_element_type=jnp.float32)
    delta = jnp.sum(probs * prob_grad, axis=2, keepdims=True)
    score_grad = (score_scale * probs * (prob_grad - delta)).astype(jnp.bfloat16)
    probs_low = probs.astype(jnp.bfloat16)
    grad_nope = jnp.einsum("hij,jhd->ihd", score_grad, keys, preferred_element_type=jnp.float32)
    grad_rope = jnp.einsum("hij,jd->ihd", score_grad, rope_rows, preferred_element_type=jnp.float32)
    key_count = keys.shape[0]
    key_part = jnp.einsum(
        "hij,ihd->jhd", score_grad, q_nope, preferred_element_type=jnp.float32
    ).astype(jnp.bfloat16)
    value_part = jnp.einsum(
        "hij,ihd->jhd", probs_low, d_out, preferred_element_type=jnp.float32
    ).astype(jnp.bfloat16)
    contract = (((1,), (1,)), ((), ()))
    latent_part = lax.dot_general(
        key_part.reshape(key_count, -1), key_cols, contract, preferred_element_type=jnp.float32
    )
    latent_part = latent_part + lax.dot_general(
        value_part.reshape(key_count, -1), value_cols, contract, preferred_element_type=jnp.float32
    )
    rope_part = jnp.einsum("hij,ihd->jd", score_grad, q_rope, preferred_element_type=jnp.float32)
    return (jnp.concatenate([grad_nope, grad_rope], axis=2), latent_part, rope_part)


def tile_pairs(rows_all, tiles):
    before = rows_all[: tiles * WIN].reshape(tiles, WIN, -1)
    own = rows_all[WIN:].reshape(tiles, WIN, -1)
    return jnp.concatenate([before, own], axis=1)


def fold_tiles(parts, width):
    later = jnp.concatenate([parts[1:, :WIN], jnp.zeros((1, WIN, width), jnp.float32)], axis=0)
    return parts[:, WIN:] + later


def local(
    query,
    out_grad,
    latent,
    rope_key,
    w_key,
    w_value,
    grad_stream,
    expert_ids,
    gate_weights,
    saved_hidden,
    w_down,
):
    tok_rows = query.shape[1]
    owners = lax.axis_size("exp")
    ctx_index = lax.axis_index("ctx")
    grads_fn = jax.vmap(window_grads, in_axes=(0, 0, 0, 0, 0, 0, None, None, 0))
    tiles = tok_rows // WIN
    q_all = query[0].reshape(tok_rows, HEADS, NOPE + ROPE)
    d_all = out_grad[0].reshape(tok_rows, HEADS, VDIM)
    prev_latent, prev_rope = from_behind(
        (latent[0][tok_rows - WIN :], rope_key[0][tok_rows - WIN :]), "ctx", 1
    )
    pair_latent = jnp.concatenate([prev_latent, latent[0]], axis=0)
    pair_rope = jnp.concatenate([prev_rope, rope_key[0]], axis=0)
    rope_tiles = tile_pairs(pair_rope, tiles)
    masks = jax.vmap(lambda index: window_mask(ctx_index * tiles + index, WIN))(
        jnp.arange(tiles, dtype=jnp.int32)
    )
    key_cols = lax.all_gather(w_key, "ctx", axis=1, tiled=True)
    value_cols = lax.all_gather(w_value, "ctx", axis=1, tiled=True)
    count = key_cols.shape[1] // NOPE
    keys = jnp.dot(pair_latent, key_cols, preferred_element_type=jnp.float32).astype(jnp.bfloat16)
    values = jnp.dot(pair_latent, value_cols, preferred_element_type=jnp.float32).astype(
        jnp.bfloat16
    )
    key_tiles = tile_pairs(keys, tiles).reshape(tiles, 2 * WIN, count, NOPE)
    value_tiles = tile_pairs(values, tiles).reshape(tiles, 2 * WIN, count, VDIM)
    q_part = q_all.reshape(tiles, WIN, count, NOPE + ROPE)
    d_part = d_all.reshape(tiles, WIN, count, VDIM)
    query_part, latent_part, rope_part = grads_fn(
        q_part[..., :NOPE],
        q_part[..., NOPE:],
        d_part,
        key_tiles,
        value_tiles,
        rope_tiles,
        key_cols,
        value_cols,
        masks,
    )
    query_acc = query_part.reshape(tok_rows, count, NOPE + ROPE)
    latent_acc, rope_acc, query_acc = (latent_part, rope_part, query_acc)
    back_latent, back_rope = from_behind((latent_acc[0, :WIN], rope_acc[0, :WIN]), "ctx", -1)
    latent_own = fold_tiles(latent_acc, LATENT).reshape(tok_rows, LATENT)
    rope_own = fold_tiles(rope_acc, ROPE).reshape(tok_rows, ROPE)
    latent_own = latent_own + jnp.concatenate(
        [jnp.zeros((tok_rows - WIN, LATENT), jnp.float32), back_latent], axis=0
    )
    rope_own = rope_own + jnp.concatenate(
        [jnp.zeros((tok_rows - WIN, ROPE), jnp.float32), back_rope], axis=0
    )
    latent_grad = latent_own.astype(jnp.bfloat16).reshape(1, tok_rows, LATENT)
    rope_grad = rope_own.astype(jnp.bfloat16).reshape(1, tok_rows, ROPE)
    query_grad = query_acc.reshape(1, tok_rows, -1).astype(jnp.bfloat16)
    slot_hot = route_plan(expert_ids[0], owners, CAP)
    token_hot = slot_hot.reshape(tok_rows, TOPK, -1).sum(axis=1).astype(jnp.bfloat16)
    stream_grad = grad_stream[0]
    outbound = lax.dot_general(
        token_hot, stream_grad, (((0,), (0,)), ((), ())), preferred_element_type=jnp.float32
    )
    outbound = outbound.astype(jnp.bfloat16).reshape(owners, CAP, -1)
    gate_send = jnp.sum(slot_hot * gate_weights[0].reshape(-1, 1).astype(jnp.float32), axis=0)
    gate_send = gate_send.astype(jnp.bfloat16).reshape(owners, CAP)
    routed, row_gate = (
        lax.all_to_all(outbound, "exp", split_axis=0, concat_axis=0, tiled=True),
        lax.all_to_all(gate_send, "exp", split_axis=0, concat_axis=0, tiled=True),
    )
    routed = routed.reshape(owners * CAP, -1)
    down_local = w_down[0]
    routed_count = routed.shape[0]
    raw_grad = lax.dot_general(
        routed,
        lax.all_gather(down_local, "ctx", axis=1, tiled=True),
        (((1,), (1,)), ((), ())),
        preferred_element_type=jnp.float32,
    )
    hidden_rows = saved_hidden[0, 0]
    gate_part = jnp.sum(hidden_rows.astype(jnp.float32) * raw_grad, axis=1)
    hidden_grad = (
        (row_gate.reshape(-1, 1).astype(jnp.float32) * raw_grad)
        .astype(jnp.bfloat16)
        .reshape(1, 1, routed_count, FFH)
    )
    returned = lax.all_to_all(
        gate_part.reshape(owners, CAP), "exp", split_axis=0, concat_axis=0, tiled=True
    )
    gate_grad = jnp.sum(slot_hot * returned.reshape(1, -1), axis=1).reshape(1, tok_rows, TOPK)
    return (query_grad, latent_grad, rope_grad, hidden_grad, gate_grad)


def solution(mesh):
    in_specs = (
        P("exp", "ctx", None),
        P("exp", "ctx", None),
        P("exp", "ctx", None),
        P("exp", "ctx", None),
        P(None, "ctx"),
        P(None, "ctx"),
        P("exp", "ctx", None),
        P("exp", "ctx", None),
        P("exp", "ctx", None),
        P("ctx", "exp", None, None),
        P("exp", None, "ctx"),
    )
    out_specs = (
        P("exp", "ctx", None),
        P("exp", "ctx", None),
        P("exp", "ctx", None),
        P("ctx", "exp", None, None),
        P("exp", "ctx", None),
    )
    return jax.shard_map(local, mesh=mesh, in_specs=in_specs, out_specs=out_specs, check_vma=False)
```

profile of v0, /device:TPU:2, one launch (start us, length us, event | category | flops | bytes accessed | tf_op | source)
XLA Modules:
  0.0 372.6 jit_solution(130135387121931267)
XLA Ops:
  11.2 1.7 reduce-window.6
  14.0 1.2 reshape.295
  15.3 9.6 %all-to-all-start.1 = ((bf16[16,6,5120]{2,1,0:T(8,128)(2,1)}), bf16[16,6,5120]{2,1,0:T(8,128)(2,1)S(1)}, u32[]{:S(2)}, u32[]{:S(2)}) async-start(bf16[16,6,5120]{2,1,0:T(8,128)(2,1)} %reshape.295), calls=%async_computation.1 | async-start | bytes 2621440 | tf_op jit(solution)/shard_map/all_to_all | solution.py:166
  25.5 1.9 collective-permute-start
  28.1 4.9 %collective-permute-start.1 = (bf16[32,64]{0,1:T(8,128)(2,1)}, bf16[32,64]{0,1:T(8,128)(2,1)}, u32[]{:S(2)}, u32[]{:S(2)}) collective-permute-start(bf16[32,64]{0,1:T(8,128)(2,1)} %slice_bitcast_fusion.7), channel_id=1, source_target_pairs={{0,16},{16,32},{32,48},{48,64},{64,80},{80,96},{96,112},{112,128},... | collective-permute-start | bytes 12296 | tf_op jit(solution)/shard_map/ppermute | solution.py:21
  34.4 7.4 %reshape_reshape_squeeze.6 = bf16[4,32,64,192]{3,2,1,0:T(8,128)(2,1)} reshape(bf16[1,128,12288]{2,1,0:T(8,128)(2,1)} %param.11) | data formatting | bytes 6291456 | tf_op jit(solution)/shard_map/reshape;reshape;squeeze | solution.py:129
  41.9 2.0 slice.78
  43.8 0.9 copy-done.6
  44.8 2.0 slice.79
  47.5 3.5 copy.120
  51.0 1.4 copy.101
  52.4 1.6 reshape.299
  54.0 1.4 pad_maximum_fusion.4
  55.4 1.4 copy.85
  57.4 1.5 reshape.296
  58.9 42.6 %all-gather.5.cloned.1.call-done = bf16[512,8192]{1,0:T(8,128)(2,1)} async-done(((bf16[512,512]{1,0:T(8,128)(2,1)}), bf16[512,8192]{1,0:T(8,128)(2,1)}) %all-gather.5.cloned.1.call-update) | async-done | bytes 8388624 | tf_op jit(solution)/shard_map/all_gather | solution.py:120
  101.5 4.9 %convolution_convert_fusion.1 = bf16[160,8192]{1,0:T(8,128)(2,1)S(1)} fusion(bf16[512,8192]{1,0:T(8,128)(2,1)} %all-gather.5.cloned.1.call-done, bf16[128,512]{1,0:T(8,128)(2,1)S(1)} %bitcast.169, bf16[32,512]{1,0:T(8,128)(2,1)} %collective-permute-done), kind=kOutput, calls=%fused_computation.4 | convolution fusion | flops 1343815680 | bytes 11173888 | tf_op jit(solution)/shard_map/dot_general | solution.py:123
  107.3 1.9 copy.116
  109.2 1.9 copy.117
  111.1 76.7 %all-gather.7.cloned.1.call-done = bf16[512,8192]{1,0:T(8,128)(2,1)} async-done(((bf16[512,512]{1,0:T(8,128)(2,1)}), bf16[512,8192]{1,0:T(8,128)(2,1)}) %all-gather.7.cloned.1.call-update) | async-done | bytes 8388624 | tf_op jit(solution)/shard_map/all_gather | solution.py:121
  187.8 4.9 %convolution_convert_fusion = bf16[160,8192]{1,0:T(8,128)(2,1)S(1)} fusion(bf16[512,8192]{1,0:T(8,128)(2,1)} %all-gather.7.cloned.1.call-done, bf16[128,512]{1,0:T(8,128)(2,1)S(1)} %bitcast.170, bf16[32,512]{1,0:T(8,128)(2,1)} %collective-permute-done), kind=kOutput, calls=%fused_computation.3 | convolution fusion | flops 1343815680 | bytes 11173888 | tf_op jit(solution)/shard_map/dot_general | solution.py:124
  192.7 0.9 slice_bitcast_fusion.1
  194.2 1.4 copy.88
  196.2 1.4 copy.89
  197.6 1.4 copy_dynamic-update-slice_fusion.1
  199.0 1.5 copy_dynamic-update-slice_fusion
  200.6 13.9 %fusion.25 = f32[4,64,64,32]{2,3,1,0:T(8,128)S(1)} fusion(bf16[4,64,64,128]{3,1,2,0:T(8,128)(2,1)S(1)} %copy_dynamic-update-slice_fusion, bf16[4,32,64,128]{3,2,1,0:T(8,128)(2,1)S(1)} %slice.78), kind=kOutput, calls=%fused_computation.44 | convolution fusion | flops 134217728 | bytes 8388608 | tf_op jit(solution)/shard_map/vmap(ihd,jhd->hij)/dot_general | solution.py:48
  214.5 2.5 fusion.19
  217.0 43.2 %fusion.63 = (f32[4,64,32]{2,1,0:T(8,128)S(1)}, f32[4,64,32,64]{3,2,1,0:T(8,128)S(1)}) fusion(f32[4,64,32,64]{3,2,1,0:T(8,128)S(1)} %fusion.19), kind=kOutput, calls=%fused_computation.121 | output fusion | flops 1048639 | bytes 4227072 | tf_op jit(solution)/shard_map/vmap()/sub | solution.py:54
  260.3 6.5 %fusion.15 = (f32[4,64,32]{2,1,0:T(8,128)S(1)}, f32[4,64,64,32]{2,3,1,0:T(8,128)S(1)}) fusion(f32[4,64,32,64]{3,2,1,0:T(8,128)S(1)} %get-tuple-element.34, f32[4,64,32]{2,1,0:T(8,128)S(1)} %get-tuple-element.33, bf16[4,32,64,128]{3,2,1,0:T(8,128)(2,1)S(1)} %bitcast.168, bf16[4,32,64,128]{3,1,2,0:T(8,128)(2,1)S(1)} %copy.89, ...), kind=kOutput, calls=%fused_computation.21 | convolution fusion | flops 144171008 | bytes 10551296 | tf_op jit(solution)/shard_map/vmap(ihd,jhd->hij)/dot_general | solution.py:56
  266.8 2.6 fusion.17
  269.4 1.5 fusion.35
  270.9 2.6 collective-permute-start.3
  273.5 21.3 %convert_bitcast_fusion = bf16[4,64,8,8,128]{4,3,2,1,0:T(8,128)(2,1)} fusion(bf16[4,32,64,128]{3,2,1,0:T(8,128)(2,1)} %bitcast.167, f32[4,64,32]{2,1,0:T(8,128)S(1)} %get-tuple-element.33, f32[4,64,32,64]{3,2,1,0:T(8,128)} %copy-done.5), kind=kOutput, calls=%fused_computation.27 | convolution fusion | flops 137896000 | bytes 8421376 | tf_op jit(solution)/shard_map/vmap(hij,ihd->jhd)/dot_general | solution.py:66
  294.8 3.9 %convert_bitcast_fusion.1 = bf16[4,64,8,8,128]{4,3,2,1,0:T(8,128)(2,1)S(1)} fusion(bf16[4,64,32,64]{3,2,1,0:T(8,128)(2,1)S(1)} %fusion.17, bf16[4,32,64,128]{3,2,1,0:T(8,128)(2,1)} %copy-done.4), kind=kOutput, calls=%fused_computation.28 | convolution fusion | flops 136314880 | bytes 7340032 | tf_op jit(solution)/shard_map/vmap(hij,ihd->jhd)/dot_general | solution.py:63
  298.8 6.0 %fusion.3 = f32[4,64,512]{2,1,0:T(8,128)S(1)} fusion(bf16[512,8192]{1,0:T(8,128)(2,1)} %all-gather.7.cloned.1.call-done, bf16[4,64,8,8,128]{4,3,2,1,0:T(8,128)(2,1)S(1)} %copy-done.20), kind=kOutput, calls=%fused_computation.5 | convolution fusion | flops 2147483648 | bytes 13107200 | tf_op jit(solution)/shard_map/vmap()/dot_general | solution.py:73
  304.8 2.4 fusion.30
  307.9 2.7 collective-permute-start.2
  311.3 1.2 convert_bitcast_fusion.3
  312.5 1.2 pad_maximum_fusion
  313.7 4.4 %copy.93 = bf16[4,32,64,192]{3,2,1,0:T(8,128)(2,1)} copy(bf16[4,32,64,192]{3,1,2,0:T(8,128)(2,1)S(1)} %pad_maximum_fusion) | data formatting | bytes 6291456 | tf_op jit(solution)/shard_map/vmap()/concatenate | solution.py:77
  318.1 7.3 %convert_element_type.107 = bf16[1,128,12288]{2,1,0:T(8,128)(2,1)} reshape(bf16[4,32,64,192]{3,2,1,0:T(8,128)(2,1)} %copy.93) | data formatting | bytes 6291456 | tf_op jit(solution)/shard_map/convert_element_type | solution.py:155
  325.6 8.3 %fusion.38 = (f32[96]{0:T(128)S(1)}, f32[96,1536]{1,0:T(8,128)S(1)}) fusion(bf16[1,1,96,1536]{3,2,1,0:T(8,128)(2,1)S(1)} %copy-done.15, bf16[96,5120]{1,0:T(8,128)(2,1)S(1)} %copy-done.10, bf16[1,1536,5120]{1,2,0:T(8,128)(2,1)} %all-gather.9.cloned.1.call-done), kind=kOutput, calls=%fused_computation.52 | convolution fusion | flops 1510391680 | bytes 17596800 | tf_op jit(solution)/shard_map/dot_general | solution.py:172
  334.5 8.0 %all-to-all-start.2 = ((f32[16,1,6]{2,1,0:T(1,128)}), f32[16,1,6]{2,1,0:T(1,128)S(1)}, u32[]{:S(2)}, u32[]{:S(2)}) async-start(f32[16,1,6]{2,1,0:T(1,128)} %bitcast.34), calls=%async_computation.2 | async-start | bytes 16384 | tf_op jit(solution)/shard_map/all_to_all | solution.py:185
  343.3 7.7 %all-to-all-done.2 = f32[16,1,6]{2,1,0:T(1,128)S(1)} async-done(((f32[16,1,6]{2,1,0:T(1,128)}), f32[16,1,6]{2,1,0:T(1,128)S(1)}, u32[]{:S(2)}, u32[]{:S(2)}) %all-to-all-start.2) | async-done | bytes 416 | tf_op jit(solution)/shard_map/all_to_all | solution.py:185
  353.1 3.5 all-to-all-start
  356.6 1.5 fusion.40
  358.9 6.0 %all-to-all-done = bf16[16,1,6]{2,1,0:T(2,128)(2,1)S(1)} async-done(((bf16[16,1,6]{2,1,0:T(2,128)(2,1)}), bf16[16,1,6]{2,1,0:T(2,128)(2,1)S(1)}, u32[]{:S(2)}, u32[]{:S(2)}) %all-to-all-start) | async-done | bytes 224 | tf_op jit(solution)/shard_map/all_to_all | solution.py:167
  (111 shorter events, 17.8 us)
Async XLA Ops:
  7.2 6.4 %copy-start = (bf16[1,128,5120]{2,1,0:T(8,128)(2,1)S(1)}, bf16[1,128,5120]{2,1,0:T(8,128)(2,1)}, u32[]{:S(2)}) copy-start(bf16[1,128,5120]{2,1,0:T(8,128)(2,1)} %param.17) | copy-start | bytes 3932164
  7.2 94.3 %all-gather.5.cloned.1.call-start = ((), (), s32[]{:S(2)}) async-start(), calls=%async_computation.3 | async-start | bytes 8912896 | tf_op jit(solution)/shard_map/all_gather | solution.py:120
  7.9 179.9 %all-gather.7.cloned.1.call-start = ((), (), s32[]{:S(2)}) async-start(), calls=%async_computation.4 | async-start | bytes 8912896 | tf_op jit(solution)/shard_map/all_gather | solution.py:121
  8.7 316.9 %all-gather.9.cloned.1.call-start = ((), (), s32[]{:S(2)}) async-start(), calls=%async_computation.5 | async-start | bytes 16711680 | tf_op jit(solution)/shard_map/all_gather | solution.py:174
  10.2 14.6 %copy-start.12 = (bf16[1,128,512]{2,1,0:T(8,128)(2,1)S(1)}, bf16[1,128,512]{2,1,0:T(8,128)(2,1)}, u32[]{:S(2)}) copy-start(bf16[1,128,512]{2,1,0:T(8,128)(2,1)} %param.13) | copy-start | bytes 393220
  10.2 17.2 %copy-start.16 = (bf16[1,128,64]{1,2,0:T(8,128)(2,1)S(1)}, bf16[1,128,64]{1,2,0:T(8,128)(2,1)}, u32[]{:S(2)}) copy-start(bf16[1,128,64]{1,2,0:T(8,128)(2,1)} %param.14) | copy-start | bytes 49156
  15.3 42.1 %all-to-all-start.1 = ((bf16[16,6,5120]{2,1,0:T(8,128)(2,1)}), bf16[16,6,5120]{2,1,0:T(8,128)(2,1)S(1)}, u32[]{:S(2)}, u32[]{:S(2)}) async-start(bf16[16,6,5120]{2,1,0:T(8,128)(2,1)} %reshape.295), calls=%async_computation.1 | async-start | bytes 2621440 | tf_op jit(solution)/shard_map/all_to_all | solution.py:166
  25.5 33.4 %collective-permute-start = (bf16[32,512]{1,0:T(8,128)(2,1)}, bf16[32,512]{1,0:T(8,128)(2,1)}, u32[]{:S(2)}, u32[]{:S(2)}) collective-permute-start(bf16[32,512]{1,0:T(8,128)(2,1)} %slice_bitcast_fusion.5), channel_id=1, source_target_pairs={{0,16},{16,32},{32,48},{48,64},{64,80},{80,96},{96,112},{112,128},... | collective-permute-start | bytes 98312 | tf_op jit(solution)/shard_map/ppermute | solution.py:21
  28.1 25.9 %collective-permute-start.1 = (bf16[32,64]{0,1:T(8,128)(2,1)}, bf16[32,64]{0,1:T(8,128)(2,1)}, u32[]{:S(2)}, u32[]{:S(2)}) collective-permute-start(bf16[32,64]{0,1:T(8,128)(2,1)} %slice_bitcast_fusion.7), channel_id=1, source_target_pairs={{0,16},{16,32},{32,48},{48,64},{64,80},{80,96},{96,112},{112,128},... | collective-permute-start | bytes 12296 | tf_op jit(solution)/shard_map/ppermute | solution.py:21
  41.9 2.9 copy-start.6
  44.8 155.7 %copy-start.4 = (bf16[4,32,64,128]{3,2,1,0:T(8,128)(2,1)}, bf16[4,32,64,128]{3,2,1,0:T(8,128)(2,1)S(1)}, u32[]{:S(2)}) copy-start(bf16[4,32,64,128]{3,2,1,0:T(8,128)(2,1)S(1)} %slice.78) | copy-start | bytes 6291460
  195.6 2.0 copy-start.8
  196.2 2.7 copy-start.9
  200.5 13.9 %copy-start.2 = (bf16[4,64,64,128]{3,1,2,0:T(8,128)(2,1)}, bf16[4,64,64,128]{3,1,2,0:T(8,128)(2,1)S(1)}, u32[]{:S(2)}) copy-start(bf16[4,64,64,128]{3,1,2,0:T(8,128)(2,1)S(1)} %copy_dynamic-update-slice_fusion) | copy-start | bytes 12582916
  200.5 13.9 %copy-start.7 = (bf16[4,32,64,64]{3,2,1,0:T(8,128)(2,1)S(1)}, bf16[4,32,64,64]{3,2,1,0:T(8,128)(2,1)}, u32[]{:S(2)}) copy-start(bf16[4,32,64,64]{3,2,1,0:T(8,128)(2,1)} %slice.79) | copy-start | bytes 3145732
  200.5 13.9 %copy-start.13 = (bf16[1,128,64]{2,1,0:T(8,128)(2,1)S(1)}, bf16[1,128,64]{2,1,0:T(8,128)(2,1)}, u32[]{:S(2)}) copy-start(bf16[1,128,64]{2,1,0:T(8,128)(2,1)} %copy.86) | copy-start | bytes 49156
  200.6 13.9 %copy-start.14 = (bf16[128,64]{1,0:T(8,128)(2,1)S(1)}, bf16[128,64]{1,0:T(8,128)(2,1)}, u32[]{:S(2)}) copy-start(bf16[128,64]{1,0:T(8,128)(2,1)} %copy.85) | copy-start | bytes 49156
  200.6 13.9 %copy-start.17 = (pred[4,32,64]{2,1,0:T(8,128)(4,1)S(1)}, pred[4,32,64]{2,1,0:T(8,128)(4,1)}, u32[]{:S(2)}) copy-start(pred[4,32,64]{2,1,0:T(8,128)(4,1)} %broadcast_and_fusion) | copy-start | bytes 24580
  217.0 43.2 %copy-start.5 = (f32[4,64,32,64]{3,2,1,0:T(8,128)}, f32[4,64,32,64]{3,2,1,0:T(8,128)S(1)}, u32[]{:S(2)}) copy-start(f32[4,64,32,64]{3,2,1,0:T(8,128)S(1)} %fusion.19) | copy-start | bytes 6291460
  217.0 43.2 %copy-start.11 = (bf16[16,8,64,128]{3,2,1,0:T(8,128)(2,1)S(1)}, bf16[16,8,64,128]{3,2,1,0:T(8,128)(2,1)}, u32[]{:S(2)}) copy-start(bf16[16,8,64,128]{3,2,1,0:T(8,128)(2,1)} %copy.120) | copy-start | bytes 6291460
  270.9 71.7 %collective-permute-start.3 = (f32[32,64]{1,0:T(8,128)S(1)}, f32[32,64]{1,0:T(8,128)S(1)}, u32[]{:S(2)}, u32[]{:S(2)}) collective-permute-start(f32[32,64]{1,0:T(8,128)S(1)} %slice_bitcast_fusion.6), channel_id=1, source_target_pairs={{16,0},{32,16},{48,32},{64,48},{80,64},{96,80},{112,96},{128,112},... | collective-permute-start | bytes 24584 | tf_op jit(solution)/shard_map/ppermute | solution.py:21
  294.8 3.9 %copy-start.20 = (bf16[4,64,8,8,128]{4,3,2,1,0:T(8,128)(2,1)S(1)}, bf16[4,64,8,8,128]{4,3,2,1,0:T(8,128)(2,1)}, u32[]{:S(2)}) copy-start(bf16[4,64,8,8,128]{4,3,2,1,0:T(8,128)(2,1)} %convert_bitcast_fusion) | copy-start | bytes 12582916
  294.8 10.0 %slice-start = ((s8[8388608]{0:T(1024)(128)(4,1)}), s8[4194304]{0:T(1024)(128)(4,1)S(1)}, s32[]{:S(2)}) async-start(s8[8388608]{0:T(1024)(128)(4,1)} %bitcast.160), calls=%async_computation.6 | async-start | bytes 8388608
  298.8 6.0 %slice-start.1 = ((s8[8388608]{0:T(1024)(128)(4,1)}), s8[4194304]{0:T(1024)(128)(4,1)S(1)}, s32[]{:S(2)}) async-start(s8[8388608]{0:T(1024)(128)(4,1)} %bitcast.160), calls=%async_computation.7 | async-start | bytes 8388608
  307.2 4.1 %copy-start.3 = (bf16[4,64,64,128]{3,1,2,0:T(8,128)(2,1)S(1)}, bf16[4,64,64,128]{3,1,2,0:T(8,128)(2,1)}, u32[]{:S(2)}) copy-start(bf16[4,64,64,128]{3,1,2,0:T(8,128)(2,1)} %copy-done.2) | copy-start | bytes 12582916
  307.9 48.7 %collective-permute-start.2 = (f32[32,512]{1,0:T(8,128)}, f32[32,512]{1,0:T(8,128)}, u32[]{:S(2)}, u32[]{:S(2)}) collective-permute-start(f32[32,512]{1,0:T(8,128)} %slice_bitcast_fusion.4), channel_id=1, source_target_pairs={{16,0},{32,16},{48,32},{64,48},{80,64},{96,80},{112,96},{128,112},... | collective-permute-start | bytes 196616 | tf_op jit(solution)/shard_map/ppermute | solution.py:21
  318.1 7.4 %copy-start.10 = (bf16[96,5120]{1,0:T(8,128)(2,1)S(1)}, bf16[96,5120]{1,0:T(8,128)(2,1)}, u32[]{:S(2)}) copy-start(bf16[96,5120]{1,0:T(8,128)(2,1)} %reshape.296) | copy-start | bytes 2949124
  318.1 7.4 %copy-start.15 = (bf16[1,1,96,1536]{3,2,1,0:T(8,128)(2,1)S(1)}, bf16[1,1,96,1536]{3,2,1,0:T(8,128)(2,1)}, u32[]{:S(2)}) copy-start(bf16[1,1,96,1536]{3,2,1,0:T(8,128)(2,1)} %param.20) | copy-start | bytes 884740
  325.5 26.7 %copy-start.18 = (f32[768]{0:T(1024)S(1)}, f32[768]{0:T(1024)}, u32[]{:S(2)}) copy-start(f32[768]{0:T(1024)} %reshape.299) | copy-start | bytes 9220
  325.5 26.7 %copy-start.19 = (s32[768]{0:T(1024)S(1)}, s32[768]{0:T(1024)}, u32[]{:S(2)}) copy-start(s32[768]{0:T(1024)} %add_select_fusion.6) | copy-start | bytes 9220
  325.6 40.3 %copy-start.1 = (bf16[1,128,5120]{2,1,0:T(8,128)(2,1)S(1)}, bf16[1,128,5120]{2,1,0:T(8,128)(2,1)}, u32[]{:S(2)}) copy-start(bf16[1,128,5120]{2,1,0:T(8,128)(2,1)} %param.17) | copy-start | bytes 3932164
  334.5 16.4 %all-to-all-start.2 = ((f32[16,1,6]{2,1,0:T(1,128)}), f32[16,1,6]{2,1,0:T(1,128)S(1)}, u32[]{:S(2)}, u32[]{:S(2)}) async-start(f32[16,1,6]{2,1,0:T(1,128)} %bitcast.34), calls=%async_computation.2 | async-start | bytes 16384 | tf_op jit(solution)/shard_map/all_to_all | solution.py:185
  353.1 11.8 %all-to-all-start = ((bf16[16,1,6]{2,1,0:T(2,128)(2,1)}), bf16[16,1,6]{2,1,0:T(2,128)(2,1)S(1)}, u32[]{:S(2)}, u32[]{:S(2)}) async-start(bf16[16,1,6]{2,1,0:T(2,128)(2,1)} %convert_element_type.132), calls=%async_computation | async-start | bytes 16384 | tf_op jit(solution)/shard_map/all_to_all | solution.py:167
Sparse Core Ops, SparseCore 0:
  10.6 90.9 all-gather.4
  104.1 83.6 all-gather.6
  190.5 108.4 all-gather.8
where the time goes:
time: 378 us; the launch traced here: 373 us
  waiting for transfers between devices  136 us (36%)
  matrix products  78.4 us (21%)
  local copies, waits for them, and re-layouts  55.4 us (15%)
  other arithmetic  55.1 us (15%)
  starting transfers between devices  33.3 us (9%)
  between operations  14.7 us (4%)
    all_gather x1, waiting for transfers between devices, local(): value_cols = lax.all_gather(w_value, 'ctx', axis=1, tiled=True)  76.7 us
    sub x1, other arithmetic, window_grads(): shifted = jnp.exp(scores - row_max)  43.2 us
    all_gather x1, waiting for transfers between devices, local(): key_cols = lax.all_gather(w_key, 'ctx', axis=1, tiled=True)  42.6 us
    dot_general x1, matrix products, window_grads(): jnp.einsum('hij,ihd->jhd', probs_low, d_out, preferred_element_type=jnp.f...  21.3 us
    unnamed x58, local copies, waits for them, and re-layouts  15.5 us
    dot_general x1, matrix products, window_grads(): jnp.einsum('ihd,jhd->hij', q_nope, keys, preferred_element_type=jnp.float32)  13.9 us
    ppermute x4, starting transfers between devices, from_behind(): return lax.ppermute(shard, axis, pairs)  12.1 us
    all_to_all x1, starting transfers between devices, local(): lax.all_to_all(outbound, 'exp', split_axis=0, concat_axis=0, tiled=True)  9.58 us
  transfers between devices with their start and end apart: 10, of which 5 were waited for; matrix products, arithmetic and copies ran while one was open for 50% of the time, Pallas kernels for 0%

commit v1 on v0

v1 whole, which is shorter than its diff:
```python
import functools

import jax
import jax.numpy as jnp
from jax import lax
from jax.experimental import pallas as pl
from jax.experimental.pallas import tpu as pltpu
from jax.sharding import PartitionSpec as P

HEADS = 64
NOPE = 128
ROPE = 64
VDIM = 128
LATENT = 512
FFH = 1536
EXPERTS = 160
TOPK = 6
WIN = 32
CAP = 6
CTX = 16
EXP = 16
TOK = 128
CHIPS = 8
GROUP = 4
QW = GROUP * (NOPE + ROPE)
VW = GROUP * VDIM
ROWS = 2 * TOK + WIN
SPAN = TOK + WIN
SCALE = (NOPE + ROPE) ** (-0.5)
COST = pl.CostEstimate(flops=1_000_000, bytes_accessed=1_000_000, transcendentals=0)


def ctx_at(x, half, core):
    return ((x % 4) * 2 + half) * 2 + core


def ctx_moves(step):
    return [
        (ctx_at(x, half, core), ctx_at(x + step, half, core))
        for x in range(4)
        for half in range(2)
        for core in range(2)
    ]


RIGHT = ctx_moves(1)
LEFT = ctx_moves(-1)
TWIN = [(i, i ^ 1) for i in range(CTX)]
ACROSS = [
    ((i * EXP + e), ((i ^ 2) * EXP + (e ^ 8))) for i in range(CTX) for e in range(EXP)
]
RING = [[ctx_at(x, half, core) for x in range(4) for core in range(2)] for half in range(2)]
RING_CORE = [[ctx_at(x, half, core) for x in range(4)] for half in range(2) for core in range(2)]


def nothing_body(*refs):
    pass


def tie(value, *others):
    return pl.pallas_call(
        nothing_body,
        in_specs=[pl.BlockSpec(memory_space=pl.ANY)] * (1 + len(others)),
        out_specs=pl.BlockSpec(memory_space=pl.ANY),
        out_shape=jax.ShapeDtypeStruct(value.shape, value.dtype),
        input_output_aliases={0: 0},
        cost_estimate=COST,
    )(value, *others)


def stack_body(key_ref, value_ref, out_ref):
    out_ref[:LATENT] = key_ref[...]
    out_ref[LATENT:] = value_ref[...]


def stack(w_key, w_value):
    return pl.pallas_call(
        stack_body,
        out_shape=jax.ShapeDtypeStruct((2 * LATENT, VW), jnp.bfloat16),
        compiler_params=pltpu.CompilerParams(vmem_limit_bytes=60 * 1024 * 1024),
        cost_estimate=COST,
    )(w_key, w_value)


def place_body(counts, where_ref, grid_ref, *refs):
    parts, out_ref = refs[: len(counts)], refs[len(counts)]
    held, in_sems, out_sems = refs[len(counts) + 1 :]
    core = where_ref[0]
    ways = []
    for part, count in zip(parts, counts):
        for i in range(count):
            at = len(ways)
            column = pl.multiple_of((2 * where_ref[1 + at] + 1 - core) * QW, QW)
            ways.append(
                (
                    pltpu.make_async_copy(part.at[i], held.at[at], in_sems.at[at]),
                    pltpu.make_async_copy(
                        held.at[at], out_ref.at[:, pl.ds(column, QW)], out_sems.at[at]
                    ),
                )
            )
    for arrive, _ in ways:
        arrive.start()
    for arrive, leave in ways:
        arrive.wait()
        leave.start()
    for _, leave in ways:
        leave.wait()


def place(where, query_grad, parts):
    counts = tuple(part.shape[0] for part in parts)
    return pl.pallas_call(
        functools.partial(place_body, counts),
        grid_spec=pltpu.PrefetchScalarGridSpec(
            num_scalar_prefetch=1,
            grid=(),
            in_specs=[pl.BlockSpec(memory_space=pl.ANY)] * (1 + len(parts)),
            out_specs=pl.BlockSpec(memory_space=pl.ANY),
            scratch_shapes=[
                pltpu.VMEM((sum(counts), TOK, QW), jnp.bfloat16),
                pltpu.SemaphoreType.DMA((sum(counts),)),
                pltpu.SemaphoreType.DMA((sum(counts),)),
            ],
        ),
        out_shape=jax.ShapeDtypeStruct(query_grad.shape, query_grad.dtype),
        input_output_aliases={1: 0},
        cost_estimate=COST,
    )(where, query_grad, *parts)


NT = (((1,), (1,)), ((), ()))
NN = (((1,), (0,)), ((), ()))
TN = (((0,), (0,)), ((), ()))


def dot(a, b, dims):
    return lax.dot_general(a, b, dims, preferred_element_type=jnp.float32)


def attend_body(count, skipped, where_ref, *refs):
    latent_ref, rope_low_ref, rope_high_ref, bias_ref = refs[:4]
    q_ref, d_ref, twin_q_ref, twin_d_ref = refs[4:8]
    weights = refs[8 + skipped : 8 + skipped + 2 * count]
    at = 8 + skipped + 2 * count
    query_out, twin_out, latent_out, rope_out, mark_out = refs[at : at + 5]
    wk_ref, wv_ref, q_both, d_both, grad_both, dk_ref, dv_ref = refs[at + 5 :]
    step = pl.program_id(0)
    core = where_ref[0]

    for i in range(count):

        @pl.when(step == i)
        def _():
            wk_ref[...] = weights[2 * i][...]
            wv_ref[...] = weights[2 * i + 1][...]

    for own in range(2):

        @pl.when(core == own)
        def _():
            q_both[own] = q_ref[...]
            d_both[own] = d_ref[...]
            q_both[1 - own] = twin_q_ref[...]
            d_both[1 - own] = twin_d_ref[...]

    latent = latent_ref[...]
    keys = dot(latent, wk_ref[...], NN)
    values = dot(latent, wv_ref[...], NN).astype(jnp.bfloat16)
    low = lax.broadcasted_iota(jnp.int32, (ROWS, NOPE), 1) < ROPE
    rope_sum = jnp.zeros((ROWS, NOPE), jnp.float32)

    def fold(first, second):
        return jnp.concatenate(
            [first[:TOK], first[TOK:] + second[:WIN], second[WIN:]], axis=0
        )

    for pair in range(GROUP // 2):
        query_parts = [[], []]
        key_parts = []
        for odd in range(2):
            head = 2 * pair + odd
            key = keys[:, head * NOPE : (head + 1) * NOPE]
            if odd:
                turned = pltpu.roll(key, ROPE, 1)
                tiles = [
                    jnp.where(low, 0.0, turned).astype(jnp.bfloat16),
                    jnp.where(low, turned, rope_high_ref[...]).astype(jnp.bfloat16),
                ]
            else:
                tiles = [key.astype(jnp.bfloat16), rope_low_ref[...]]
            wide = jnp.concatenate(tiles, axis=1)
            value = values[:, head * VDIM : (head + 1) * VDIM]
            start = pair * 2 * (NOPE + ROPE) + odd * NOPE
            dk, dv = [], []
            for s in range(2):
                span = slice(s * TOK, s * TOK + SPAN)
                q = q_both[s, :, start : start + 2 * NOPE]
                d = d_both[s, :, head * VDIM : (head + 1) * VDIM]
                scores = dot(wide[span], q, NT) * SCALE + bias_ref[s]
                shifted = jnp.exp(scores - jnp.max(scores, axis=0, keepdims=True))
                inverse = 1.0 / jnp.sum(shifted, axis=0, keepdims=True)
                prob_grad = dot(value[span], d, NT)
                probs = shifted * inverse
                delta = jnp.sum(probs * prob_grad, axis=0, keepdims=True)
                score_grad = (SCALE * probs * (prob_grad - delta)).astype(jnp.bfloat16)
                probs_low = probs.astype(jnp.bfloat16)
                query_parts[s].append(dot(score_grad, wide[span], TN))
                dk.append(dot(score_grad, q, NN))
                dv.append(dot(probs_low, d, NN))
            dv_ref[:, head * VDIM : (head + 1) * VDIM] = fold(*dv).astype(jnp.bfloat16)
            key_parts.append(fold(*dk))
        even, odd = key_parts
        dk_ref[:, 2 * pair * NOPE : (2 * pair + 1) * NOPE] = even[:, :NOPE].astype(jnp.bfloat16)
        dk_ref[:, (2 * pair + 1) * NOPE : (2 * pair + 2) * NOPE] = pltpu.roll(
            jnp.where(low, odd[:, NOPE:], odd[:, :NOPE]), ROPE, 1
        ).astype(jnp.bfloat16)
        rope_sum = rope_sum + jnp.where(low, even[:, NOPE:], odd[:, NOPE:])
        for s in range(2):
            first, second = query_parts[s]
            left = pair * 3 * NOPE
            grad_both[s, :, left : left + NOPE] = first[:, :NOPE].astype(jnp.bfloat16)
            grad_both[s, :, left + NOPE : left + 2 * NOPE] = (
                first[:, NOPE:] + second[:, :NOPE]
            ).astype(jnp.bfloat16)
            grad_both[s, :, left + 2 * NOPE : left + 3 * NOPE] = second[:, NOPE:].astype(
                jnp.bfloat16
            )

    latent_sum = dot(dk_ref[...], wk_ref[...], NT) + dot(dv_ref[...], wv_ref[...], NT)

    @pl.when(step == 0)
    def _():
        latent_out[...] = latent_sum
        rope_out[...] = rope_sum
        mark_out[...] = jnp.zeros_like(mark_out)

    @pl.when(step > 0)
    def _():
        latent_out[...] += latent_sum
        rope_out[...] += rope_sum

    for own in range(2):

        @pl.when(core == own)
        def _():
            query_out[...] = grad_both[own]
            twin_out[0] = grad_both[1 - own]


def attend(
    where, shared, query, out_grad, twin_query, twin_grad, query_grad, weights, after=(), heavy=1
):
    count = len(weights)
    chained = query_grad is not None
    skipped = ([query_grad] if chained else []) + list(after)
    head_block = lambda width: pl.BlockSpec((TOK, width), lambda g, w: (0, 2 * w[1 + g] + w[0]))
    whole = lambda shape: pl.BlockSpec(shape, lambda g, w: (0,) * len(shape))
    in_specs = [
        whole((ROWS, LATENT)),
        whole((ROWS, NOPE)),
        whole((ROWS, NOPE)),
        whole((2, SPAN, TOK)),
        head_block(QW),
        head_block(VW),
        head_block(QW),
        head_block(VW),
    ]
    operands = [where, *shared, query, out_grad, twin_query, twin_grad, *skipped]
    in_specs += [pl.BlockSpec(memory_space=pl.ANY)] * len(skipped)
    for (key_part, key_at), (value_part, value_at) in weights:
        in_specs.append(pl.BlockSpec((LATENT, VW), lambda g, w, at=key_at: (at, 0)))
        in_specs.append(pl.BlockSpec((LATENT, VW), lambda g, w, at=value_at: (at, 0)))
        operands += [key_part, value_part]
    return pl.pallas_call(
        functools.partial(attend_body, count, len(skipped)),
        grid_spec=pltpu.PrefetchScalarGridSpec(
            num_scalar_prefetch=1,
            grid=(count,),
            in_specs=in_specs,
            out_specs=[
                head_block(QW),
                pl.BlockSpec((1, TOK, QW), lambda g, w: (g, 0, 0)),
                whole((ROWS, LATENT)),
                whole((ROWS, NOPE)),
                whole((8, NOPE)),
            ],
            scratch_shapes=[
                pltpu.VMEM((LATENT, VW), jnp.bfloat16),
                pltpu.VMEM((LATENT, VW), jnp.bfloat16),
                pltpu.VMEM((2, TOK, QW), jnp.bfloat16),
                pltpu.VMEM((2, TOK, VW), jnp.bfloat16),
                pltpu.VMEM((2, TOK, QW), jnp.bfloat16),
                pltpu.VMEM((ROWS, VW), jnp.bfloat16),
                pltpu.VMEM((ROWS, VW), jnp.bfloat16),
            ],
        ),
        out_shape=[
            jax.ShapeDtypeStruct((TOK, HEADS * (NOPE + ROPE)), jnp.bfloat16),
            jax.ShapeDtypeStruct((count, TOK, QW), jnp.bfloat16),
            jax.ShapeDtypeStruct((ROWS, LATENT), jnp.float32),
            jax.ShapeDtypeStruct((ROWS, NOPE), jnp.float32),
            jax.ShapeDtypeStruct((8, NOPE), jnp.float32),
        ],
        input_output_aliases={9: 0} if chained else {},
        compiler_params=pltpu.CompilerParams(vmem_limit_bytes=60 * 1024 * 1024),
        cost_estimate=pl.CostEstimate(
            flops=heavy * count * 500_000_000, bytes_accessed=count * 500_000, transcendentals=0
        ),
    )(*operands)


def local(
    query,
    out_grad,
    latent,
    rope_key,
    w_key,
    w_value,
    grad_stream,
    expert_ids,
    gate_weights,
    saved_hidden,
    w_down,
):
    query, out_grad, latent, rope_key = query[0], out_grad[0], latent[0], rope_key[0]
    grad_stream, expert_ids, gate_weights = grad_stream[0], expert_ids[0], gate_weights[0]
    index = lax.axis_index("ctx")
    core = index % 2
    chip = index // 2
    x = chip // 2
    half = chip % 2

    def group(step, flip):
        return 2 * ((x + step) % 4) + (half ^ flip)

    def spots(*groups):
        return jnp.stack([core, *groups]).astype(jnp.int32)

    def both(stack):
        return ((stack, 0), (stack, 1))

    mine = jnp.concatenate([latent, rope_key], axis=1)
    twin_rows = lax.ppermute(mine, "ctx", TWIN)
    chip_rows = jnp.where(
        core == 0,
        jnp.concatenate([mine, twin_rows], axis=0),
        jnp.concatenate([twin_rows, mine], axis=0),
    )
    halo = lax.ppermute(
        chip_rows[2 * TOK - WIN :], "ctx", [(i, i + 2) for i in range(CTX - 2)]
    )
    own = stack(w_key, w_value)
    before = lax.ppermute(own, "ctx", RIGHT)
    after = lax.ppermute(own, "ctx", LEFT)
    beside = lax.ppermute(own, ("ctx", "exp"), ACROSS)
    twin_query = lax.ppermute(query, "ctx", TWIN)
    twin_grad = lax.ppermute(out_grad, "ctx", TWIN)
    down = w_down[0]
    other_down = lax.ppermute(down, "ctx", [(i, i ^ 2) for i in range(CTX)])
    down = jnp.where(
        half == 0,
        jnp.concatenate([down, other_down], axis=1),
        jnp.concatenate([other_down, down], axis=1),
    )

    share = EXPERTS // EXP
    slots = jnp.arange(EXP * CAP, dtype=jnp.int32)[None, :]
    ids = tie(expert_ids, halo)
    match = [ids[:, k : k + 1] == slots // CAP * share for k in range(TOPK)]
    live = functools.reduce(jnp.logical_or, match)
    token_at = jnp.arange(TOK, dtype=jnp.int32)
    earlier = dot(
        (token_at[:, None] > token_at[None, :]).astype(jnp.bfloat16), live.astype(jnp.bfloat16), NN
    )
    token_hot = (live & (earlier == (slots % CAP).astype(jnp.float32))).astype(jnp.bfloat16)
    gates = sum(
        jnp.where(match[k], gate_weights[:, k : k + 1].astype(jnp.float32), 0.0)
        for k in range(TOPK)
    )
    gate_send = jnp.sum(token_hot.astype(jnp.float32) * gates, axis=0).reshape(EXP, 1, CAP)
    outbound = dot(token_hot, grad_stream, TN).astype(jnp.bfloat16)
    tiles = outbound.shape[1] // NOPE
    outbound = jnp.concatenate(
        [
            outbound.reshape(EXP, CAP * tiles, NOPE),
            jnp.pad(gate_send.astype(jnp.bfloat16), ((0, 0), (0, 7), (0, NOPE - CAP))),
        ],
        axis=1,
    )
    outbound = tie(outbound, twin_query, own)
    routed = lax.all_to_all(outbound, "exp", split_axis=0, concat_axis=0, tiled=True)

    rows = jnp.concatenate([halo, chip_rows], axis=0)
    rope_rows = rows[:, LATENT:]
    blank = jnp.zeros_like(rope_rows)
    key_at = jnp.arange(SPAN, dtype=jnp.int32)[:, None]
    query_at = jnp.arange(TOK, dtype=jnp.int32)[None, :]
    inside = (key_at > query_at) & (key_at <= query_at + WIN)
    first = inside & ((chip > 0) | (key_at >= WIN))
    shared = (
        rows[:, :LATENT],
        jnp.concatenate([rope_rows, blank], axis=1),
        jnp.concatenate([blank, rope_rows], axis=1).astype(jnp.float32),
        jnp.where(jnp.stack([first, inside]), 0.0, -jnp.inf).astype(jnp.float32),
    )
    common = (shared, query, out_grad, twin_query, twin_grad)

    where_a = spots(group(0, 0))
    query_grad, part_a, latent_a, rope_a, mark_a = attend(where_a, *common, None, [both(own)])

    opposite = lax.ppermute(before, "ctx", RIGHT)
    beside_after = lax.ppermute(beside, "ctx", LEFT)
    beside_before = lax.ppermute(before, ("ctx", "exp"), ACROSS)
    where_b = spots(group(-1, 0), group(1, 0), group(0, 1))
    query_grad, part_b, latent_b, rope_b, mark_b = attend(
        where_b, *common, query_grad, [both(before), both(after), both(beside)], heavy=10
    )
    routed = tie(routed, mark_b)
    row_gate = routed[:, CAP * tiles, :CAP].reshape(EXP * CAP, 1)
    slices = routed[:, : CAP * tiles].reshape(EXP * CAP, 4, 2, 2, -1)
    slices = slices.transpose(1, 3, 0, 2, 4).reshape(CHIPS, EXP * CAP, -1)
    slices = lax.all_to_all(
        slices, "ctx", split_axis=0, concat_axis=0, tiled=True, axis_index_groups=RING
    )

    part_a = lax.ppermute(part_a, "ctx", TWIN)
    part_b = lax.ppermute(part_b, "ctx", TWIN)

    last_key = lax.ppermute(tie(beside_after[:LATENT], mark_b), "ctx", LEFT)
    last_value = lax.ppermute(tie(opposite[LATENT:], mark_b), ("ctx", "exp"), ACROSS)
    where_c = spots(group(2, 0), group(-1, 1))
    query_grad, part_c, latent_c, rope_c, mark_c = attend(
        where_c, *common, query_grad, [both(opposite), both(beside_before)], (mark_b,)
    )
    part_c = lax.ppermute(part_c, "ctx", TWIN)

    slices = tie(slices, mark_c).reshape(4, 2, EXP * CAP, -1)

    def terms(number):
        rows = lax.dynamic_index_in_dim(slices, number, 1, keepdims=False)
        rows = rows.reshape(4 * EXP * CAP, -1)
        return dot(rows, down, NT).astype(jnp.bfloat16).reshape(4, EXP * CAP, FFH)

    give = terms(1 - core)
    keep = terms(core)
    taken = lax.ppermute(give, "ctx", TWIN)

    keep = (keep.astype(jnp.float32) + taken.astype(jnp.float32)).astype(jnp.bfloat16)
    pieces = lax.all_to_all(
        keep, "ctx", split_axis=0, concat_axis=0, tiled=True, axis_index_groups=RING_CORE
    )

    where_d = spots(group(1, 1), group(2, 1))
    query_grad, part_d, latent_d, rope_d, mark_d = attend(
        where_d,
        *common,
        query_grad,
        [both(beside_after), ((last_key, 0), (last_value, 0))],
        (keep,),
    )
    part_d = lax.ppermute(part_d, "ctx", TWIN)
    rope_sum = rope_a + rope_b + rope_c + rope_d
    sums = jnp.concatenate(
        [latent_a + latent_b + latent_c + latent_d, rope_sum[:, :ROPE] + rope_sum[:, ROPE:]], axis=1
    )
    back = lax.ppermute(sums[:WIN], "ctx", [(i + 2, i) for i in range(CTX - 2)])
    low = sums[WIN : WIN + TOK]
    high = sums[WIN + TOK :]
    high = jnp.concatenate([high[: TOK - WIN], high[TOK - WIN :] + back], axis=0)
    kept = jnp.where(core == 0, low, high)
    given = lax.ppermute(jnp.where(core == 0, high, low), "ctx", TWIN)
    total = (kept + given).astype(jnp.bfloat16)
    query_grad = place(
        jnp.concatenate([where_a, where_b[1:], where_c[1:], where_d[1:]]),
        query_grad,
        (part_a, part_b, part_c, part_d),
    )

    raw_grad = jnp.sum(pieces.astype(jnp.float32), axis=0)
    gate_part = jnp.sum(saved_hidden[0, 0].astype(jnp.float32) * raw_grad, axis=1)
    hidden_grad = (row_gate.astype(jnp.float32) * raw_grad).astype(jnp.bfloat16)
    returned = lax.all_to_all(
        gate_part.reshape(EXP, CAP), "exp", split_axis=0, concat_axis=0, tiled=True
    )
    found = token_hot.astype(jnp.float32) * returned.reshape(1, -1)
    gate_grad = jnp.stack(
        [jnp.sum(jnp.where(match[k], found, 0.0), axis=1) for k in range(TOPK)], axis=1
    )
    return (
        query_grad[None],
        total[None, :, :LATENT],
        total[None, :, LATENT:],
        hidden_grad[None, None],
        gate_grad[None],
    )


def solution(mesh):
    in_specs = (
        P("exp", "ctx", None),
        P("exp", "ctx", None),
        P("exp", "ctx", None),
        P("exp", "ctx", None),
        P(None, "ctx"),
        P(None, "ctx"),
        P("exp", "ctx", None),
        P("exp", "ctx", None),
        P("exp", "ctx", None),
        P("ctx", "exp", None, None),
        P("exp", None, "ctx"),
    )
    out_specs = (
        P("exp", "ctx", None),
        P("exp", "ctx", None),
        P("exp", "ctx", None),
        P("ctx", "exp", None, None),
        P("exp", "ctx", None),
    )
    return jax.shard_map(local, mesh=mesh, in_specs=in_specs, out_specs=out_specs, check_vma=False)
```

time: 378 us -> 211 us (0.56)
  waiting for transfers between devices: 136 us -> 41.6 us
  matrix products: 78.4 us -> 10.4 us
  Pallas kernels: 0 us -> 48.5 us
  other arithmetic: 55.1 us -> 25.1 us
  local copies, waits for them, and re-layouts: 55.4 us -> 29.8 us
  starting transfers between devices: 33.3 us -> 50.6 us
  between operations: 14.7 us -> 1.26 us
    all_gather x3 -> x0, waiting for transfers between devices: 119 us -> none  [the longest x1 76.7 us: local(): value_cols = lax.all_gather(w_value, 'ctx', axis=1, tiled=True)]
    dot_general x14 -> x4, matrix products: 78.4 us -> 10.4 us  [dot(): return lax.dot_general(a, b, dims, preferred_element_type=jnp.float32)]
    pallas_call x0 -> x12, Pallas kernels: none -> 48.5 us  [the longest x4 43.2 us: attend(): pl.pallas_call(functools.partial(attend_body, count, len(skipped)), grid_...]
    sub x1 -> x0, other arithmetic: 43.2 us -> none  [window_grads(): shifted = jnp.exp(scores - row_max)]
    ppermute x4 -> x20, waiting for transfers between devices: 0.01 us -> 29.4 us  [the longest x1 11.4 us: local(): lax.ppermute(chip_rows[2 * TOK - WIN:], 'ctx', [(i, i + 2) for i in range...]
    ppermute x4 -> x20, starting transfers between devices: 12.1 us -> 24.1 us  [the longest x1 5.62 us: local(): back = lax.ppermute(sums[:WIN], 'ctx', [(i + 2, i) for i in range(CTX - 2)])]
    convert_element_type x5 -> x2, local copies, waits for them, and re-layouts: 11.1 us -> 1.39 us  [the longest x1 1.3 us: local(): hidden_grad = (row_gate.astype(jnp.float32) * raw_grad).astype(jnp.bfloat16)]
    concatenate x4 -> x1, local copies, waits for them, and re-layouts: 8.63 us -> 0.65 us  [local(): jnp.concatenate([where_a, where_b[1:], where_c[1:], where_d[1:]])]
  transfers between devices with their start and end apart: 10 -> 24, of which waited for: 5 -> 8; matrix products, arithmetic and copies ran while one was open for 50% -> 26% of each run, Pallas kernels for 0% -> 18%
where the time goes in v1:
time: 211 us; the launch traced here: 207 us
  starting transfers between devices  50.6 us (24%)
  Pallas kernels  48.5 us (23%)
  waiting for transfers between devices  41.6 us (20%)
  local copies, waits for them, and re-layouts  29.8 us (14%)
  other arithmetic  25.1 us (12%)
  matrix products  10.4 us (5%)
    pallas_call x4, Pallas kernels, attend(): pl.pallas_call(functools.partial(attend_body, count, len(skipped)), grid_...  43.2 us
    ppermute x1, waiting for transfers between devices, local(): lax.ppermute(chip_rows[2 * TOK - WIN:], 'ctx', [(i, i + 2) for i in range...  11.4 us
    dot_general x4, matrix products, dot(): return lax.dot_general(a, b, dims, preferred_element_type=jnp.float32)  10.4 us
    all_to_all x1, starting transfers between devices, local(): lax.all_to_all(outbound, 'exp', split_axis=0, concat_axis=0, tiled=True)  8.85 us
    unnamed x74, local copies, waits for them, and re-layouts  8.36 us
    ppermute x1, waiting for transfers between devices, local(): other_down = lax.ppermute(down, 'ctx', [(i, i ^ 2) for i in range(CTX)])  7.98 us
    all_to_all x1, waiting for transfers between devices, local(): lax.all_to_all(gate_part.reshape(EXP, CAP), 'exp', split_axis=0, concat_a...  7.63 us
    all_to_all x1, starting transfers between devices, local(): lax.all_to_all(gate_part.reshape(EXP, CAP), 'exp', split_axis=0, concat_a...  7.17 us
  transfers between devices with their start and end apart: 24, of which 8 were waited for; matrix products, arithmetic and copies ran while one was open for 26% of the time, Pallas kernels for 18%

profile of v1, /device:TPU:2, one launch (start us, length us, event | category | flops | bytes accessed | tf_op | source)
XLA Modules:
  0.0 207.3 jit_solution(16635659689086729216)
XLA Ops:
  0.8 2.4 %shard_map.146.refs_8_.refs_9_.refs_2_ = bf16[1024,512]{1,0:T(8,128)(2,1)} custom-call(bf16[512,512]{1,0:T(8,128)(2,1)} %key_ref.1, bf16[512,512]{1,0:T(8,128)(2,1)} %value_ref.1), custom_call_target="tpu_custom_call" | custom-call | flops 1000000 | bytes 1000000 | tf_op jit(solution)/shard_map/pallas_call | solution.py:77
  3.2 1.5 collective-permute-start.4
  4.7 3.0 %collective-permute-start.6 = (bf16[1024,512]{1,0:T(8,128)(2,1)}, bf16[1024,512]{1,0:T(8,128)(2,1)}, u32[]{:S(2)}, u32[]{:S(2)}) collective-permute-start(bf16[1024,512]{1,0:T(8,128)(2,1)} %shard_map.146.refs_8_.refs_9_.refs_2_), channel_id=1, source_target_pairs={{0,40},{1,41},{2,42},{3,43},{4,44},{5,45},{6,46},{7,47},{8,32},{9,... | collective-permute-start | bytes 3145736 | tf_op jit(solution)/shard_map/ppermute | solution.py:356
  8.4 1.4 pad_maximum_fusion.1
  10.4 1.5 bitcast_convert_fusion.5
  13.2 1.4 add_select_fusion.refs_3_
  14.6 1.1 maximum_select_fusion.3
  16.4 2.5 %collective-permute-start.1 = (bf16[32,576]{1,0:T(8,128)(2,1)S(1)}, bf16[32,576]{1,0:T(8,128)(2,1)S(1)}, u32[]{:S(2)}, u32[]{:S(2)}) collective-permute-start(bf16[32,576]{1,0:T(8,128)(2,1)S(1)} %slice.117), channel_id=1, source_target_pairs={{0,32},{16,48},{32,64},{48,80},{64,96},{80,112},{96,128},{112,144}... | collective-permute-start | bytes 110600 | tf_op jit(solution)/shard_map/ppermute | solution.py:350
  19.6 1.4 copy.39
  21.0 11.4 %collective-permute-done.1.refs_1_ = bf16[32,576]{1,0:T(8,128)(2,1)S(1)} collective-permute-done((bf16[32,576]{1,0:T(8,128)(2,1)S(1)}, bf16[32,576]{1,0:T(8,128)(2,1)S(1)}, u32[]{:S(2)}, u32[]{:S(2)}) %collective-permute-start.1) | collective-permute-done | bytes 36896 | tf_op jit(solution)/shard_map/ppermute | solution.py:350
  33.0 1.4 slice_reduce_fusion.5
  36.6 1.4 convolution_convert_fusion
  38.0 2.3 %reshape.250 = bf16[16,240,128]{2,1,0:T(8,128)(2,1)} reshape(bf16[96,5120]{1,0:T(8,128)(2,1)} %convolution_convert_fusion) | data formatting | bytes 1966080 | tf_op jit(solution)/shard_map/reshape | solution.py:386
  40.4 2.3 %fusion.4.refs_0_ = bf16[16,248,128]{2,1,0:T(8,128)(2,1)} fusion(bf16[16,1,6]{2,1,0:T(2,128)(2,1)S(1)} %convert_element_type.119, bf16[16,240,128]{2,1,0:T(8,128)(2,1)} %reshape.250), kind=kLoop, calls=%fused_computation.16 | loop fusion | flops 3047424 | bytes 1999040 | tf_op jit(solution)/shard_map/concatenate | solution.py:384
  42.6 8.9 %all-to-all-start = ((bf16[16,248,128]{2,1,0:T(8,128)(2,1)}), bf16[16,248,128]{2,1,0:T(8,128)(2,1)}, u32[]{:S(2)}, u32[]{:S(2)}) async-start(bf16[16,248,128]{2,1,0:T(8,128)(2,1)} %shard_map.151), calls=%async_computation | async-start | bytes 2031616 | tf_op jit(solution)/shard_map/all_to_all | solution.py:392
  53.8 1.7 fusion.8.refs_0_
  55.4 1.5 collective-permute-start.7
  57.5 6.8 %shard_map.147 = (bf16[128,12288]{1,0:T(8,128)(2,1)}, bf16[1,128,768]{2,1,0:T(8,128)(2,1)}, f32[288,512]{1,0:T(8,128)}, f32[288,128]{1,0:T(8,128)}, f32[8,128]{1,0:T(8,128)}) custom-call(s32[2]{0:T(128)} %pad_add_fusion.3.where_ref, bf16[288,512]{1,0:T(8,128)(2,1)} %fusion.8.refs_0_, bf16[288,128]{1,0:T(8,128)(2,1)} %get-tuple-element.71.refs_1_, ...), custom_call_target="tpu_custom_call" | custom-call | flops 500000000 | bytes 500000 | tf_op jit(solution)/shard_map/pallas_call | solution.py:275
  64.3 14.6 %shard_map.148 = (bf16[128,12288]{1,0:T(8,128)(2,1)}, bf16[3,128,768]{2,1,0:T(8,128)(2,1)}, f32[288,512]{1,0:T(8,128)}, f32[288,128]{1,0:T(8,128)}, f32[8,128]{1,0:T(8,128)}) custom-call(s32[4]{0:T(128)} %pad_add_fusion.2.where_ref, bf16[288,512]{1,0:T(8,128)(2,1)} %fusion.8.refs_0_, ...), custom_call_target="tpu_custom_call", output_to_operand_aliasing={{0}: (9, {})} | custom-call | flops 15000000512 | bytes 1500000 | tf_op jit(solution)/shard_map/pallas_call | solution.py:275
  79.0 1.3 slice.126
  80.3 1.1 reshape.251
  81.4 2.0 copy.46
  83.4 3.5 %reshape.252 = bf16[8,96,640]{2,1,0:T(8,128)(2,1)} reshape(bf16[4,2,96,2,320]{4,3,2,1,0:T(2,128)(2,1)} %bitcast.81) | data formatting | bytes 1966080 | tf_op jit(solution)/shard_map/reshape | solution.py:422
  86.9 5.2 %all-to-all-start.1 = ((bf16[8,96,640]{2,1,0:T(8,128)(2,1)}), bf16[8,96,640]{2,1,0:T(8,128)(2,1)S(1)}, u32[]{:S(2)}, u32[]{:S(2)}) async-start(bf16[8,96,640]{2,1,0:T(8,128)(2,1)} %reshape.252), calls=%async_computation.1 | async-start | bytes 1966080 | tf_op jit(solution)/shard_map/all_to_all | solution.py:423
  92.1 3.9 %collective-permute-start.9 = (bf16[1536,320]{0,1:T(8,128)(2,1)}, bf16[1536,320]{0,1:T(8,128)(2,1)}, u32[]{:S(2)}, u32[]{:S(2)}) collective-permute-start(bf16[1536,320]{0,1:T(8,128)(2,1)} %bitcast.25), channel_id=1, source_target_pairs={{0,32},{16,48},{32,0},{48,16},{64,96},{80,112},{96,64},{112,80},{1... | collective-permute-start | bytes 2949128 | tf_op jit(solution)/shard_map/ppermute | solution.py:360
  96.7 10.8 %shard_map.149 = (bf16[128,12288]{1,0:T(8,128)(2,1)}, bf16[2,128,768]{2,1,0:T(8,128)(2,1)}, f32[288,512]{1,0:T(8,128)}, f32[288,128]{1,0:T(8,128)}, f32[8,128]{1,0:T(8,128)}) custom-call(s32[3]{0:T(128)} %pad_add_fusion.1.where_ref, bf16[288,512]{1,0:T(8,128)(2,1)} %fusion.8.refs_0_, ...), custom_call_target="tpu_custom_call", output_to_operand_aliasing={{0}: (9, {})} | custom-call | flops 1000000000 | bytes 1000000 | tf_op jit(solution)/shard_map/pallas_call | solution.py:275
  108.4 2.0 constant_dynamic-slice_fusion
  110.5 8.0 %collective-permute-done.9 = bf16[1536,320]{0,1:T(8,128)(2,1)} collective-permute-done((bf16[1536,320]{0,1:T(8,128)(2,1)}, bf16[1536,320]{0,1:T(8,128)(2,1)}, u32[]{:S(2)}, u32[]{:S(2)}) %collective-permute-start.9) | collective-permute-done | bytes 983072 | tf_op jit(solution)/shard_map/ppermute | solution.py:360
  118.5 4.5 %convolution_convert_fusion.1 = bf16[384,1536]{1,0:T(8,128)(2,1)} fusion(bf16[384,640]{1,0:T(8,128)(2,1)S(1)} %bitcast.87, bf16[1536,320]{0,1:T(8,128)(2,1)} %collective-permute-done.9, bf16[1536,320]{0,1:T(8,128)(2,1)} %bitcast.25, pred[]{:T(512)S(6)} %eq.141), kind=kOutput, calls=%fused_computation.1 | convolution fusion | flops 764411904 | bytes 3637249 | tf_op jit(solution)/shard_map/dot_general | solution.py:138
  123.5 1.9 slice.128.refs_0_
  125.4 2.4 %collective-permute-done.11.refs_10_.refs_11_ = bf16[1024,512]{1,0:T(8,128)(2,1)S(1)} collective-permute-done((bf16[1024,512]{1,0:T(8,128)(2,1)}, bf16[1024,512]{1,0:T(8,128)(2,1)S(1)}, u32[]{:S(2)}, u32[]{:S(2)}) %collective-permute-start.11) | collective-permute-done | bytes 1048608 | tf_op jit(solution)/shard_map/ppermute | solution.py:413
  129.3 3.2 %collective-permute-start.13 = (bf16[512,512]{1,0:T(8,128)(2,1)}, bf16[512,512]{1,0:T(8,128)(2,1)S(1)}, u32[]{:S(2)}, u32[]{:S(2)}) collective-permute-start(bf16[512,512]{1,0:T(8,128)(2,1)} %shard_map.155), channel_id=1, source_target_pairs={{0,40},{1,41},{2,42},{3,43},{4,44},{5,45},{6,46},{7,47},{8,32},{9,... | collective-permute-start | bytes 1572872 | tf_op jit(solution)/shard_map/ppermute | solution.py:431
  132.6 3.6 %convolution_convert_fusion.2 = bf16[384,1536]{1,0:T(8,128)(2,1)S(1)} fusion(bf16[384,640]{1,0:T(8,128)(2,1)} %bitcast.86, bf16[1536,320]{0,1:T(8,128)(2,1)} %collective-permute-done.9, bf16[1536,320]{0,1:T(8,128)(2,1)} %bitcast.25, pred[]{:T(512)S(6)} %eq.141), kind=kOutput, calls=%fused_computation.2 | convolution fusion | flops 764411904 | bytes 3637249 | tf_op jit(solution)/shard_map/dot_general | solution.py:138
  136.2 2.6 %fusion.refs_9_ = bf16[4,96,1536]{2,1,0:T(8,128)(2,1)} fusion(bf16[4,96,1536]{2,1,0:T(8,128)(2,1)S(1)} %bitcast.83, bf16[4,96,1536]{2,1,0:T(8,128)(2,1)} %collective-permute-done.10), kind=kLoop, calls=%fused_computation.4 | loop fusion | flops 2359296 | bytes 3538944 | tf_op jit(solution)/shard_map/convert_element_type | solution.py:449
  138.9 3.6 %collective-permute-done.12.refs_12_ = bf16[512,512]{1,0:T(8,128)(2,1)S(1)} collective-permute-done((bf16[512,512]{1,0:T(8,128)(2,1)}, bf16[512,512]{1,0:T(8,128)(2,1)S(1)}, u32[]{:S(2)}, u32[]{:S(2)}) %collective-permute-start.12) | collective-permute-done | bytes 524320 | tf_op jit(solution)/shard_map/ppermute | solution.py:430
  142.4 1.8 collective-permute-done.13.refs_13_
  145.0 10.9 %shard_map.156 = (bf16[128,12288]{1,0:T(8,128)(2,1)}, bf16[2,128,768]{2,1,0:T(8,128)(2,1)}, f32[288,512]{1,0:T(8,128)}, f32[288,128]{1,0:T(8,128)}, f32[8,128]{1,0:T(8,128)}) custom-call(s32[3]{0:T(128)} %pad_add_fusion.where_ref, bf16[288,512]{1,0:T(8,128)(2,1)} %fusion.8.refs_0_, ...), custom_call_target="tpu_custom_call", output_to_operand_aliasing={{0}: (9, {})} | custom-call | flops 1000000000 | bytes 1000000 | tf_op jit(solution)/shard_map/pallas_call | solution.py:275
  157.1 1.5 add_add_fusion
  158.6 5.6 %collective-permute-start.18 = (f32[32,576]{1,0:T(8,128)S(1)}, f32[32,576]{1,0:T(8,128)S(1)}, u32[]{:S(2)}, u32[]{:S(2)}) collective-permute-start(f32[32,576]{1,0:T(8,128)S(1)} %pad_maximum_fusion.2), channel_id=1, source_target_pairs={{32,0},{48,16},{64,32},{80,48},{96,64},{112,80},{128,96},{144,112}... | collective-permute-start | bytes 221192 | tf_op jit(solution)/shard_map/ppermute | solution.py:467
  164.2 2.2 %collective-permute-done.18 = f32[32,576]{1,0:T(8,128)S(1)} collective-permute-done((f32[32,576]{1,0:T(8,128)S(1)}, f32[32,576]{1,0:T(8,128)S(1)}, u32[]{:S(2)}, u32[]{:S(2)}) %collective-permute-start.18) | collective-permute-done | bytes 73760 | tf_op jit(solution)/shard_map/ppermute | solution.py:467
  167.2 5.3 %all-to-all-start.2 = ((bf16[4,96,1536]{2,1,0:T(8,128)(2,1)}), bf16[4,96,1536]{2,1,0:T(8,128)(2,1)S(1)}, u32[]{:S(2)}, u32[]{:S(2)}) async-start(bf16[4,96,1536]{2,1,0:T(8,128)(2,1)} %fusion.refs_9_), calls=%async_computation.2 | async-start | bytes 2359296 | tf_op jit(solution)/shard_map/all_to_all | solution.py:450
  173.9 1.4 fusion.33
  175.3 1.3 reshape.264
  179.3 1.6 slice_bitcast_fusion
  180.9 3.0 %shard_map.157 = bf16[128,12288]{1,0:T(8,128)(2,1)} custom-call(s32[9]{0:T(128)} %concatenate.41.where_ref, bf16[128,12288]{1,0:T(8,128)(2,1)} %get-tuple-element.28.grid_ref, bf16[1,128,768]{2,1,0:T(8,128)(2,1)} %collective-permute-done.14.refs_0_, bf16[3,128,768]{2,1,0:T(8,128)(2,1)} %collective-permute-done.15.refs_1_, ...), custom_call_target="tpu_custom_call", output_to_operand_aliasing={{}: (1, {})} | custom-call | flops 1000000 | bytes 1000000 | tf_op jit(solution)/shard_map/pallas_call | solution.py:113
  184.0 4.6 %all-to-all-done.2 = bf16[4,96,1536]{2,1,0:T(8,128)(2,1)S(1)} async-done(((bf16[4,96,1536]{2,1,0:T(8,128)(2,1)}), bf16[4,96,1536]{2,1,0:T(8,128)(2,1)S(1)}, u32[]{:S(2)}, u32[]{:S(2)}) %all-to-all-start.2) | async-done | bytes 1179680 | tf_op jit(solution)/shard_map/all_to_all | solution.py:450
  189.5 7.2 %all-to-all-start.3 = ((f32[16,1,6]{2,1,0:T(1,128)}), f32[16,1,6]{2,1,0:T(1,128)S(1)}, u32[]{:S(2)}, u32[]{:S(2)}) async-start(f32[16,1,6]{2,1,0:T(1,128)} %bitcast.34), calls=%async_computation.3 | async-start | bytes 16384 | tf_op jit(solution)/shard_map/all_to_all | solution.py:483
  197.5 7.6 %all-to-all-done.3 = f32[16,1,6]{2,1,0:T(1,128)S(1)} async-done(((f32[16,1,6]{2,1,0:T(1,128)}), f32[16,1,6]{2,1,0:T(1,128)S(1)}, u32[]{:S(2)}, u32[]{:S(2)}) %all-to-all-start.3) | async-done | bytes 416 | tf_op jit(solution)/shard_map/all_to_all | solution.py:483
  (140 shorter events, 23.9 us)
Async XLA Ops:
  0.6 36.0 %copy-start = (bf16[1,128,5120]{2,1,0:T(8,128)(2,1)S(1)}, bf16[1,128,5120]{2,1,0:T(8,128)(2,1)}, u32[]{:S(2)}) copy-start(bf16[1,128,5120]{2,1,0:T(8,128)(2,1)} %param.17) | copy-start | bytes 3932164
  0.6 7.0 %copy-start.19 = (bf16[1,128,64]{1,2,0:T(8,128)(2,1)S(1)}, bf16[1,128,64]{1,2,0:T(8,128)(2,1)}, u32[]{:S(2)}) copy-start(bf16[1,128,64]{1,2,0:T(8,128)(2,1)} %param.14) | copy-start | bytes 49156
  0.7 7.8 %copy-start.10 = (bf16[1,128,512]{2,1,0:T(8,128)(2,1)S(1)}, bf16[1,128,512]{2,1,0:T(8,128)(2,1)}, u32[]{:S(2)}) copy-start(bf16[1,128,512]{2,1,0:T(8,128)(2,1)} %param.13) | copy-start | bytes 393220
  0.7 9.2 %copy-start.1 = (bf16[1,128,8192]{2,1,0:T(8,128)(2,1)S(1)}, bf16[1,128,8192]{2,1,0:T(8,128)(2,1)}, u32[]{:S(2)}) copy-start(bf16[1,128,8192]{2,1,0:T(8,128)(2,1)} %param.12) | copy-start | bytes 6291460
  0.7 42.0 %collective-permute-start.2 = (bf16[128,12288]{1,0:T(8,128)(2,1)}, bf16[128,12288]{1,0:T(8,128)(2,1)}, u32[]{:S(2)}, u32[]{:S(2)}) collective-permute-start(bf16[128,12288]{1,0:T(8,128)(2,1)} %bitcast.69), channel_id=1, source_target_pairs={{0,16},{16,0},{32,48},{48,32},{64,80},{80,64},{96,112},{112,96},{1... | collective-permute-start | bytes 9437192 | tf_op jit(solution)/shard_map/ppermute | solution.py:357
  3.2 52.3 %collective-permute-start.4 = (bf16[1024,512]{1,0:T(8,128)(2,1)}, bf16[1024,512]{1,0:T(8,128)(2,1)}, u32[]{:S(2)}, u32[]{:S(2)}) collective-permute-start(bf16[1024,512]{1,0:T(8,128)(2,1)} %shard_map.146.refs_8_.refs_9_.refs_2_), channel_id=1, source_target_pairs={{0,64},{16,80},{32,96},{48,112},{64,128},{80,144},{96,160},{112,17... | collective-permute-start | bytes 3145736 | tf_op jit(solution)/shard_map/ppermute | solution.py:354
  4.7 59.6 %collective-permute-start.6 = (bf16[1024,512]{1,0:T(8,128)(2,1)}, bf16[1024,512]{1,0:T(8,128)(2,1)}, u32[]{:S(2)}, u32[]{:S(2)}) collective-permute-start(bf16[1024,512]{1,0:T(8,128)(2,1)} %shard_map.146.refs_8_.refs_9_.refs_2_), channel_id=1, source_target_pairs={{0,40},{1,41},{2,42},{3,43},{4,44},{5,45},{6,46},{7,47},{8,32},{9,... | collective-permute-start | bytes 3145736 | tf_op jit(solution)/shard_map/ppermute | solution.py:356
  9.9 4.7 %collective-permute-start = (bf16[128,576]{1,0:T(8,128)(2,1)}, bf16[128,576]{1,0:T(8,128)(2,1)}, u32[]{:S(2)}, u32[]{:S(2)}) collective-permute-start(bf16[128,576]{1,0:T(8,128)(2,1)} %pad_maximum_fusion.1), channel_id=1, source_target_pairs={{0,16},{16,0},{32,48},{48,32},{64,80},{80,64},{96,112},{112,96},{1... | collective-permute-start | bytes 442376 | tf_op jit(solution)/shard_map/ppermute | solution.py:344
  9.9 47.6 %collective-permute-start.3 = (bf16[128,8192]{1,0:T(8,128)(2,1)S(1)}, bf16[128,8192]{1,0:T(8,128)(2,1)}, u32[]{:S(2)}, u32[]{:S(2)}) collective-permute-start(bf16[128,8192]{1,0:T(8,128)(2,1)S(1)} %bitcast.79), channel_id=1, source_target_pairs={{0,16},{16,0},{32,48},{48,32},{64,80},{80,64},{96,112},{112,96},{1... | collective-permute-start | bytes 6291464 | tf_op jit(solution)/shard_map/ppermute | solution.py:358
  13.2 24.8 %copy-start.33 = (s32[96]{0:T(128)}, s32[96]{0:T(128)S(1)}, u32[]{:S(2)}) copy-start(s32[96]{0:T(128)S(1)} %get-tuple-element.83) | copy-start | bytes 1156
  16.4 16.0 %collective-permute-start.1 = (bf16[32,576]{1,0:T(8,128)(2,1)S(1)}, bf16[32,576]{1,0:T(8,128)(2,1)S(1)}, u32[]{:S(2)}, u32[]{:S(2)}) collective-permute-start(bf16[32,576]{1,0:T(8,128)(2,1)S(1)} %slice.117), channel_id=1, source_target_pairs={{0,32},{16,48},{32,64},{48,80},{64,96},{80,112},{96,128},{112,144}... | collective-permute-start | bytes 110600 | tf_op jit(solution)/shard_map/ppermute | solution.py:350
  32.4 31.9 %collective-permute-start.5 = (bf16[1024,512]{1,0:T(8,128)(2,1)}, bf16[1024,512]{1,0:T(8,128)(2,1)}, u32[]{:S(2)}, u32[]{:S(2)}) collective-permute-start(bf16[1024,512]{1,0:T(8,128)(2,1)} %shard_map.146.refs_8_.refs_9_.refs_2_), channel_id=1, source_target_pairs={{0,192},{16,208},{32,224},{48,240},{64,0},{80,16},{96,32},{112,48}... | collective-permute-start | bytes 3145736 | tf_op jit(solution)/shard_map/ppermute | solution.py:355
  34.4 1.5 copy-start.22
  42.6 9.5 %copy-start.12 = (bf16[32,576]{1,0:T(8,128)(2,1)S(1)}, bf16[32,576]{1,0:T(8,128)(2,1)}, u32[]{:S(2)}) copy-start(bf16[32,576]{1,0:T(8,128)(2,1)} %copy-done.11) | copy-start | bytes 110596
  42.6 36.3 %all-to-all-start = ((bf16[16,248,128]{2,1,0:T(8,128)(2,1)}), bf16[16,248,128]{2,1,0:T(8,128)(2,1)}, u32[]{:S(2)}, u32[]{:S(2)}) async-start(bf16[16,248,128]{2,1,0:T(8,128)(2,1)} %shard_map.151), calls=%async_computation | async-start | bytes 2031616 | tf_op jit(solution)/shard_map/all_to_all | solution.py:392
  55.4 41.3 %collective-permute-start.7 = (bf16[1024,512]{1,0:T(8,128)(2,1)}, bf16[1024,512]{1,0:T(8,128)(2,1)}, u32[]{:S(2)}, u32[]{:S(2)}) collective-permute-start(bf16[1024,512]{1,0:T(8,128)(2,1)} %collective-permute-done.4.refs_9_.refs_10_), channel_id=1, source_target_pairs={{0,64},{16,80},{32,96},{48,112},{64,128},{80,144},{96,160},{112,17... | collective-permute-start | bytes 3145736 | tf_op jit(solution)/shard_map/ppermute | solution.py:412
  56.9 39.8 %collective-permute-start.8 = (bf16[1024,512]{1,0:T(8,128)(2,1)}, bf16[1024,512]{1,0:T(8,128)(2,1)}, u32[]{:S(2)}, u32[]{:S(2)}) collective-permute-start(bf16[1024,512]{1,0:T(8,128)(2,1)} %collective-permute-done.4.refs_9_.refs_10_), channel_id=1, source_target_pairs={{0,40},{1,41},{2,42},{3,43},{4,44},{5,45},{6,46},{7,47},{8,32},{9,... | collective-permute-start | bytes 3145736 | tf_op jit(solution)/shard_map/ppermute | solution.py:414
  86.9 20.5 %all-to-all-start.1 = ((bf16[8,96,640]{2,1,0:T(8,128)(2,1)}), bf16[8,96,640]{2,1,0:T(8,128)(2,1)S(1)}, u32[]{:S(2)}, u32[]{:S(2)}) async-start(bf16[8,96,640]{2,1,0:T(8,128)(2,1)} %reshape.252), calls=%async_computation.1 | async-start | bytes 1966080 | tf_op jit(solution)/shard_map/all_to_all | solution.py:423
  92.1 26.3 %collective-permute-start.9 = (bf16[1536,320]{0,1:T(8,128)(2,1)}, bf16[1536,320]{0,1:T(8,128)(2,1)}, u32[]{:S(2)}, u32[]{:S(2)}) collective-permute-start(bf16[1536,320]{0,1:T(8,128)(2,1)} %bitcast.25), channel_id=1, source_target_pairs={{0,32},{16,48},{32,0},{48,16},{64,96},{80,112},{96,64},{112,80},{1... | collective-permute-start | bytes 2949128 | tf_op jit(solution)/shard_map/ppermute | solution.py:360
  96.7 31.1 %collective-permute-start.11 = (bf16[1024,512]{1,0:T(8,128)(2,1)}, bf16[1024,512]{1,0:T(8,128)(2,1)S(1)}, u32[]{:S(2)}, u32[]{:S(2)}) collective-permute-start(bf16[1024,512]{1,0:T(8,128)(2,1)} %collective-permute-done.6.refs_13_.refs_14_), channel_id=1, source_target_pairs={{0,192},{16,208},{32,224},{48,240},{64,0},{80,16},{96,32},{112,48}... | collective-permute-start | bytes 3145736 | tf_op jit(solution)/shard_map/ppermute | solution.py:413
  122.9 13.3 %collective-permute-start.10 = (bf16[4,96,1536]{2,1,0:T(8,128)(2,1)}, bf16[4,96,1536]{2,1,0:T(8,128)(2,1)}, u32[]{:S(2)}, u32[]{:S(2)}) collective-permute-start(bf16[4,96,1536]{2,1,0:T(8,128)(2,1)} %bitcast.28), channel_id=1, source_target_pairs={{0,16},{16,0},{32,48},{48,32},{64,80},{80,64},{96,112},{112,96},{1... | collective-permute-start | bytes 3538952 | tf_op jit(solution)/shard_map/ppermute | solution.py:447
  127.8 8.4 %copy-start.3 = (bf16[1024,512]{1,0:T(8,128)(2,1)}, bf16[1024,512]{1,0:T(8,128)(2,1)S(1)}, u32[]{:S(2)}) copy-start(bf16[1024,512]{1,0:T(8,128)(2,1)S(1)} %collective-permute-done.11.refs_10_.refs_11_) | copy-start | bytes 3145732
  128.7 13.7 %collective-permute-start.12 = (bf16[512,512]{1,0:T(8,128)(2,1)}, bf16[512,512]{1,0:T(8,128)(2,1)S(1)}, u32[]{:S(2)}, u32[]{:S(2)}) collective-permute-start(bf16[512,512]{1,0:T(8,128)(2,1)} %shard_map.154), channel_id=1, source_target_pairs={{0,192},{16,208},{32,224},{48,240},{64,0},{80,16},{96,32},{112,48}... | collective-permute-start | bytes 1572872 | tf_op jit(solution)/shard_map/ppermute | solution.py:430
  129.3 14.9 %collective-permute-start.13 = (bf16[512,512]{1,0:T(8,128)(2,1)}, bf16[512,512]{1,0:T(8,128)(2,1)S(1)}, u32[]{:S(2)}, u32[]{:S(2)}) collective-permute-start(bf16[512,512]{1,0:T(8,128)(2,1)} %shard_map.155), channel_id=1, source_target_pairs={{0,40},{1,41},{2,42},{3,43},{4,44},{5,45},{6,46},{7,47},{8,32},{9,... | collective-permute-start | bytes 1572872 | tf_op jit(solution)/shard_map/ppermute | solution.py:431
  142.4 1.8 copy-start.8
  145.0 10.9 %copy-start.14 = (f32[288,128]{1,0:T(8,128)S(1)}, f32[288,128]{1,0:T(8,128)}, u32[]{:S(2)}) copy-start(f32[288,128]{1,0:T(8,128)} %get-tuple-element.37) | copy-start | bytes 442372
  145.0 10.9 %copy-start.15 = (f32[288,128]{1,0:T(8,128)S(1)}, f32[288,128]{1,0:T(8,128)}, u32[]{:S(2)}) copy-start(f32[288,128]{1,0:T(8,128)} %get-tuple-element.38) | copy-start | bytes 442372
  145.0 11.0 %copy-start.16 = (f32[288,128]{1,0:T(8,128)S(1)}, f32[288,128]{1,0:T(8,128)}, u32[]{:S(2)}) copy-start(f32[288,128]{1,0:T(8,128)} %get-tuple-element.39) | copy-start | bytes 442372
  145.0 12.0 %copy-start.6 = (f32[288,512]{1,0:T(8,128)S(1)}, f32[288,512]{1,0:T(8,128)}, u32[]{:S(2)}) copy-start(f32[288,512]{1,0:T(8,128)} %get-tuple-element.33) | copy-start | bytes 1769476
  145.0 12.0 %copy-start.7 = (f32[288,512]{1,0:T(8,128)S(1)}, f32[288,512]{1,0:T(8,128)}, u32[]{:S(2)}) copy-start(f32[288,512]{1,0:T(8,128)} %get-tuple-element.34) | copy-start | bytes 1769476
  158.6 7.8 %collective-permute-start.18 = (f32[32,576]{1,0:T(8,128)S(1)}, f32[32,576]{1,0:T(8,128)S(1)}, u32[]{:S(2)}, u32[]{:S(2)}) collective-permute-start(f32[32,576]{1,0:T(8,128)S(1)} %pad_maximum_fusion.2), channel_id=1, source_target_pairs={{32,0},{48,16},{64,32},{80,48},{96,64},{112,80},{128,96},{144,112}... | collective-permute-start | bytes 221192 | tf_op jit(solution)/shard_map/ppermute | solution.py:467
  167.2 9.7 %collective-permute-start.19 = (f32[128,576]{1,0:T(8,128)}, f32[128,576]{1,0:T(8,128)}, u32[]{:S(2)}, u32[]{:S(2)}) collective-permute-start(f32[128,576]{1,0:T(8,128)} %fusion.9), channel_id=1, source_target_pairs={{0,16},{16,0},{32,48},{48,32},{64,80},{80,64},{96,112},{112,96},{1... | collective-permute-start | bytes 884744 | tf_op jit(solution)/shard_map/ppermute | solution.py:472
  167.2 21.3 %all-to-all-start.2 = ((bf16[4,96,1536]{2,1,0:T(8,128)(2,1)}), bf16[4,96,1536]{2,1,0:T(8,128)(2,1)S(1)}, u32[]{:S(2)}, u32[]{:S(2)}) async-start(bf16[4,96,1536]{2,1,0:T(8,128)(2,1)} %fusion.refs_9_), calls=%async_computation.2 | async-start | bytes 2359296 | tf_op jit(solution)/shard_map/all_to_all | solution.py:450
  173.2 7.7 %collective-permute-start.16 = (bf16[2,128,768]{2,1,0:T(8,128)(2,1)}, bf16[2,128,768]{2,1,0:T(8,128)(2,1)}, u32[]{:S(2)}, u32[]{:S(2)}) collective-permute-start(bf16[2,128,768]{2,1,0:T(8,128)(2,1)} %get-tuple-element.31), channel_id=1, source_target_pairs={{0,16},{16,0},{32,48},{48,32},{64,80},{80,64},{96,112},{112,96},{1... | collective-permute-start | bytes 1179656 | tf_op jit(solution)/shard_map/ppermute | solution.py:436
  173.4 7.4 %collective-permute-start.15 = (bf16[3,128,768]{2,1,0:T(8,128)(2,1)}, bf16[3,128,768]{2,1,0:T(8,128)(2,1)}, u32[]{:S(2)}, u32[]{:S(2)}) collective-permute-start(bf16[3,128,768]{2,1,0:T(8,128)(2,1)} %get-tuple-element.30), channel_id=1, source_target_pairs={{0,16},{16,0},{32,48},{48,32},{64,80},{80,64},{96,112},{112,96},{1... | collective-permute-start | bytes 1769480 | tf_op jit(solution)/shard_map/ppermute | solution.py:428
  173.7 7.2 %collective-permute-start.14 = (bf16[1,128,768]{2,1,0:T(8,128)(2,1)}, bf16[1,128,768]{2,1,0:T(8,128)(2,1)}, u32[]{:S(2)}, u32[]{:S(2)}) collective-permute-start(bf16[1,128,768]{2,1,0:T(8,128)(2,1)} %get-tuple-element.29), channel_id=1, source_target_pairs={{0,16},{16,0},{32,48},{48,32},{64,80},{80,64},{96,112},{112,96},{1... | collective-permute-start | bytes 589832 | tf_op jit(solution)/shard_map/ppermute | solution.py:427
  176.6 4.3 %collective-permute-start.17 = (bf16[2,128,768]{2,1,0:T(8,128)(2,1)}, bf16[2,128,768]{2,1,0:T(8,128)(2,1)}, u32[]{:S(2)}, u32[]{:S(2)}) collective-permute-start(bf16[2,128,768]{2,1,0:T(8,128)(2,1)} %get-tuple-element.32), channel_id=1, source_target_pairs={{0,16},{16,0},{32,48},{48,32},{64,80},{80,64},{96,112},{112,96},{1... | collective-permute-start | bytes 1179656 | tf_op jit(solution)/shard_map/ppermute | solution.py:462
  183.9 4.8 %copy-start.13 = (bf16[1,1,96,1536]{3,2,1,0:T(8,128)(2,1)S(1)}, bf16[1,1,96,1536]{3,2,1,0:T(8,128)(2,1)}, u32[]{:S(2)}) copy-start(bf16[1,1,96,1536]{3,2,1,0:T(8,128)(2,1)} %param.20) | copy-start | bytes 884740
  183.9 12.9 %copy-start.32 = (f32[96]{0:T(128)S(1)}, f32[96]{0:T(128)}, u32[]{:S(2)}) copy-start(f32[96]{0:T(128)} %reshape.264) | copy-start | bytes 1156
  183.9 22.6 %copy-start.18 = (pred[128,96]{0,1:T(32,128)(4,1)S(1)}, pred[128,96]{0,1:T(32,128)(4,1)}, u32[]{:S(2)}) copy-start(pred[128,96]{0,1:T(32,128)(4,1)} %copy-done.17) | copy-start | bytes 36868
  183.9 22.6 %copy-start.21 = (s32[128]{0:T(128)S(1)}, s32[128]{0:T(128)}, u32[]{:S(2)}) copy-start(s32[128]{0:T(128)} %copy-done.20) | copy-start | bytes 1540
  183.9 22.6 %copy-start.23 = (s32[128]{0:T(128)S(1)}, s32[128]{0:T(128)}, u32[]{:S(2)}) copy-start(s32[128]{0:T(128)} %copy-done.22) | copy-start | bytes 1540
  183.9 22.6 %copy-start.25 = (s32[128]{0:T(128)S(1)}, s32[128]{0:T(128)}, u32[]{:S(2)}) copy-start(s32[128]{0:T(128)} %copy-done.24) | copy-start | bytes 1540
  183.9 22.6 %copy-start.27 = (s32[128]{0:T(128)S(1)}, s32[128]{0:T(128)}, u32[]{:S(2)}) copy-start(s32[128]{0:T(128)} %copy-done.26) | copy-start | bytes 1540
  183.9 22.6 %copy-start.29 = (s32[128]{0:T(128)S(1)}, s32[128]{0:T(128)}, u32[]{:S(2)}) copy-start(s32[128]{0:T(128)} %copy-done.28) | copy-start | bytes 1540
  183.9 22.6 %copy-start.31 = (s32[128]{0:T(128)S(1)}, s32[128]{0:T(128)}, u32[]{:S(2)}) copy-start(s32[128]{0:T(128)} %copy-done.30) | copy-start | bytes 1540
  183.9 22.6 %copy-start.34 = (s32[96]{0:T(128)S(1)}, s32[96]{0:T(128)}, u32[]{:S(2)}) copy-start(s32[96]{0:T(128)} %copy-done.33) | copy-start | bytes 1156
  189.5 15.6 %all-to-all-start.3 = ((f32[16,1,6]{2,1,0:T(1,128)}), f32[16,1,6]{2,1,0:T(1,128)S(1)}, u32[]{:S(2)}, u32[]{:S(2)}) async-start(f32[16,1,6]{2,1,0:T(1,128)} %bitcast.34), calls=%async_computation.3 | async-start | bytes 16384 | tf_op jit(solution)/shard_map/all_to_all | solution.py:483
  (11 other events, 11.0 us)

commit v2 on v1

--- a/solution.py
+++ b/solution.py
@@ -27,6 +27,7 @@
 ROWS = 2 * TOK + WIN
 SPAN = TOK + WIN
 SCALE = (NOPE + ROPE) ** (-0.5)
+CHIP_AT, HALF_AT = 9, 10
 COST = pl.CostEstimate(flops=1_000_000, bytes_accessed=1_000_000, transcendentals=0)
 
 
@@ -82,7 +83,56 @@
     )(w_key, w_value)
 
 
-def place_body(counts, where_ref, grid_ref, *refs):
+def join_body(latent_ref, rope_ref, out_ref):
+    out_ref[:, :LATENT] = latent_ref[...]
+    rope = rope_ref[...].astype(jnp.float32).T
+    out_ref[:, LATENT:] = jnp.concatenate([rope, jnp.zeros_like(rope)], axis=1).astype(jnp.bfloat16)
+
+
+def join(latent, rope_turned):
+    return pl.pallas_call(
+        join_body,
+        out_shape=jax.ShapeDtypeStruct((TOK, LATENT + NOPE), jnp.bfloat16),
+        compiler_params=pltpu.CompilerParams(vmem_limit_bytes=60 * 1024 * 1024),
+        cost_estimate=COST,
+    )(latent, rope_turned)
+
+
+def prepare_body(where_ref, mine_ref, twin_ref, halo_ref, latent_ref, low_ref, high_ref):
+    core = where_ref[0]
+
+    def put(at, ref):
+        rows = pl.ds(at, ref.shape[0])
+        latent_ref[rows, :] = ref[:, :LATENT]
+        rope = ref[:, LATENT:]
+        low_ref[rows, :] = rope
+        high_ref[rows, :] = pltpu.roll(rope.astype(jnp.float32), ROPE, 1)
+
+    put(0, halo_ref)
+    for own in range(2):
+
+        @pl.when(core == own)
+        def _():
+            put(WIN + own * TOK, mine_ref)
+            put(WIN + (1 - own) * TOK, twin_ref)
+
+
+def prepare(where, mine, twin_rows, halo):
+    return pl.pallas_call(
+        prepare_body,
+        in_specs=[pl.BlockSpec(memory_space=pltpu.SMEM)]
+        + [pl.BlockSpec(memory_space=pltpu.VMEM)] * 3,
+        out_shape=[
+            jax.ShapeDtypeStruct((ROWS, LATENT), jnp.bfloat16),
+            jax.ShapeDtypeStruct((ROWS, NOPE), jnp.bfloat16),
+            jax.ShapeDtypeStruct((ROWS, NOPE), jnp.float32),
+        ],
+        compiler_params=pltpu.CompilerParams(vmem_limit_bytes=60 * 1024 * 1024),
+        cost_estimate=COST,
+    )(where, mine, twin_rows, halo)
+
+
+def place_body(counts, where_ref, grid_ref, after_ref, *refs):
     parts, out_ref = refs[: len(counts)], refs[len(counts)]
     held, in_sems, out_sems = refs[len(counts) + 1 :]
     core = where_ref[0]
@@ -108,14 +158,14 @@
         leave.wait()
 
 
-def place(where, query_grad, parts):
+def place(where, query_grad, parts, after):
     counts = tuple(part.shape[0] for part in parts)
     return pl.pallas_call(
         functools.partial(place_body, counts),
         grid_spec=pltpu.PrefetchScalarGridSpec(
             num_scalar_prefetch=1,
             grid=(),
-            in_specs=[pl.BlockSpec(memory_space=pl.ANY)] * (1 + len(parts)),
+            in_specs=[pl.BlockSpec(memory_space=pl.ANY)] * (2 + len(parts)),
             out_specs=pl.BlockSpec(memory_space=pl.ANY),
             scratch_shapes=[
                 pltpu.VMEM((sum(counts), TOK, QW), jnp.bfloat16),
@@ -126,7 +176,7 @@
         out_shape=jax.ShapeDtypeStruct(query_grad.shape, query_grad.dtype),
         input_output_aliases={1: 0},
         cost_estimate=COST,
-    )(where, query_grad, *parts)
+    )(where, query_grad, after, *parts)
 
 
 NT = (((1,), (1,)), ((), ()))
@@ -138,15 +188,22 @@
     return lax.dot_general(a, b, dims, preferred_element_type=jnp.float32)
 
 
-def attend_body(count, skipped, where_ref, *refs):
-    latent_ref, rope_low_ref, rope_high_ref, bias_ref = refs[:4]
-    q_ref, d_ref, twin_q_ref, twin_d_ref = refs[4:8]
-    weights = refs[8 + skipped : 8 + skipped + 2 * count]
-    at = 8 + skipped + 2 * count
+def attend_body(count, base, skipped, where_ref, *refs):
+    latent_ref, rope_low_ref, rope_high_ref = refs[:3]
+    q_ref, d_ref, twin_q_ref, twin_d_ref = refs[3:7]
+    weights = refs[7 + skipped : 7 + skipped + 2 * count]
+    at = 7 + skipped + 2 * count
+    sums = refs[at : at + 2] if skipped else ()
+    at += len(sums)
     query_out, twin_out, latent_out, rope_out, mark_out = refs[at : at + 5]
     wk_ref, wv_ref, q_both, d_both, grad_both, dk_ref, dv_ref = refs[at + 5 :]
     step = pl.program_id(0)
     core = where_ref[0]
+    key_at = lax.broadcasted_iota(jnp.int32, (SPAN, TOK), 0)
+    query_at = lax.broadcasted_iota(jnp.int32, (SPAN, TOK), 1)
+    inside = (key_at > query_at) & (key_at <= query_at + WIN)
+    started = key_at >= jnp.where(where_ref[CHIP_AT] > 0, 0, WIN)
+    masks = (inside & started, inside)
 
     for i in range(count):
 
@@ -197,7 +254,7 @@
                 span = slice(s * TOK, s * TOK + SPAN)
                 q = q_both[s, :, start : start + 2 * NOPE]
                 d = d_both[s, :, head * VDIM : (head + 1) * VDIM]
-                scores = dot(wide[span], q, NT) * SCALE + bias_ref[s]
+                scores = jnp.where(masks[s], dot(wide[span], q, NT) * SCALE, -jnp.inf)
                 shifted = jnp.exp(scores - jnp.max(scores, axis=0, keepdims=True))
                 inverse = 1.0 / jnp.sum(shifted, axis=0, keepdims=True)
                 prob_grad = dot(value[span], d, NT)
@@ -231,8 +288,8 @@
 
     @pl.when(step == 0)
     def _():
-        latent_out[...] = latent_sum
-        rope_out[...] = rope_sum
+        latent_out[...] = sums[0][...] + latent_sum if sums else latent_sum
+        rope_out[...] = sums[1][...] + rope_sum if sums else rope_sum
         mark_out[...] = jnp.zeros_like(mark_out)
 
     @pl.when(step > 0)
@@ -249,18 +306,16 @@
 
 
 def attend(
-    where, shared, query, out_grad, twin_query, twin_grad, query_grad, weights, after=(), heavy=1
+    where, base, shared, query, out_grad, twin_query, twin_grad, weights, earlier=(), after=(), heavy=1
 ):
     count = len(weights)
-    chained = query_grad is not None
-    skipped = ([query_grad] if chained else []) + list(after)
-    head_block = lambda width: pl.BlockSpec((TOK, width), lambda g, w: (0, 2 * w[1 + g] + w[0]))
+    skipped = list(earlier[:1]) + list(after)
+    head_block = lambda width: pl.BlockSpec((TOK, width), lambda g, w: (0, 2 * w[base + g] + w[0]))
     whole = lambda shape: pl.BlockSpec(shape, lambda g, w: (0,) * len(shape))
     in_specs = [
         whole((ROWS, LATENT)),
         whole((ROWS, NOPE)),
         whole((ROWS, NOPE)),
-        whole((2, SPAN, TOK)),
         head_block(QW),
         head_block(VW),
         head_block(QW),
@@ -272,8 +327,11 @@
         in_specs.append(pl.BlockSpec((LATENT, VW), lambda g, w, at=key_at: (at, 0)))
         in_specs.append(pl.BlockSpec((LATENT, VW), lambda g, w, at=value_at: (at, 0)))
         operands += [key_part, value_part]
-    return pl.pallas_call(
-        functools.partial(attend_body, count, len(skipped)),
+    if earlier:
+        in_specs += [whole((ROWS, LATENT)), whole((ROWS, NOPE))]
+        operands += earlier[1:]
+    query_grad, part, latent_sum, rope_sum, mark = pl.pallas_call(
+        functools.partial(attend_body, count, base, len(skipped)),
         grid_spec=pltpu.PrefetchScalarGridSpec(
             num_scalar_prefetch=1,
             grid=(count,),
@@ -302,12 +360,54 @@
             jax.ShapeDtypeStruct((ROWS, NOPE), jnp.float32),
             jax.ShapeDtypeStruct((8, NOPE), jnp.float32),
         ],
-        input_output_aliases={9: 0} if chained else {},
+        input_output_aliases={8: 0} if earlier else {},
         compiler_params=pltpu.CompilerParams(vmem_limit_bytes=60 * 1024 * 1024),
         cost_estimate=pl.CostEstimate(
             flops=heavy * count * 500_000_000, bytes_accessed=count * 500_000, transcendentals=0
         ),
     )(*operands)
+    return query_grad, latent_sum, rope_sum, part, mark
+
+
+def terms_body(where_ref, rows_ref, own_ref, other_ref, *refs):
+    out_ref = refs[-1]
+    here = where_ref[HALF_AT] * (EXP * CAP)
+    there = (1 - where_ref[HALF_AT]) * (EXP * CAP)
+
+    def rows(at):
+        part = rows_ref[:, 0, pl.ds(pl.multiple_of(at, EXP * CAP), EXP * CAP), :]
+        return part.reshape(4 * EXP * CAP, -1)
+
+    total = dot(rows(here), own_ref[...], NN) + dot(rows(there), other_ref[...], NN)
+    out_ref[...] = total.astype(jnp.bfloat16).reshape(out_ref.shape)
+
+
+def terms(where, twin, slices, own_down, other_down, after):
+    rows = slices.reshape(4, 2, 2 * EXP * CAP, -1)
+    depth = rows.shape[3]
+    weight = pl.BlockSpec((depth, FFH), lambda g, w: (0, 0))
+    number = (lambda w: 1 - w[0]) if twin else (lambda w: w[0])
+    return pl.pallas_call(
+        terms_body,
+        grid_spec=pltpu.PrefetchScalarGridSpec(
+            num_scalar_prefetch=1,
+            grid=(1,),
+            in_specs=[
+                pl.BlockSpec(
+                    (4, 1, 2 * EXP * CAP, depth), lambda g, w: (0, number(w), 0, 0)
+                ),
+                weight,
+                weight,
+            ]
+            + [pl.BlockSpec(memory_space=pl.ANY)] * len(after),
+            out_specs=pl.BlockSpec((4, EXP * CAP, FFH), lambda g, w: (0, 0, 0)),
+        ),
+        out_shape=jax.ShapeDtypeStruct((4, EXP * CAP, FFH), jnp.bfloat16),
+        compiler_params=pltpu.CompilerParams(vmem_limit_bytes=60 * 1024 * 1024),
+        cost_estimate=pl.CostEstimate(
+            flops=100_000_000, bytes_accessed=100_000, transcendentals=0
+        ),
+    )(where, rows, own_down, other_down, *after)
 
 
 def local(
@@ -334,21 +434,25 @@
     def group(step, flip):
         return 2 * ((x + step) % 4) + (half ^ flip)
 
-    def spots(*groups):
-        return jnp.stack([core, *groups]).astype(jnp.int32)
+    groups = [
+        group(0, 0),
+        group(-1, 0),
+        group(1, 0),
+        group(0, 1),
+        group(2, 0),
+        group(-1, 1),
+        group(1, 1),
+        group(2, 1),
+    ]
+    where = jnp.stack([core, *groups, chip, half]).astype(jnp.int32)
 
     def both(stack):
         return ((stack, 0), (stack, 1))
 
-    mine = jnp.concatenate([latent, rope_key], axis=1)
+    mine = join(latent, rope_key.T)
     twin_rows = lax.ppermute(mine, "ctx", TWIN)
-    chip_rows = jnp.where(
-        core == 0,
-        jnp.concatenate([mine, twin_rows], axis=0),
-        jnp.concatenate([twin_rows, mine], axis=0),
-    )
     halo = lax.ppermute(
-        chip_rows[2 * TOK - WIN :], "ctx", [(i, i + 2) for i in range(CTX - 2)]
+        jnp.where(core == 0, twin_rows[TOK - WIN :], mine[TOK - WIN :]), "ctx", [(i, i + 2) for i in range(CTX - 2)]
     )
     own = stack(w_key, w_value)
     before = lax.ppermute(own, "ctx", RIGHT)
@@ -356,17 +460,12 @@
     beside = lax.ppermute(own, ("ctx", "exp"), ACROSS)
     twin_query = lax.ppermute(query, "ctx", TWIN)
     twin_grad = lax.ppermute(out_grad, "ctx", TWIN)
-    down = w_down[0]
+    down = w_down[0].T
     other_down = lax.ppermute(down, "ctx", [(i, i ^ 2) for i in range(CTX)])
-    down = jnp.where(
-        half == 0,
-        jnp.concatenate([down, other_down], axis=1),
-        jnp.concatenate([other_down, down], axis=1),
-    )
 
     share = EXPERTS // EXP
     slots = jnp.arange(EXP * CAP, dtype=jnp.int32)[None, :]
-    ids = tie(expert_ids, halo)
+    ids = tie(expert_ids, own)
     match = [ids[:, k : k + 1] == slots // CAP * share for k in range(TOPK)]
     live = functools.reduce(jnp.logical_or, match)
     token_at = jnp.arange(TOK, dtype=jnp.int32)
@@ -391,35 +490,21 @@
     outbound = tie(outbound, twin_query, own)
     routed = lax.all_to_all(outbound, "exp", split_axis=0, concat_axis=0, tiled=True)
 
-    rows = jnp.concatenate([halo, chip_rows], axis=0)
-    rope_rows = rows[:, LATENT:]
-    blank = jnp.zeros_like(rope_rows)
-    key_at = jnp.arange(SPAN, dtype=jnp.int32)[:, None]
-    query_at = jnp.arange(TOK, dtype=jnp.int32)[None, :]
-    inside = (key_at > query_at) & (key_at <= query_at + WIN)
-    first = inside & ((chip > 0) | (key_at >= WIN))
-    shared = (
-        rows[:, :LATENT],
-        jnp.concatenate([rope_rows, blank], axis=1),
-        jnp.concatenate([blank, rope_rows], axis=1).astype(jnp.float32),
-        jnp.where(jnp.stack([first, inside]), 0.0, -jnp.inf).astype(jnp.float32),
-    )
+    shared = prepare(where, mine, twin_rows, halo)
     common = (shared, query, out_grad, twin_query, twin_grad)
 
-    where_a = spots(group(0, 0))
-    query_grad, part_a, latent_a, rope_a, mark_a = attend(where_a, *common, None, [both(own)])
+    *sums, part_a, mark_a = attend(where, 1, *common, [both(own)])
 
     opposite = lax.ppermute(before, "ctx", RIGHT)
     beside_after = lax.ppermute(beside, "ctx", LEFT)
     beside_before = lax.ppermute(before, ("ctx", "exp"), ACROSS)
-    where_b = spots(group(-1, 0), group(1, 0), group(0, 1))
-    query_grad, part_b, latent_b, rope_b, mark_b = attend(
-        where_b, *common, query_grad, [both(before), both(after), both(beside)], heavy=10
-    )
-    routed = tie(routed, mark_b)
+    *sums, part_b, mark_b = attend(
+        where, 2, *common, [both(before), both(after), both(beside)], sums, heavy=10
+    )
+    routed = tie(routed, mark_b, other_down)
     row_gate = routed[:, CAP * tiles, :CAP].reshape(EXP * CAP, 1)
     slices = routed[:, : CAP * tiles].reshape(EXP * CAP, 4, 2, 2, -1)
-    slices = slices.transpose(1, 3, 0, 2, 4).reshape(CHIPS, EXP * CAP, -1)
+    slices = slices.transpose(1, 3, 2, 0, 4).reshape(CHIPS, 2 * EXP * CAP, -1)
     slices = lax.all_to_all(
         slices, "ctx", split_axis=0, concat_axis=0, tiled=True, axis_index_groups=RING
     )
@@ -427,23 +512,15 @@
     part_a = lax.ppermute(part_a, "ctx", TWIN)
     part_b = lax.ppermute(part_b, "ctx", TWIN)
 
-    last_key = lax.ppermute(tie(beside_after[:LATENT], mark_b), "ctx", LEFT)
-    last_value = lax.ppermute(tie(opposite[LATENT:], mark_b), ("ctx", "exp"), ACROSS)
-    where_c = spots(group(2, 0), group(-1, 1))
-    query_grad, part_c, latent_c, rope_c, mark_c = attend(
-        where_c, *common, query_grad, [both(opposite), both(beside_before)], (mark_b,)
-    )
-    part_c = lax.ppermute(part_c, "ctx", TWIN)
-
-    slices = tie(slices, mark_c).reshape(4, 2, EXP * CAP, -1)
-
-    def terms(number):
-        rows = lax.dynamic_index_in_dim(slices, number, 1, keepdims=False)
-        rows = rows.reshape(4 * EXP * CAP, -1)
-        return dot(rows, down, NT).astype(jnp.bfloat16).reshape(4, EXP * CAP, FFH)
-
-    give = terms(1 - core)
-    keep = terms(core)
+    key_half = tie(beside_after[:LATENT], mark_b)
+    value_half = tie(opposite[LATENT:], mark_b)
+    last_key = lax.ppermute(key_half, "ctx", LEFT)
+    last_value = lax.ppermute(value_half, ("ctx", "exp"), ACROSS)
+
+    give = terms(
+        where, True, slices, down, other_down, (mark_b, beside_before, key_half, value_half)
+    )
+    keep = terms(where, False, slices, down, other_down, (give,))
     taken = lax.ppermute(give, "ctx", TWIN)
 
     keep = (keep.astype(jnp.float32) + taken.astype(jnp.float32)).astype(jnp.bfloat16)
@@ -451,19 +528,24 @@
         keep, "ctx", split_axis=0, concat_axis=0, tiled=True, axis_index_groups=RING_CORE
     )
 
-    where_d = spots(group(1, 1), group(2, 1))
-    query_grad, part_d, latent_d, rope_d, mark_d = attend(
-        where_d,
+    *sums, part_c, mark_c = attend(
+        where,
+        5,
         *common,
-        query_grad,
-        [both(beside_after), ((last_key, 0), (last_value, 0))],
+        [
+            both(opposite),
+            both(beside_before),
+            both(beside_after),
+            ((last_key, 0), (last_value, 0)),
+        ],
+        sums,
         (keep,),
     )
-    part_d = lax.ppermute(part_d, "ctx", TWIN)
-    rope_sum = rope_a + rope_b + rope_c + rope_d
-    sums = jnp.concatenate(
-        [latent_a + latent_b + latent_c + latent_d, rope_sum[:, :ROPE] + rope_sum[:, ROPE:]], axis=1
-    )
+    part_c = lax.ppermute(part_c, "ctx", TWIN)
+
+    query_grad, latent_sum, rope_sum = sums
+    latent_sum = tie(latent_sum, pieces)
+    sums = jnp.concatenate([latent_sum, rope_sum[:, :ROPE] + rope_sum[:, ROPE:]], axis=1)
     back = lax.ppermute(sums[:WIN], "ctx", [(i + 2, i) for i in range(CTX - 2)])
     low = sums[WIN : WIN + TOK]
     high = sums[WIN + TOK :]
@@ -471,18 +553,13 @@
     kept = jnp.where(core == 0, low, high)
     given = lax.ppermute(jnp.where(core == 0, high, low), "ctx", TWIN)
     total = (kept + given).astype(jnp.bfloat16)
-    query_grad = place(
-        jnp.concatenate([where_a, where_b[1:], where_c[1:], where_d[1:]]),
-        query_grad,
-        (part_a, part_b, part_c, part_d),
-    )
-
     raw_grad = jnp.sum(pieces.astype(jnp.float32), axis=0)
     gate_part = jnp.sum(saved_hidden[0, 0].astype(jnp.float32) * raw_grad, axis=1)
     hidden_grad = (row_gate.astype(jnp.float32) * raw_grad).astype(jnp.bfloat16)
     returned = lax.all_to_all(
         gate_part.reshape(EXP, CAP), "exp", split_axis=0, concat_axis=0, tiled=True
     )
+    query_grad = place(where, query_grad, (part_a, part_b, part_c), gate_part[None])
     found = token_hot.astype(jnp.float32) * returned.reshape(1, -1)
     gate_grad = jnp.stack(
         [jnp.sum(jnp.where(match[k], found, 0.0), axis=1) for k in range(TOPK)], axis=1

time: 211 us -> 168 us (0.80)
  waiting for transfers between devices: 41.6 us -> 20.2 us
  Pallas kernels: 48.5 us -> 59 us
  other arithmetic: 25.1 us -> 15.3 us
  matrix products: 10.4 us -> 0.73 us
  local copies, waits for them, and re-layouts: 29.8 us -> 22.5 us
  starting transfers between devices: 50.6 us -> 47.3 us
    ppermute x4 -> x3, waiting for transfers between devices: 16.8 us -> 4.97 us  [the longest x1 4.69 us: local(): lax.ppermute(jnp.where(core == 0, twin_rows[TOK - WIN:], mine[TOK - WIN:]...]
    pallas_call x4 -> x7, Pallas kernels: 43.2 us -> 53.8 us  [the longest x3 40.6 us: attend(): pl.pallas_call(functools.partial(attend_body, count, base, len(skipped)),...]
    all_to_all x1, waiting for transfers between devices: 0.01 us -> 10.6 us  [local(): lax.all_to_all(slices, 'ctx', split_axis=0, concat_axis=0, tiled=True, ax...]
    dot_general x4 -> x2, matrix products: 10.4 us -> 0.73 us  [dot(): return lax.dot_general(a, b, dims, preferred_element_type=jnp.float32)]
    ppermute x1, waiting for transfers between devices: 7.98 us -> 0.01 us  [local(): other_down = lax.ppermute(down, 'ctx', [(i, i ^ 2) for i in range(CTX)])]
    all_to_all x1, waiting for transfers between devices: 7.63 us -> 1.44 us  [local(): lax.all_to_all(gate_part.reshape(EXP, CAP), 'exp', split_axis=0, concat_a...]
    all_to_all x1, waiting for transfers between devices: 4.57 us -> 0.01 us  [local(): lax.all_to_all(keep, 'ctx', split_axis=0, concat_axis=0, tiled=True, axis...]
    ppermute x1, starting transfers between devices: 5.62 us -> 2.01 us  [local(): back = lax.ppermute(sums[:WIN], 'ctx', [(i + 2, i) for i in range(CTX - 2)])]
  transfers between devices with their start and end apart: 24 -> 23, of which waited for: 8 -> 6; matrix products, arithmetic and copies ran while one was open for 26% -> 18% of each run, Pallas kernels for 18% -> 33%
where the time goes in v2:
time: 168 us; the launch traced here: 166 us
  Pallas kernels  59 us (35%)
  starting transfers between devices  47.3 us (28%)
  local copies, waits for them, and re-layouts  22.5 us (13%)
  waiting for transfers between devices  20.2 us (12%)
  other arithmetic  15.3 us (9%)
    pallas_call x3, Pallas kernels, attend(): pl.pallas_call(functools.partial(attend_body, count, base, len(skipped)),...  40.6 us
    all_to_all x1, waiting for transfers between devices, local(): lax.all_to_all(slices, 'ctx', split_axis=0, concat_axis=0, tiled=True, ax...  10.6 us
    pallas_call x2, Pallas kernels, terms(): pl.pallas_call(terms_body, grid_spec=pltpu.PrefetchScalarGridSpec(num_sca...  9.57 us
    all_to_all x1, starting transfers between devices, local(): lax.all_to_all(gate_part.reshape(EXP, CAP), 'exp', split_axis=0, concat_a...  8.81 us
    all_to_all x1, starting transfers between devices, local(): lax.all_to_all(outbound, 'exp', split_axis=0, concat_axis=0, tiled=True)  8.56 us
    unnamed x61, local copies, waits for them, and re-layouts  6.73 us
    all_to_all x1, starting transfers between devices, local(): lax.all_to_all(slices, 'ctx', split_axis=0, concat_axis=0, tiled=True, ax...  4.82 us
    ppermute x1, waiting for transfers between devices, local(): lax.ppermute(jnp.where(core == 0, twin_rows[TOK - WIN:], mine[TOK - WIN:]...  4.69 us
  transfers between devices with their start and end apart: 23, of which 6 were waited for; matrix products, arithmetic and copies ran while one was open for 18% of the time, Pallas kernels for 33%

profile of v2, /device:TPU:2, one launch (start us, length us, event | category | flops | bytes accessed | tf_op | source)
XLA Modules:
  0.0 166.2 jit_solution(8499984972935085818)
XLA Ops:
  1.3 2.2 %shard_map.148.refs_7_.refs_8_.refs_1_.refs_2_ = bf16[1024,512]{1,0:T(8,128)(2,1)} custom-call(bf16[512,512]{1,0:T(8,128)(2,1)} %key_ref.1, bf16[512,512]{1,0:T(8,128)(2,1)} %value_ref.1), custom_call_target="tpu_custom_call" | custom-call | flops 1000000 | bytes 1000000 | tf_op jit(solution)/shard_map/pallas_call | solution.py:78
  3.5 1.5 collective-permute-start.4
  5.8 2.8 %collective-permute-start.6 = (bf16[1024,512]{1,0:T(8,128)(2,1)}, bf16[1024,512]{1,0:T(8,128)(2,1)}, u32[]{:S(2)}, u32[]{:S(2)}) collective-permute-start(bf16[1024,512]{1,0:T(8,128)(2,1)} %shard_map.148.refs_7_.refs_8_.refs_1_.refs_2_), channel_id=1, source_target_pairs={{0,40},{1,41},{2,42},{3,43},{4,44},{5,45},{6,46},{7,47},{8,32},{9,... | collective-permute-start | bytes 3145736 | tf_op jit(solution)/shard_map/ppermute | solution.py:460
  9.3 1.4 slice_reduce_fusion.5
  12.8 1.1 fusion.3.refs_0_
  13.9 8.6 %all-to-all-start = ((bf16[16,248,128]{2,1,0:T(8,128)(2,1)}), bf16[16,248,128]{2,1,0:T(8,128)(2,1)S(1)}, u32[]{:S(2)}, u32[]{:S(2)}) async-start(bf16[16,248,128]{2,1,0:T(8,128)(2,1)} %shard_map.152), calls=%async_computation | async-start | bytes 2031616 | tf_op jit(solution)/shard_map/all_to_all | solution.py:491
  22.4 1.7 %shard_map.146.mine_ref = bf16[128,640]{1,0:T(8,128)(2,1)} custom-call(bf16[128,512]{1,0:T(8,128)(2,1)} %bitcast.82, bf16[64,128]{1,0:T(8,128)(2,1)} %bitcast.83), custom_call_target="tpu_custom_call" | custom-call | flops 1000000 | bytes 1000000 | tf_op jit(solution)/shard_map/pallas_call | solution.py:93
  24.1 1.6 collective-permute-done.twin_ref
  25.7 0.8 slice_select_fusion
  26.5 3.0 %collective-permute-start.1 = (bf16[32,640]{1,0:T(8,128)(2,1)S(1)}, bf16[32,640]{1,0:T(8,128)(2,1)S(1)}, u32[]{:S(2)}, u32[]{:S(2)}) collective-permute-start(bf16[32,640]{1,0:T(8,128)(2,1)S(1)} %slice_select_fusion), channel_id=1, source_target_pairs={{0,32},{16,48},{32,64},{48,80},{64,96},{80,112},{96,128},{112,144}... | collective-permute-start | bytes 122888 | tf_op jit(solution)/shard_map/ppermute | solution.py:454
  30.4 4.7 %collective-permute-done.1.halo_ref = bf16[32,640]{1,0:T(8,128)(2,1)S(1)} collective-permute-done((bf16[32,640]{1,0:T(8,128)(2,1)S(1)}, bf16[32,640]{1,0:T(8,128)(2,1)S(1)}, u32[]{:S(2)}, u32[]{:S(2)}) %collective-permute-start.1) | collective-permute-done | bytes 40992 | tf_op jit(solution)/shard_map/ppermute | solution.py:454
  35.1 0.8 collective-permute-start.7
  35.9 1.9 %shard_map.147 = (bf16[288,512]{1,0:T(8,128)(2,1)}, bf16[288,128]{1,0:T(8,128)(2,1)}, f32[288,128]{1,0:T(8,128)}) custom-call(s32[11]{0:T(128)} %stack.68.where_ref, bf16[128,640]{1,0:T(8,128)(2,1)} %shard_map.146.mine_ref, bf16[128,640]{1,0:T(8,128)(2,1)} %copy-done.8, bf16[32,640]{1,0:T(8,128)(2,1)} %copy-done.11), custom_call_target="tpu_custom_call" | custom-call | flops 1000000 | bytes 1000000 | tf_op jit(solution)/shard_map/pallas_call | solution.py:121
  37.8 3.7 %collective-permute-start.8 = (bf16[1024,512]{1,0:T(8,128)(2,1)}, bf16[1024,512]{1,0:T(8,128)(2,1)S(1)}, u32[]{:S(2)}, u32[]{:S(2)}) collective-permute-start(bf16[1024,512]{1,0:T(8,128)(2,1)} %collective-permute-done.4.refs_8_.refs_9_), channel_id=1, source_target_pairs={{0,40},{1,41},{2,42},{3,43},{4,44},{5,45},{6,46},{7,47},{8,32},{9,... | collective-permute-start | bytes 3145736 | tf_op jit(solution)/shard_map/ppermute | solution.py:500
  41.5 1.5 collective-permute-start.10
  43.5 6.8 %shard_map.149 = (bf16[128,12288]{1,0:T(8,128)(2,1)}, bf16[1,128,768]{2,1,0:T(8,128)(2,1)}, f32[288,512]{1,0:T(8,128)}, f32[288,128]{1,0:T(8,128)}, f32[8,128]{1,0:T(8,128)}) custom-call(s32[11]{0:T(128)} %stack.68.where_ref, bf16[288,512]{1,0:T(8,128)(2,1)} %get-tuple-element.21.refs_0_, bf16[288,128]{1,0:T(8,128)(2,1)} %get-tuple-element.22.refs_1_, ...), custom_call_target="tpu_custom_call" | custom-call | flops 500000000 | bytes 500000 | tf_op jit(solution)/shard_map/pallas_call | solution.py:333
  50.3 14.9 %shard_map.150 = (bf16[128,12288]{1,0:T(8,128)(2,1)}, bf16[3,128,768]{2,1,0:T(8,128)(2,1)}, f32[288,512]{1,0:T(8,128)}, f32[288,128]{1,0:T(8,128)}, f32[8,128]{1,0:T(8,128)}) custom-call(s32[11]{0:T(128)} %stack.68.where_ref, bf16[288,512]{1,0:T(8,128)(2,1)} %get-tuple-element.21.refs_0_, ...), custom_call_target="tpu_custom_call", output_to_operand_aliasing={{0}: (8, {})} | custom-call | flops 15000000512 | bytes 1500000 | tf_op jit(solution)/shard_map/pallas_call | solution.py:333
  65.3 1.0 copy-done.5
  66.3 2.2 %slice.115 = bf16[16,240,128]{2,1,0:T(8,128)(2,1)} slice(bf16[16,248,128]{2,1,0:T(8,128)(2,1)} %shard_map.153), slice={[0:16], [0:240], [0:128]} | slice | bytes 1966080 | tf_op jit(solution)/shard_map/slice | solution.py:506
  68.5 3.2 %reshape.124 = bf16[96,4,2,2,320]{4,3,2,1,0:T(2,128)(2,1)S(1)} reshape(bf16[16,240,128]{2,1,0:T(8,128)(2,1)} %slice.115) | data formatting | bytes 1966080 | tf_op jit(solution)/shard_map/reshape | solution.py:506
  71.7 1.3 copy.37
  73.0 4.8 %all-to-all-start.1 = ((bf16[8,192,320]{2,1,0:T(8,128)(2,1)}), bf16[8,192,320]{2,1,0:T(8,128)(2,1)S(1)}, u32[]{:S(2)}, u32[]{:S(2)}) async-start(bf16[8,192,320]{2,1,0:T(8,128)(2,1)} %bitcast.79), calls=%async_computation.1 | async-start | bytes 2359296 | tf_op jit(solution)/shard_map/all_to_all | solution.py:508
  77.9 1.9 %slice.116.refs_0_ = bf16[512,512]{1,0:T(8,128)(2,1)} slice(bf16[1024,512]{1,0:T(8,128)(2,1)} %collective-permute-done.9.refs_13_.refs_14_), slice={[0:512], [0:512]} | slice | bytes 1048576 | tf_op jit(solution)/shard_map/slice | solution.py:515
  79.7 1.9 %slice.117.refs_0_ = bf16[512,512]{1,0:T(8,128)(2,1)} slice(bf16[1024,512]{1,0:T(8,128)(2,1)} %collective-permute-done.10.refs_9_.refs_10_), slice={[512:1024], [0:512]} | slice | bytes 1048576 | tf_op jit(solution)/shard_map/slice | solution.py:516
  81.6 1.6 collective-permute-done.8.refs_1_.refs_11_.refs_12_
  83.2 10.6 %all-to-all-done.1 = bf16[8,192,320]{2,1,0:T(8,128)(2,1)S(1)} async-done(((bf16[8,192,320]{2,1,0:T(8,128)(2,1)}), bf16[8,192,320]{2,1,0:T(8,128)(2,1)S(1)}, u32[]{:S(2)}, u32[]{:S(2)}) %all-to-all-start.1) | async-done | bytes 983072 | tf_op jit(solution)/shard_map/all_to_all | solution.py:508
  93.8 1.1 copy-done.3
  94.8 4.7 %shard_map.156.refs_0_ = bf16[4,96,1536]{2,1,0:T(8,128)(2,1)} custom-call(s32[11]{0:T(128)} %stack.68.where_ref, bf16[4,2,192,320]{3,2,1,0:T(8,128)(2,1)} %bitcast.73, bf16[320,1536]{1,0:T(8,128)(2,1)} %bitcast.26.own_ref, bf16[320,1536]{1,0:T(8,128)(2,1)} %collective-permute-done.7.refs_2_.other_ref, f32[8,128]{1,0:T(8,128)} %get-tuple-element.28.refs_1_.refs_0_, ...), custom_call_target="tpu_custom_call" | custom-call | flops 100000000 | bytes 100000 | tf_op jit(solution)/shard_map/pallas_call | solution.py:390
  99.6 1.4 collective-permute-start.12
  101.0 1.2 collective-permute-start.13
  102.2 4.8 %shard_map.157 = bf16[4,96,1536]{2,1,0:T(8,128)(2,1)} custom-call(s32[11]{0:T(128)} %stack.68.where_ref, bf16[4,2,192,320]{3,2,1,0:T(8,128)(2,1)} %bitcast.74, bf16[320,1536]{1,0:T(8,128)(2,1)} %bitcast.26.own_ref, bf16[320,1536]{1,0:T(8,128)(2,1)} %collective-permute-done.7.refs_2_.other_ref, bf16[4,96,1536]{2,1,0:T(8,128)(2,1)} %shard_map.156.refs_0_), custom_call_target="tpu_custom_call" | custom-call | flops 100000000 | bytes 100000 | tf_op jit(solution)/shard_map/pallas_call | solution.py:390
  107.0 2.7 %add_convert_fusion.refs_8_ = bf16[4,96,1536]{2,1,0:T(8,128)(2,1)} fusion(bf16[4,96,1536]{2,1,0:T(8,128)(2,1)S(1)} %collective-permute-done.11, bf16[4,96,1536]{2,1,0:T(8,128)(2,1)} %shard_map.157), kind=kLoop, calls=%fused_computation.2 | loop fusion | flops 2359296 | bytes 3538944 | tf_op jit(solution)/shard_map/convert_element_type | solution.py:526
  109.7 4.7 %all-to-all-start.2 = ((bf16[4,96,1536]{2,1,0:T(8,128)(2,1)}), bf16[4,96,1536]{2,1,0:T(8,128)(2,1)S(1)}, u32[]{:S(2)}, u32[]{:S(2)}) async-start(bf16[4,96,1536]{2,1,0:T(8,128)(2,1)} %add_convert_fusion.refs_8_), calls=%async_computation.2 | async-start | bytes 2359296 | tf_op jit(solution)/shard_map/all_to_all | solution.py:527
  114.9 0.8 fusion.30
  116.6 18.9 %shard_map.158 = (bf16[128,12288]{1,0:T(8,128)(2,1)}, bf16[4,128,768]{2,1,0:T(8,128)(2,1)}, f32[288,512]{1,0:T(8,128)}, f32[288,128]{1,0:T(8,128)}, f32[8,128]{1,0:T(8,128)}) custom-call(s32[11]{0:T(128)} %stack.68.where_ref, bf16[288,512]{1,0:T(8,128)(2,1)} %get-tuple-element.21.refs_0_, ...), custom_call_target="tpu_custom_call", output_to_operand_aliasing={{0}: (8, {})} | custom-call | flops 2000000000 | bytes 2000000 | tf_op jit(solution)/shard_map/pallas_call | solution.py:333
  135.6 1.1 slice_add_fusion
  136.7 1.0 copy-done.2
  137.7 1.6 pad_maximum_fusion.1
  139.3 2.0 %collective-permute-start.17 = (f32[32,576]{1,0:T(8,128)}, f32[32,576]{1,0:T(8,128)}, u32[]{:S(2)}, u32[]{:S(2)}) collective-permute-start(f32[32,576]{1,0:T(8,128)} %pad_maximum_fusion.1), channel_id=1, source_target_pairs={{32,0},{48,16},{64,32},{80,48},{96,64},{112,80},{128,96},{144,112}... | collective-permute-start | bytes 221192 | tf_op jit(solution)/shard_map/ppermute | solution.py:549
  141.3 1.5 convert_reduce_fusion
  143.6 8.8 %all-to-all-start.3 = ((f32[16,1,6]{2,1,0:T(1,128)}), f32[16,1,6]{2,1,0:T(1,128)}, u32[]{:S(2)}, u32[]{:S(2)}) async-start(f32[16,1,6]{2,1,0:T(1,128)} %bitcast.37), calls=%async_computation.3 | async-start | bytes 16384 | tf_op jit(solution)/shard_map/all_to_all | solution.py:559
  152.5 0.9 fusion.10
  154.2 1.5 fusion.5
  155.7 0.8 copy-done.6
  156.6 3.0 %shard_map.159 = bf16[128,12288]{1,0:T(8,128)(2,1)} custom-call(s32[11]{0:T(128)} %stack.68.where_ref, bf16[128,12288]{1,0:T(8,128)(2,1)} %get-tuple-element.31.grid_ref, f32[1,96]{1,0:T(1,128)} %bitcast.85, bf16[1,128,768]{2,1,0:T(8,128)(2,1)} %collective-permute-done.14.refs_0_, bf16[3,128,768]{2,1,0:T(8,128)(2,1)} %copy-done.6, ...), custom_call_target="tpu_custom_call", output_to_operand_aliasing={{}: (1, {})} | custom-call | flops 1000000 | bytes 1000000 | tf_op jit(solution)/shard_map/pallas_call | solution.py:163
  159.5 1.4 all-to-all-done.3
  161.5 1.4 reduce.19
  163.8 1.0 add_convert_fusion.1
  (109 shorter events, 11.4 us)
Async XLA Ops:
  0.6 11.3 %copy-start = (bf16[1,128,5120]{2,1,0:T(8,128)(2,1)S(1)}, bf16[1,128,5120]{2,1,0:T(8,128)(2,1)}, u32[]{:S(2)}) copy-start(bf16[1,128,5120]{2,1,0:T(8,128)(2,1)} %param.17) | copy-start | bytes 3932164
  0.6 7.9 %copy-start.14 = (s32[1,128,6]{1,0,2:T(1,128)S(1)}, s32[1,128,6]{1,0,2:T(1,128)}, u32[]{:S(2)}) copy-start(s32[1,128,6]{1,0,2:T(1,128)} %param.18) | copy-start | bytes 9220
  0.7 10.1 %copy-start.13 = (bf16[1,128,6]{1,2,0:T(8,128)(2,1)S(1)}, bf16[1,128,6]{1,2,0:T(8,128)(2,1)}, u32[]{:S(2)}) copy-start(bf16[1,128,6]{1,2,0:T(8,128)(2,1)} %param.19) | copy-start | bytes 4612
  0.7 13.2 %collective-permute-start.2 = (bf16[128,12288]{1,0:T(8,128)(2,1)}, bf16[128,12288]{1,0:T(8,128)(2,1)}, u32[]{:S(2)}, u32[]{:S(2)}) collective-permute-start(bf16[128,12288]{1,0:T(8,128)(2,1)} %bitcast.68), channel_id=1, source_target_pairs={{0,16},{16,0},{32,48},{48,32},{64,80},{80,64},{96,112},{112,96},{1... | collective-permute-start | bytes 9437192 | tf_op jit(solution)/shard_map/ppermute | solution.py:461
  0.8 42.2 %collective-permute-start.3 = (bf16[128,8192]{1,0:T(8,128)(2,1)}, bf16[128,8192]{1,0:T(8,128)(2,1)}, u32[]{:S(2)}, u32[]{:S(2)}) collective-permute-start(bf16[128,8192]{1,0:T(8,128)(2,1)} %bitcast.75), channel_id=1, source_target_pairs={{0,16},{16,0},{32,48},{48,32},{64,80},{80,64},{96,112},{112,96},{1... | collective-permute-start | bytes 6291464 | tf_op jit(solution)/shard_map/ppermute | solution.py:462
  3.5 34.3 %collective-permute-start.4 = (bf16[1024,512]{1,0:T(8,128)(2,1)}, bf16[1024,512]{1,0:T(8,128)(2,1)}, u32[]{:S(2)}, u32[]{:S(2)}) collective-permute-start(bf16[1024,512]{1,0:T(8,128)(2,1)} %shard_map.148.refs_7_.refs_8_.refs_1_.refs_2_), channel_id=1, source_target_pairs={{0,64},{16,80},{32,96},{48,112},{64,128},{80,144},{96,160},{112,17... | collective-permute-start | bytes 3145736 | tf_op jit(solution)/shard_map/ppermute | solution.py:458
  5.0 45.3 %collective-permute-start.5 = (bf16[1024,512]{1,0:T(8,128)(2,1)}, bf16[1024,512]{1,0:T(8,128)(2,1)}, u32[]{:S(2)}, u32[]{:S(2)}) collective-permute-start(bf16[1024,512]{1,0:T(8,128)(2,1)} %shard_map.148.refs_7_.refs_8_.refs_1_.refs_2_), channel_id=1, source_target_pairs={{0,192},{16,208},{32,224},{48,240},{64,0},{80,16},{96,32},{112,48}... | collective-permute-start | bytes 3145736 | tf_op jit(solution)/shard_map/ppermute | solution.py:459
  5.8 35.7 %collective-permute-start.6 = (bf16[1024,512]{1,0:T(8,128)(2,1)}, bf16[1024,512]{1,0:T(8,128)(2,1)}, u32[]{:S(2)}, u32[]{:S(2)}) collective-permute-start(bf16[1024,512]{1,0:T(8,128)(2,1)} %shard_map.148.refs_7_.refs_8_.refs_1_.refs_2_), channel_id=1, source_target_pairs={{0,40},{1,41},{2,42},{3,43},{4,44},{5,45},{6,46},{7,47},{8,32},{9,... | collective-permute-start | bytes 3145736 | tf_op jit(solution)/shard_map/ppermute | solution.py:460
  9.3 1.8 %copy-start.27 = (s32[96]{0:T(128)}, s32[96]{0:T(128)S(1)}, u32[]{:S(2)}) copy-start(s32[96]{0:T(128)S(1)} %get-tuple-element.73) | copy-start | bytes 1156
  10.7 0.6 copy-start.23
  10.7 0.6 copy-start.25
  11.3 0.6 copy-start.9
  13.9 51.4 %all-to-all-start = ((bf16[16,248,128]{2,1,0:T(8,128)(2,1)}), bf16[16,248,128]{2,1,0:T(8,128)(2,1)S(1)}, u32[]{:S(2)}, u32[]{:S(2)}) async-start(bf16[16,248,128]{2,1,0:T(8,128)(2,1)} %shard_map.152), calls=%async_computation | async-start | bytes 2031616 | tf_op jit(solution)/shard_map/all_to_all | solution.py:491
  24.1 1.6 collective-permute-start
  25.7 10.1 %copy-start.8 = (bf16[128,640]{1,0:T(8,128)(2,1)}, bf16[128,640]{1,0:T(8,128)(2,1)S(1)}, u32[]{:S(2)}) copy-start(bf16[128,640]{1,0:T(8,128)(2,1)S(1)} %collective-permute-done.twin_ref) | copy-start | bytes 491524
  26.5 8.5 %collective-permute-start.1 = (bf16[32,640]{1,0:T(8,128)(2,1)S(1)}, bf16[32,640]{1,0:T(8,128)(2,1)S(1)}, u32[]{:S(2)}, u32[]{:S(2)}) collective-permute-start(bf16[32,640]{1,0:T(8,128)(2,1)S(1)} %slice_select_fusion), channel_id=1, source_target_pairs={{0,32},{16,48},{32,64},{48,80},{64,96},{80,112},{96,128},{112,144}... | collective-permute-start | bytes 122888 | tf_op jit(solution)/shard_map/ppermute | solution.py:454
  35.1 0.8 copy-start.11
  35.1 30.2 %collective-permute-start.7 = (bf16[320,1536]{1,0:T(8,128)(2,1)}, bf16[320,1536]{1,0:T(8,128)(2,1)}, u32[]{:S(2)}, u32[]{:S(2)}) collective-permute-start(bf16[320,1536]{1,0:T(8,128)(2,1)} %bitcast.26.own_ref), channel_id=1, source_target_pairs={{0,32},{16,48},{32,0},{48,16},{64,96},{80,112},{96,64},{112,80},{1... | collective-permute-start | bytes 2949128 | tf_op jit(solution)/shard_map/ppermute | solution.py:464
  37.8 45.4 %collective-permute-start.8 = (bf16[1024,512]{1,0:T(8,128)(2,1)}, bf16[1024,512]{1,0:T(8,128)(2,1)S(1)}, u32[]{:S(2)}, u32[]{:S(2)}) collective-permute-start(bf16[1024,512]{1,0:T(8,128)(2,1)} %collective-permute-done.4.refs_8_.refs_9_), channel_id=1, source_target_pairs={{0,40},{1,41},{2,42},{3,43},{4,44},{5,45},{6,46},{7,47},{8,32},{9,... | collective-permute-start | bytes 3145736 | tf_op jit(solution)/shard_map/ppermute | solution.py:500
  41.5 38.3 %collective-permute-start.10 = (bf16[1024,512]{1,0:T(8,128)(2,1)}, bf16[1024,512]{1,0:T(8,128)(2,1)}, u32[]{:S(2)}, u32[]{:S(2)}) collective-permute-start(bf16[1024,512]{1,0:T(8,128)(2,1)} %collective-permute-done.4.refs_8_.refs_9_), channel_id=1, source_target_pairs={{0,64},{16,80},{32,96},{48,112},{64,128},{80,144},{96,160},{112,17... | collective-permute-start | bytes 3145736 | tf_op jit(solution)/shard_map/ppermute | solution.py:498
  43.0 34.9 %collective-permute-start.9 = (bf16[1024,512]{1,0:T(8,128)(2,1)}, bf16[1024,512]{1,0:T(8,128)(2,1)}, u32[]{:S(2)}, u32[]{:S(2)}) collective-permute-start(bf16[1024,512]{1,0:T(8,128)(2,1)} %collective-permute-done.6.refs_12_.refs_13_), channel_id=1, source_target_pairs={{0,192},{16,208},{32,224},{48,240},{64,0},{80,16},{96,32},{112,48}... | collective-permute-start | bytes 3145736 | tf_op jit(solution)/shard_map/ppermute | solution.py:499
  65.3 1.0 copy-start.5
  73.0 20.7 %all-to-all-start.1 = ((bf16[8,192,320]{2,1,0:T(8,128)(2,1)}), bf16[8,192,320]{2,1,0:T(8,128)(2,1)S(1)}, u32[]{:S(2)}, u32[]{:S(2)}) async-start(bf16[8,192,320]{2,1,0:T(8,128)(2,1)} %bitcast.79), calls=%async_computation.1 | async-start | bytes 2359296 | tf_op jit(solution)/shard_map/all_to_all | solution.py:508
  83.2 10.6 %copy-start.4 = (bf16[1024,512]{1,0:T(8,128)(2,1)}, bf16[1024,512]{1,0:T(8,128)(2,1)S(1)}, u32[]{:S(2)}) copy-start(bf16[1024,512]{1,0:T(8,128)(2,1)S(1)} %collective-permute-done.8.refs_1_.refs_11_.refs_12_) | copy-start | bytes 3145732
  93.8 1.1 copy-start.3
  99.6 7.5 %collective-permute-start.11 = (bf16[4,96,1536]{2,1,0:T(8,128)(2,1)}, bf16[4,96,1536]{2,1,0:T(8,128)(2,1)S(1)}, u32[]{:S(2)}, u32[]{:S(2)}) collective-permute-start(bf16[4,96,1536]{2,1,0:T(8,128)(2,1)} %shard_map.156.refs_0_), channel_id=1, source_target_pairs={{0,16},{16,0},{32,48},{48,32},{64,80},{80,64},{96,112},{112,96},{1... | collective-permute-start | bytes 3538952 | tf_op jit(solution)/shard_map/ppermute | solution.py:524
  99.6 16.8 %collective-permute-start.12 = (bf16[512,512]{1,0:T(8,128)(2,1)}, bf16[512,512]{1,0:T(8,128)(2,1)}, u32[]{:S(2)}, u32[]{:S(2)}) collective-permute-start(bf16[512,512]{1,0:T(8,128)(2,1)} %shard_map.154.refs_2_), channel_id=1, source_target_pairs={{0,192},{16,208},{32,224},{48,240},{64,0},{80,16},{96,32},{112,48}... | collective-permute-start | bytes 1572872 | tf_op jit(solution)/shard_map/ppermute | solution.py:517
  101.0 15.6 %collective-permute-start.13 = (bf16[512,512]{1,0:T(8,128)(2,1)}, bf16[512,512]{1,0:T(8,128)(2,1)}, u32[]{:S(2)}, u32[]{:S(2)}) collective-permute-start(bf16[512,512]{1,0:T(8,128)(2,1)} %shard_map.155.refs_3_), channel_id=1, source_target_pairs={{0,40},{1,41},{2,42},{3,43},{4,44},{5,45},{6,46},{7,47},{8,32},{9,... | collective-permute-start | bytes 1572872 | tf_op jit(solution)/shard_map/ppermute | solution.py:518
  109.7 27.0 %all-to-all-start.2 = ((bf16[4,96,1536]{2,1,0:T(8,128)(2,1)}), bf16[4,96,1536]{2,1,0:T(8,128)(2,1)S(1)}, u32[]{:S(2)}, u32[]{:S(2)}) async-start(bf16[4,96,1536]{2,1,0:T(8,128)(2,1)} %add_convert_fusion.refs_8_), calls=%async_computation.2 | async-start | bytes 2359296 | tf_op jit(solution)/shard_map/all_to_all | solution.py:527
  114.4 41.3 %collective-permute-start.14 = (bf16[1,128,768]{2,1,0:T(8,128)(2,1)}, bf16[1,128,768]{2,1,0:T(8,128)(2,1)}, u32[]{:S(2)}, u32[]{:S(2)}) collective-permute-start(bf16[1,128,768]{2,1,0:T(8,128)(2,1)} %get-tuple-element.32), channel_id=1, source_target_pairs={{0,16},{16,0},{32,48},{48,32},{64,80},{80,64},{96,112},{112,96},{1... | collective-permute-start | bytes 589832 | tf_op jit(solution)/shard_map/ppermute | solution.py:512
  114.4 41.3 %collective-permute-start.15 = (bf16[3,128,768]{2,1,0:T(8,128)(2,1)}, bf16[3,128,768]{2,1,0:T(8,128)(2,1)S(1)}, u32[]{:S(2)}, u32[]{:S(2)}) collective-permute-start(bf16[3,128,768]{2,1,0:T(8,128)(2,1)} %get-tuple-element.33), channel_id=1, source_target_pairs={{0,16},{16,0},{32,48},{48,32},{64,80},{80,64},{96,112},{112,96},{1... | collective-permute-start | bytes 1769480 | tf_op jit(solution)/shard_map/ppermute | solution.py:513
  135.5 20.2 %collective-permute-start.16 = (bf16[4,128,768]{2,1,0:T(8,128)(2,1)}, bf16[4,128,768]{2,1,0:T(8,128)(2,1)}, u32[]{:S(2)}, u32[]{:S(2)}) collective-permute-start(bf16[4,128,768]{2,1,0:T(8,128)(2,1)} %get-tuple-element.34), channel_id=1, source_target_pairs={{0,16},{16,0},{32,48},{48,32},{64,80},{80,64},{96,112},{112,96},{1... | collective-permute-start | bytes 2359304 | tf_op jit(solution)/shard_map/ppermute | solution.py:544
  136.7 1.0 copy-start.2
  137.7 5.1 %copy-start.7 = (bf16[1,1,96,1536]{3,2,1,0:T(8,128)(2,1)S(1)}, bf16[1,1,96,1536]{3,2,1,0:T(8,128)(2,1)}, u32[]{:S(2)}) copy-start(bf16[1,1,96,1536]{3,2,1,0:T(8,128)(2,1)} %param.20) | copy-start | bytes 884740
  137.7 14.7 %copy-start.1 = (f32[288,512]{1,0:T(8,128)S(1)}, f32[288,512]{1,0:T(8,128)}, u32[]{:S(2)}) copy-start(f32[288,512]{1,0:T(8,128)} %shard_map.160) | copy-start | bytes 1769476
  139.3 13.2 %collective-permute-start.17 = (f32[32,576]{1,0:T(8,128)}, f32[32,576]{1,0:T(8,128)}, u32[]{:S(2)}, u32[]{:S(2)}) collective-permute-start(f32[32,576]{1,0:T(8,128)} %pad_maximum_fusion.1), channel_id=1, source_target_pairs={{32,0},{48,16},{64,32},{80,48},{96,64},{112,80},{128,96},{144,112}... | collective-permute-start | bytes 221192 | tf_op jit(solution)/shard_map/ppermute | solution.py:549
  143.0 9.5 %copy-start.12 = (f32[96]{0:T(128)}, f32[96]{0:T(128)S(1)}, u32[]{:S(2)}) copy-start(f32[96]{0:T(128)S(1)} %fusion.4) | copy-start | bytes 1156
  143.6 17.3 %all-to-all-start.3 = ((f32[16,1,6]{2,1,0:T(1,128)}), f32[16,1,6]{2,1,0:T(1,128)}, u32[]{:S(2)}, u32[]{:S(2)}) async-start(f32[16,1,6]{2,1,0:T(1,128)} %bitcast.37), calls=%async_computation.3 | async-start | bytes 16384 | tf_op jit(solution)/shard_map/all_to_all | solution.py:559
  154.2 9.6 %collective-permute-start.18 = (f32[128,576]{1,0:T(8,128)}, f32[128,576]{1,0:T(8,128)}, u32[]{:S(2)}, u32[]{:S(2)}) collective-permute-start(f32[128,576]{1,0:T(8,128)} %fusion.7), channel_id=1, source_target_pairs={{0,16},{16,0},{32,48},{48,32},{64,80},{80,64},{96,112},{112,96},{1... | collective-permute-start | bytes 884744 | tf_op jit(solution)/shard_map/ppermute | solution.py:554
  155.7 0.8 copy-start.6
  156.5 6.4 %copy-start.10 = (pred[128,96]{0,1:T(32,128)(4,1)S(1)}, pred[128,96]{0,1:T(32,128)(4,1)}, u32[]{:S(2)}) copy-start(pred[128,96]{0,1:T(32,128)(4,1)} %copy-done.9) | copy-start | bytes 36868
  156.5 6.4 %copy-start.16 = (s32[128]{0:T(128)S(1)}, s32[128]{0:T(128)}, u32[]{:S(2)}) copy-start(s32[128]{0:T(128)} %copy-done.15) | copy-start | bytes 1540
  156.5 6.5 %copy-start.18 = (s32[128]{0:T(128)S(1)}, s32[128]{0:T(128)}, u32[]{:S(2)}) copy-start(s32[128]{0:T(128)} %copy-done.17) | copy-start | bytes 1540
  156.5 6.5 %copy-start.20 = (s32[128]{0:T(128)S(1)}, s32[128]{0:T(128)}, u32[]{:S(2)}) copy-start(s32[128]{0:T(128)} %copy-done.19) | copy-start | bytes 1540
  156.5 6.5 %copy-start.22 = (s32[128]{0:T(128)S(1)}, s32[128]{0:T(128)}, u32[]{:S(2)}) copy-start(s32[128]{0:T(128)} %copy-done.21) | copy-start | bytes 1540
  156.5 6.5 %copy-start.24 = (s32[128]{0:T(128)S(1)}, s32[128]{0:T(128)}, u32[]{:S(2)}) copy-start(s32[128]{0:T(128)} %copy-done.23) | copy-start | bytes 1540
  156.5 6.5 %copy-start.26 = (s32[128]{0:T(128)S(1)}, s32[128]{0:T(128)}, u32[]{:S(2)}) copy-start(s32[128]{0:T(128)} %copy-done.25) | copy-start | bytes 1540
  156.6 6.5 %copy-start.28 = (s32[96]{0:T(128)S(1)}, s32[96]{0:T(128)}, u32[]{:S(2)}) copy-start(s32[96]{0:T(128)} %copy-done.27) | copy-start | bytes 1156
  (4 other events, 2.2 us)

commit v3 on v2

--- a/solution.py
+++ b/solution.py
@@ -499,21 +499,26 @@
     beside_after = lax.ppermute(beside, "ctx", LEFT)
     beside_before = lax.ppermute(before, ("ctx", "exp"), ACROSS)
     *sums, part_b, mark_b = attend(
-        where, 2, *common, [both(before), both(after), both(beside)], sums, heavy=10
+        where, 2, *common, [both(before), both(after)], sums, heavy=10
     )
     routed = tie(routed, mark_b, other_down)
     row_gate = routed[:, CAP * tiles, :CAP].reshape(EXP * CAP, 1)
     slices = routed[:, : CAP * tiles].reshape(EXP * CAP, 4, 2, 2, -1)
     slices = slices.transpose(1, 3, 2, 0, 4).reshape(CHIPS, 2 * EXP * CAP, -1)
+    sent = slices
     slices = lax.all_to_all(
         slices, "ctx", split_axis=0, concat_axis=0, tiled=True, axis_index_groups=RING
     )
 
+    *sums, part_d, mark_d = attend(where, 4, *common, [both(beside)], sums, (sent,))
     part_a = lax.ppermute(part_a, "ctx", TWIN)
+    part_d = lax.ppermute(part_d, "ctx", TWIN)
     part_b = lax.ppermute(part_b, "ctx", TWIN)
 
-    key_half = tie(beside_after[:LATENT], mark_b)
-    value_half = tie(opposite[LATENT:], mark_b)
+    beside_after = tie(beside_after, mark_d)
+    opposite = tie(opposite, mark_d)
+    key_half = beside_after[:LATENT]
+    value_half = opposite[LATENT:]
     last_key = lax.ppermute(key_half, "ctx", LEFT)
     last_value = lax.ppermute(value_half, ("ctx", "exp"), ACROSS)
 
@@ -559,7 +564,7 @@
     returned = lax.all_to_all(
         gate_part.reshape(EXP, CAP), "exp", split_axis=0, concat_axis=0, tiled=True
     )
-    query_grad = place(where, query_grad, (part_a, part_b, part_c), gate_part[None])
+    query_grad = place(where, query_grad, (part_a, part_b, part_d, part_c), gate_part[None])
     found = token_hot.astype(jnp.float32) * returned.reshape(1, -1)
     gate_grad = jnp.stack(
         [jnp.sum(jnp.where(match[k], found, 0.0), axis=1) for k in range(TOPK)], axis=1

time: 168 us -> 168 us (level)
  waiting for transfers between devices: 20.2 us -> 15.8 us
  Pallas kernels: 59 us -> 62.1 us
  starting transfers between devices: 47.3 us -> 49.5 us
  other arithmetic: 15.3 us -> 13.5 us
    all_to_all x1, waiting for transfers between devices: 10.6 us -> 5.32 us  [local(): lax.all_to_all(slices, 'ctx', split_axis=0, concat_axis=0, tiled=True, ax...]
    pallas_call x3 -> x4, Pallas kernels: 40.6 us -> 43.6 us  [attend(): pl.pallas_call(functools.partial(attend_body, count, base, len(skipped)),...]
    reshape x1, local copies, waits for them, and re-layouts: 0.45 us -> 2.34 us  [local(): outbound.reshape(EXP, CAP * tiles, NOPE)]
    reshape x1 -> x2, local copies, waits for them, and re-layouts: 3.18 us -> 4.48 us  [local(): slices = routed[:, :CAP * tiles].reshape(EXP * CAP, 4, 2, 2, -1)]
    unnamed x61 -> x27, local copies, waits for them, and re-layouts: 6.73 us -> 5.69 us
  transfers between devices with their start and end apart: 23 -> 24, of which waited for: 6 -> 5; matrix products, arithmetic and copies ran while one was open for 18% -> 19% of each run, Pallas kernels for 33% -> 34%
where the time goes in v3:
time: 168 us; the launch traced here: 166 us
  Pallas kernels  62.1 us (37%)
  starting transfers between devices  49.5 us (29%)
  local copies, waits for them, and re-layouts  22.7 us (14%)
  waiting for transfers between devices  15.8 us (9%)
  other arithmetic  13.5 us (8%)
    pallas_call x4, Pallas kernels, attend(): pl.pallas_call(functools.partial(attend_body, count, base, len(skipped)),...  43.6 us
    pallas_call x2, Pallas kernels, terms(): pl.pallas_call(terms_body, grid_spec=pltpu.PrefetchScalarGridSpec(num_sca...  9.65 us
    all_to_all x1, starting transfers between devices, local(): lax.all_to_all(outbound, 'exp', split_axis=0, concat_axis=0, tiled=True)  8.62 us
    all_to_all x1, starting transfers between devices, local(): lax.all_to_all(gate_part.reshape(EXP, CAP), 'exp', split_axis=0, concat_a...  8.41 us
    unnamed x27, local copies, waits for them, and re-layouts  5.69 us
    all_to_all x1, waiting for transfers between devices, local(): lax.all_to_all(slices, 'ctx', split_axis=0, concat_axis=0, tiled=True, ax...  5.32 us
    all_to_all x1, starting transfers between devices, local(): lax.all_to_all(slices, 'ctx', split_axis=0, concat_axis=0, tiled=True, ax...  4.83 us
    ppermute x1, waiting for transfers between devices, local(): lax.ppermute(jnp.where(core == 0, twin_rows[TOK - WIN:], mine[TOK - WIN:]...  4.69 us
  transfers between devices with their start and end apart: 24, of which 5 were waited for; matrix products, arithmetic and copies ran while one was open for 19% of the time, Pallas kernels for 34%

profile of v3, /device:TPU:2, one launch (start us, length us, event | category | flops | bytes accessed | tf_op | source)
XLA Modules:
  0.0 166.3 jit_solution(17396424344857131293)
XLA Ops:
  1.3 2.3 %shard_map.148.refs_7_.refs_8_.refs_1_.refs_2_ = bf16[1024,512]{1,0:T(8,128)(2,1)} custom-call(bf16[512,512]{1,0:T(8,128)(2,1)} %key_ref.1, bf16[512,512]{1,0:T(8,128)(2,1)} %value_ref.1), custom_call_target="tpu_custom_call" | custom-call | flops 1000000 | bytes 1000000 | tf_op jit(solution)/shard_map/pallas_call | solution.py:78
  3.5 1.5 collective-permute-start.4
  5.8 2.8 %collective-permute-start.7 = (bf16[1024,512]{1,0:T(8,128)(2,1)}, bf16[1024,512]{1,0:T(8,128)(2,1)}, u32[]{:S(2)}, u32[]{:S(2)}) collective-permute-start(bf16[1024,512]{1,0:T(8,128)(2,1)} %shard_map.148.refs_7_.refs_8_.refs_1_.refs_2_), channel_id=1, source_target_pairs={{0,40},{1,41},{2,42},{3,43},{4,44},{5,45},{6,46},{7,47},{8,32},{9,... | collective-permute-start | bytes 3145736 | tf_op jit(solution)/shard_map/ppermute | solution.py:460
  9.3 1.4 slice_reduce_fusion.5
  11.2 1.4 convolution_convert_fusion
  12.5 2.3 %reshape.123 = bf16[16,240,128]{2,1,0:T(8,128)(2,1)} reshape(bf16[96,5120]{1,0:T(8,128)(2,1)} %convolution_convert_fusion) | data formatting | bytes 1966080 | tf_op jit(solution)/shard_map/reshape | solution.py:485
  14.9 2.2 %fusion.3.refs_0_ = bf16[16,248,128]{2,1,0:T(8,128)(2,1)} fusion(bf16[16,1,6]{2,1,0:T(2,128)(2,1)S(1)} %convert_element_type.102, bf16[16,240,128]{2,1,0:T(8,128)(2,1)} %reshape.123), kind=kLoop, calls=%fused_computation.11 | loop fusion | flops 3047424 | bytes 1999040 | tf_op jit(solution)/shard_map/concatenate | solution.py:483
  17.1 8.6 %all-to-all-start = ((bf16[16,248,128]{2,1,0:T(8,128)(2,1)}), bf16[16,248,128]{2,1,0:T(8,128)(2,1)}, u32[]{:S(2)}, u32[]{:S(2)}) async-start(bf16[16,248,128]{2,1,0:T(8,128)(2,1)} %shard_map.152), calls=%async_computation | async-start | bytes 2031616 | tf_op jit(solution)/shard_map/all_to_all | solution.py:491
  25.7 1.7 %shard_map.146.mine_ref = bf16[128,640]{1,0:T(8,128)(2,1)} custom-call(bf16[128,512]{1,0:T(8,128)(2,1)} %bitcast.86, bf16[64,128]{1,0:T(8,128)(2,1)} %bitcast.87), custom_call_target="tpu_custom_call" | custom-call | flops 1000000 | bytes 1000000 | tf_op jit(solution)/shard_map/pallas_call | solution.py:93
  27.4 1.7 %collective-permute-done.twin_ref = bf16[128,640]{1,0:T(8,128)(2,1)} collective-permute-done((bf16[128,640]{1,0:T(8,128)(2,1)}, bf16[128,640]{1,0:T(8,128)(2,1)}, u32[]{:S(2)}, u32[]{:S(2)}) %collective-permute-start) | collective-permute-done | bytes 163872 | tf_op jit(solution)/shard_map/ppermute | solution.py:453
  29.2 0.8 slice_select_fusion
  30.0 3.0 %collective-permute-start.1 = (bf16[32,640]{1,0:T(8,128)(2,1)S(1)}, bf16[32,640]{1,0:T(8,128)(2,1)S(1)}, u32[]{:S(2)}, u32[]{:S(2)}) collective-permute-start(bf16[32,640]{1,0:T(8,128)(2,1)S(1)} %slice_select_fusion), channel_id=1, source_target_pairs={{0,32},{16,48},{32,64},{48,80},{64,96},{80,112},{96,128},{112,144}... | collective-permute-start | bytes 122888 | tf_op jit(solution)/shard_map/ppermute | solution.py:454
  33.8 4.7 %collective-permute-done.1.halo_ref = bf16[32,640]{1,0:T(8,128)(2,1)S(1)} collective-permute-done((bf16[32,640]{1,0:T(8,128)(2,1)S(1)}, bf16[32,640]{1,0:T(8,128)(2,1)S(1)}, u32[]{:S(2)}, u32[]{:S(2)}) %collective-permute-start.1) | collective-permute-done | bytes 40992 | tf_op jit(solution)/shard_map/ppermute | solution.py:454
  38.5 0.8 collective-permute-start.6
  39.3 1.9 %shard_map.147 = (bf16[288,512]{1,0:T(8,128)(2,1)}, bf16[288,128]{1,0:T(8,128)(2,1)}, f32[288,128]{1,0:T(8,128)}) custom-call(s32[11]{0:T(128)} %stack.68.where_ref, bf16[128,640]{1,0:T(8,128)(2,1)} %shard_map.146.mine_ref, bf16[128,640]{1,0:T(8,128)(2,1)} %collective-permute-done.twin_ref, bf16[32,640]{1,0:T(8,128)(2,1)} %copy-done.8), custom_call_target="tpu_custom_call" | custom-call | flops 1000000 | bytes 1000000 | tf_op jit(solution)/shard_map/pallas_call | solution.py:121
  41.3 3.6 %collective-permute-start.8 = (bf16[1024,512]{1,0:T(8,128)(2,1)}, bf16[1024,512]{1,0:T(8,128)(2,1)}, u32[]{:S(2)}, u32[]{:S(2)}) collective-permute-start(bf16[1024,512]{1,0:T(8,128)(2,1)} %collective-permute-done.4.refs_8_.refs_9_), channel_id=1, source_target_pairs={{0,40},{1,41},{2,42},{3,43},{4,44},{5,45},{6,46},{7,47},{8,32},{9,... | collective-permute-start | bytes 3145736 | tf_op jit(solution)/shard_map/ppermute | solution.py:500
  44.9 1.5 collective-permute-start.10
  46.9 0.8 copy-done.2
  47.7 6.8 %shard_map.149 = (bf16[128,12288]{1,0:T(8,128)(2,1)}, bf16[1,128,768]{2,1,0:T(8,128)(2,1)}, f32[288,512]{1,0:T(8,128)}, f32[288,128]{1,0:T(8,128)}, f32[8,128]{1,0:T(8,128)}) custom-call(s32[11]{0:T(128)} %stack.68.where_ref, bf16[288,512]{1,0:T(8,128)(2,1)} %get-tuple-element.26.refs_0_, bf16[288,128]{1,0:T(8,128)(2,1)} %get-tuple-element.27.refs_1_, ...), custom_call_target="tpu_custom_call" | custom-call | flops 500000000 | bytes 500000 | tf_op jit(solution)/shard_map/pallas_call | solution.py:333
  54.5 11.0 %shard_map.150 = (bf16[128,12288]{1,0:T(8,128)(2,1)}, bf16[2,128,768]{2,1,0:T(8,128)(2,1)}, f32[288,512]{1,0:T(8,128)}, f32[288,128]{1,0:T(8,128)}, f32[8,128]{1,0:T(8,128)}) custom-call(s32[11]{0:T(128)} %stack.68.where_ref, bf16[288,512]{1,0:T(8,128)(2,1)} %get-tuple-element.26.refs_0_, ...), custom_call_target="tpu_custom_call", output_to_operand_aliasing={{0}: (8, {})} | custom-call | flops 10000000000 | bytes 1000000 | tf_op jit(solution)/shard_map/pallas_call | solution.py:333
  65.5 1.1 collective-permute-done.6.refs_2_.other_ref
  66.6 2.2 %slice.115 = bf16[16,240,128]{2,1,0:T(8,128)(2,1)} slice(bf16[16,248,128]{2,1,0:T(8,128)(2,1)} %shard_map.153), slice={[0:16], [0:240], [0:128]} | slice | bytes 1966080 | tf_op jit(solution)/shard_map/slice | solution.py:506
  68.8 3.2 %reshape.124 = bf16[96,4,2,2,320]{4,3,2,1,0:T(2,128)(2,1)S(1)} reshape(bf16[16,240,128]{2,1,0:T(8,128)(2,1)} %slice.115) | data formatting | bytes 1966080 | tf_op jit(solution)/shard_map/reshape | solution.py:506
  72.0 1.3 copy.38
  73.3 4.8 %all-to-all-start.1 = ((bf16[8,192,320]{2,1,0:T(8,128)(2,1)}), bf16[8,192,320]{2,1,0:T(8,128)(2,1)S(1)}, u32[]{:S(2)}, u32[]{:S(2)}) async-start(bf16[8,192,320]{2,1,0:T(8,128)(2,1)} %bitcast.28.refs_8_), calls=%async_computation.1 | async-start | bytes 2359296 | tf_op jit(solution)/shard_map/all_to_all | solution.py:509
  78.1 6.8 %shard_map.154 = (bf16[128,12288]{1,0:T(8,128)(2,1)}, bf16[1,128,768]{2,1,0:T(8,128)(2,1)}, f32[288,512]{1,0:T(8,128)}, f32[288,128]{1,0:T(8,128)}, f32[8,128]{1,0:T(8,128)}) custom-call(s32[11]{0:T(128)} %stack.68.where_ref, bf16[288,512]{1,0:T(8,128)(2,1)} %get-tuple-element.26.refs_0_, ...), custom_call_target="tpu_custom_call", output_to_operand_aliasing={{0}: (8, {})} | custom-call | flops 500000000 | bytes 500000 | tf_op jit(solution)/shard_map/pallas_call | solution.py:333
  85.0 1.9 %slice.116.refs_2_ = bf16[512,512]{1,0:T(8,128)(2,1)} slice(bf16[1024,512]{1,0:T(8,128)(2,1)} %shard_map.155.refs_13_.refs_14_), slice={[0:512], [0:512]} | slice | bytes 1048576 | tf_op jit(solution)/shard_map/slice | solution.py:520
  86.9 1.9 %slice.117.refs_3_ = bf16[512,512]{1,0:T(8,128)(2,1)} slice(bf16[1024,512]{1,0:T(8,128)(2,1)} %shard_map.156.refs_9_.refs_10_), slice={[512:1024], [0:512]} | slice | bytes 1048576 | tf_op jit(solution)/shard_map/slice | solution.py:521
  88.7 5.3 %all-to-all-done.1 = bf16[8,192,320]{2,1,0:T(8,128)(2,1)S(1)} async-done(((bf16[8,192,320]{2,1,0:T(8,128)(2,1)}), bf16[8,192,320]{2,1,0:T(8,128)(2,1)S(1)}, u32[]{:S(2)}, u32[]{:S(2)}) %all-to-all-start.1) | async-done | bytes 983072 | tf_op jit(solution)/shard_map/all_to_all | solution.py:509
  94.1 1.0 copy-done.4
  95.1 4.9 %shard_map.157.refs_0_ = bf16[4,96,1536]{2,1,0:T(8,128)(2,1)} custom-call(s32[11]{0:T(128)} %stack.68.where_ref, bf16[4,2,192,320]{3,2,1,0:T(8,128)(2,1)} %bitcast.80, bf16[320,1536]{1,0:T(8,128)(2,1)} %bitcast.84, bf16[320,1536]{1,0:T(8,128)(2,1)} %collective-permute-done.6.refs_2_.other_ref, f32[8,128]{1,0:T(8,128)} %get-tuple-element.33.refs_1_.refs_0_, ...), custom_call_target="tpu_custom_call" | custom-call | flops 100000000 | bytes 100000 | tf_op jit(solution)/shard_map/pallas_call | solution.py:390
  100.0 1.5 collective-permute-start.12
  101.5 2.3 %collective-permute-start.13 = (bf16[512,512]{1,0:T(8,128)(2,1)}, bf16[512,512]{1,0:T(8,128)(2,1)}, u32[]{:S(2)}, u32[]{:S(2)}) collective-permute-start(bf16[512,512]{1,0:T(8,128)(2,1)} %slice.117.refs_3_), channel_id=1, source_target_pairs={{0,40},{1,41},{2,42},{3,43},{4,44},{5,45},{6,46},{7,47},{8,32},{9,... | collective-permute-start | bytes 1572872 | tf_op jit(solution)/shard_map/ppermute | solution.py:523
  103.7 4.8 %shard_map.158 = bf16[4,96,1536]{2,1,0:T(8,128)(2,1)} custom-call(s32[11]{0:T(128)} %stack.68.where_ref, bf16[4,2,192,320]{3,2,1,0:T(8,128)(2,1)} %bitcast.81, bf16[320,1536]{1,0:T(8,128)(2,1)} %bitcast.85, bf16[320,1536]{1,0:T(8,128)(2,1)} %collective-permute-done.6.refs_2_.other_ref, bf16[4,96,1536]{2,1,0:T(8,128)(2,1)} %shard_map.157.refs_0_), custom_call_target="tpu_custom_call" | custom-call | flops 100000000 | bytes 100000 | tf_op jit(solution)/shard_map/pallas_call | solution.py:390
  108.5 2.6 %add_convert_fusion.refs_8_ = bf16[4,96,1536]{2,1,0:T(8,128)(2,1)} fusion(bf16[4,96,1536]{2,1,0:T(8,128)(2,1)S(1)} %collective-permute-done.11, bf16[4,96,1536]{2,1,0:T(8,128)(2,1)} %shard_map.158), kind=kLoop, calls=%fused_computation.2 | loop fusion | flops 2359296 | bytes 3538944 | tf_op jit(solution)/shard_map/convert_element_type | solution.py:531
  111.1 4.7 %all-to-all-start.2 = ((bf16[4,96,1536]{2,1,0:T(8,128)(2,1)}), bf16[4,96,1536]{2,1,0:T(8,128)(2,1)S(1)}, u32[]{:S(2)}, u32[]{:S(2)}) async-start(bf16[4,96,1536]{2,1,0:T(8,128)(2,1)} %add_convert_fusion.refs_8_), calls=%async_computation.2 | async-start | bytes 2359296 | tf_op jit(solution)/shard_map/all_to_all | solution.py:532
  116.2 0.8 fusion.30
  117.1 18.9 %shard_map.159 = (bf16[128,12288]{1,0:T(8,128)(2,1)}, bf16[4,128,768]{2,1,0:T(8,128)(2,1)}, f32[288,512]{1,0:T(8,128)}, f32[288,128]{1,0:T(8,128)}, f32[8,128]{1,0:T(8,128)}) custom-call(s32[11]{0:T(128)} %stack.68.where_ref, bf16[288,512]{1,0:T(8,128)(2,1)} %get-tuple-element.26.refs_0_, ...), custom_call_target="tpu_custom_call", output_to_operand_aliasing={{0}: (8, {})} | custom-call | flops 2000000000 | bytes 2000000 | tf_op jit(solution)/shard_map/pallas_call | solution.py:333
  136.7 1.1 slice_add_fusion
  137.8 1.0 copy-done.3
  138.8 0.9 pad_maximum_fusion.1
  139.8 3.0 %collective-permute-start.18 = (f32[32,576]{1,0:T(8,128)S(1)}, f32[32,576]{1,0:T(8,128)S(1)}, u32[]{:S(2)}, u32[]{:S(2)}) collective-permute-start(f32[32,576]{1,0:T(8,128)S(1)} %pad_maximum_fusion.1), channel_id=1, source_target_pairs={{32,0},{48,16},{64,32},{80,48},{96,64},{112,80},{128,96},{144,112}... | collective-permute-start | bytes 221192 | tf_op jit(solution)/shard_map/ppermute | solution.py:554
  142.8 1.5 convert_reduce_fusion
  145.1 8.4 %all-to-all-start.3 = ((f32[16,1,6]{2,1,0:T(1,128)}), f32[16,1,6]{2,1,0:T(1,128)S(1)}, u32[]{:S(2)}, u32[]{:S(2)}) async-start(f32[16,1,6]{2,1,0:T(1,128)} %bitcast.38), calls=%async_computation.3 | async-start | bytes 16384 | tf_op jit(solution)/shard_map/all_to_all | solution.py:564
  154.4 0.8 fusion.5
  156.0 3.0 %shard_map.160 = bf16[128,12288]{1,0:T(8,128)(2,1)} custom-call(s32[11]{0:T(128)} %stack.68.where_ref, bf16[128,12288]{1,0:T(8,128)(2,1)} %get-tuple-element.40.grid_ref, f32[1,96]{1,0:T(1,128)} %bitcast.89, bf16[1,128,768]{2,1,0:T(8,128)(2,1)} %collective-permute-done.14.refs_0_, bf16[2,128,768]{2,1,0:T(8,128)(2,1)} %copy-done.6, ...), custom_call_target="tpu_custom_call", output_to_operand_aliasing={{}: (1, {})} | custom-call | flops 1000000 | bytes 1000000 | tf_op jit(solution)/shard_map/pallas_call | solution.py:163
  158.9 3.0 %all-to-all-done.3 = f32[16,1,6]{2,1,0:T(1,128)S(1)} async-done(((f32[16,1,6]{2,1,0:T(1,128)}), f32[16,1,6]{2,1,0:T(1,128)S(1)}, u32[]{:S(2)}, u32[]{:S(2)}) %all-to-all-start.3) | async-done | bytes 416 | tf_op jit(solution)/shard_map/all_to_all | solution.py:564
  163.9 1.0 add_convert_fusion.1
  (78 shorter events, 10.8 us)
Async XLA Ops:
  0.6 10.5 %copy-start = (bf16[1,128,5120]{2,1,0:T(8,128)(2,1)S(1)}, bf16[1,128,5120]{2,1,0:T(8,128)(2,1)}, u32[]{:S(2)}) copy-start(bf16[1,128,5120]{2,1,0:T(8,128)(2,1)} %param.17) | copy-start | bytes 3932164
  0.6 7.9 %copy-start.11 = (s32[1,128,6]{1,0,2:T(1,128)S(1)}, s32[1,128,6]{1,0,2:T(1,128)}, u32[]{:S(2)}) copy-start(s32[1,128,6]{1,0,2:T(1,128)} %param.18) | copy-start | bytes 9220
  0.7 10.1 %copy-start.10 = (bf16[1,128,6]{1,2,0:T(8,128)(2,1)S(1)}, bf16[1,128,6]{1,2,0:T(8,128)(2,1)}, u32[]{:S(2)}) copy-start(bf16[1,128,6]{1,2,0:T(8,128)(2,1)} %param.19) | copy-start | bytes 4612
  0.7 16.4 %collective-permute-start.2 = (bf16[128,12288]{1,0:T(8,128)(2,1)}, bf16[128,12288]{1,0:T(8,128)(2,1)}, u32[]{:S(2)}, u32[]{:S(2)}) collective-permute-start(bf16[128,12288]{1,0:T(8,128)(2,1)} %bitcast.69), channel_id=1, source_target_pairs={{0,16},{16,0},{32,48},{48,32},{64,80},{80,64},{96,112},{112,96},{1... | collective-permute-start | bytes 9437192 | tf_op jit(solution)/shard_map/ppermute | solution.py:461
  0.8 45.6 %collective-permute-start.3 = (bf16[128,8192]{1,0:T(8,128)(2,1)}, bf16[128,8192]{1,0:T(8,128)(2,1)S(1)}, u32[]{:S(2)}, u32[]{:S(2)}) collective-permute-start(bf16[128,8192]{1,0:T(8,128)(2,1)} %bitcast.75), channel_id=1, source_target_pairs={{0,16},{16,0},{32,48},{48,32},{64,80},{80,64},{96,112},{112,96},{1... | collective-permute-start | bytes 6291464 | tf_op jit(solution)/shard_map/ppermute | solution.py:462
  3.5 37.7 %collective-permute-start.4 = (bf16[1024,512]{1,0:T(8,128)(2,1)}, bf16[1024,512]{1,0:T(8,128)(2,1)}, u32[]{:S(2)}, u32[]{:S(2)}) collective-permute-start(bf16[1024,512]{1,0:T(8,128)(2,1)} %shard_map.148.refs_7_.refs_8_.refs_1_.refs_2_), channel_id=1, source_target_pairs={{0,64},{16,80},{32,96},{48,112},{64,128},{80,144},{96,160},{112,17... | collective-permute-start | bytes 3145736 | tf_op jit(solution)/shard_map/ppermute | solution.py:458
  5.0 49.5 %collective-permute-start.5 = (bf16[1024,512]{1,0:T(8,128)(2,1)}, bf16[1024,512]{1,0:T(8,128)(2,1)}, u32[]{:S(2)}, u32[]{:S(2)}) collective-permute-start(bf16[1024,512]{1,0:T(8,128)(2,1)} %shard_map.148.refs_7_.refs_8_.refs_1_.refs_2_), channel_id=1, source_target_pairs={{0,192},{16,208},{32,224},{48,240},{64,0},{80,16},{96,32},{112,48}... | collective-permute-start | bytes 3145736 | tf_op jit(solution)/shard_map/ppermute | solution.py:459
  5.8 39.0 %collective-permute-start.7 = (bf16[1024,512]{1,0:T(8,128)(2,1)}, bf16[1024,512]{1,0:T(8,128)(2,1)}, u32[]{:S(2)}, u32[]{:S(2)}) collective-permute-start(bf16[1024,512]{1,0:T(8,128)(2,1)} %shard_map.148.refs_7_.refs_8_.refs_1_.refs_2_), channel_id=1, source_target_pairs={{0,40},{1,41},{2,42},{3,43},{4,44},{5,45},{6,46},{7,47},{8,32},{9,... | collective-permute-start | bytes 3145736 | tf_op jit(solution)/shard_map/ppermute | solution.py:460
  17.1 49.5 %all-to-all-start = ((bf16[16,248,128]{2,1,0:T(8,128)(2,1)}), bf16[16,248,128]{2,1,0:T(8,128)(2,1)}, u32[]{:S(2)}, u32[]{:S(2)}) async-start(bf16[16,248,128]{2,1,0:T(8,128)(2,1)} %shard_map.152), calls=%async_computation | async-start | bytes 2031616 | tf_op jit(solution)/shard_map/all_to_all | solution.py:491
  27.4 1.7 %collective-permute-start = (bf16[128,640]{1,0:T(8,128)(2,1)}, bf16[128,640]{1,0:T(8,128)(2,1)}, u32[]{:S(2)}, u32[]{:S(2)}) collective-permute-start(bf16[128,640]{1,0:T(8,128)(2,1)} %shard_map.146.mine_ref), channel_id=1, source_target_pairs={{0,16},{16,0},{32,48},{48,32},{64,80},{80,64},{96,112},{112,96},{1... | collective-permute-start | bytes 491528 | tf_op jit(solution)/shard_map/ppermute | solution.py:453
  30.0 8.5 %collective-permute-start.1 = (bf16[32,640]{1,0:T(8,128)(2,1)S(1)}, bf16[32,640]{1,0:T(8,128)(2,1)S(1)}, u32[]{:S(2)}, u32[]{:S(2)}) collective-permute-start(bf16[32,640]{1,0:T(8,128)(2,1)S(1)} %slice_select_fusion), channel_id=1, source_target_pairs={{0,32},{16,48},{32,64},{48,80},{64,96},{80,112},{96,128},{112,144}... | collective-permute-start | bytes 122888 | tf_op jit(solution)/shard_map/ppermute | solution.py:454
  38.5 0.8 copy-start.8
  38.5 28.1 %collective-permute-start.6 = (bf16[320,1536]{1,0:T(8,128)(2,1)}, bf16[320,1536]{1,0:T(8,128)(2,1)}, u32[]{:S(2)}, u32[]{:S(2)}) collective-permute-start(bf16[320,1536]{1,0:T(8,128)(2,1)} %bitcast.83), channel_id=1, source_target_pairs={{0,32},{16,48},{32,0},{48,16},{64,96},{80,112},{96,64},{112,80},{1... | collective-permute-start | bytes 2949128 | tf_op jit(solution)/shard_map/ppermute | solution.py:464
  41.3 47.5 %collective-permute-start.8 = (bf16[1024,512]{1,0:T(8,128)(2,1)}, bf16[1024,512]{1,0:T(8,128)(2,1)}, u32[]{:S(2)}, u32[]{:S(2)}) collective-permute-start(bf16[1024,512]{1,0:T(8,128)(2,1)} %collective-permute-done.4.refs_8_.refs_9_), channel_id=1, source_target_pairs={{0,40},{1,41},{2,42},{3,43},{4,44},{5,45},{6,46},{7,47},{8,32},{9,... | collective-permute-start | bytes 3145736 | tf_op jit(solution)/shard_map/ppermute | solution.py:500
  44.9 42.0 %collective-permute-start.10 = (bf16[1024,512]{1,0:T(8,128)(2,1)}, bf16[1024,512]{1,0:T(8,128)(2,1)}, u32[]{:S(2)}, u32[]{:S(2)}) collective-permute-start(bf16[1024,512]{1,0:T(8,128)(2,1)} %collective-permute-done.4.refs_8_.refs_9_), channel_id=1, source_target_pairs={{0,64},{16,80},{32,96},{48,112},{64,128},{80,144},{96,160},{112,17... | collective-permute-start | bytes 3145736 | tf_op jit(solution)/shard_map/ppermute | solution.py:498
  46.4 1.4 copy-start.2
  46.4 38.6 %collective-permute-start.9 = (bf16[1024,512]{1,0:T(8,128)(2,1)}, bf16[1024,512]{1,0:T(8,128)(2,1)}, u32[]{:S(2)}, u32[]{:S(2)}) collective-permute-start(bf16[1024,512]{1,0:T(8,128)(2,1)} %collective-permute-done.7.refs_9_.refs_10_), channel_id=1, source_target_pairs={{0,192},{16,208},{32,224},{48,240},{64,0},{80,16},{96,32},{112,48}... | collective-permute-start | bytes 3145736 | tf_op jit(solution)/shard_map/ppermute | solution.py:499
  73.3 20.7 %all-to-all-start.1 = ((bf16[8,192,320]{2,1,0:T(8,128)(2,1)}), bf16[8,192,320]{2,1,0:T(8,128)(2,1)S(1)}, u32[]{:S(2)}, u32[]{:S(2)}) async-start(bf16[8,192,320]{2,1,0:T(8,128)(2,1)} %bitcast.28.refs_8_), calls=%async_computation.1 | async-start | bytes 2359296 | tf_op jit(solution)/shard_map/all_to_all | solution.py:509
  94.1 1.0 copy-start.4
  95.1 4.9 %copy-start.5 = (bf16[512,512]{1,0:T(8,128)(2,1)S(1)}, bf16[512,512]{1,0:T(8,128)(2,1)}, u32[]{:S(2)}) copy-start(bf16[512,512]{1,0:T(8,128)(2,1)} %slice.116.refs_2_) | copy-start | bytes 1572868
  100.0 8.5 %collective-permute-start.11 = (bf16[4,96,1536]{2,1,0:T(8,128)(2,1)}, bf16[4,96,1536]{2,1,0:T(8,128)(2,1)S(1)}, u32[]{:S(2)}, u32[]{:S(2)}) collective-permute-start(bf16[4,96,1536]{2,1,0:T(8,128)(2,1)} %shard_map.157.refs_0_), channel_id=1, source_target_pairs={{0,16},{16,0},{32,48},{48,32},{64,80},{80,64},{96,112},{112,96},{1... | collective-permute-start | bytes 3538952 | tf_op jit(solution)/shard_map/ppermute | solution.py:529
  100.0 17.1 %collective-permute-start.12 = (bf16[512,512]{1,0:T(8,128)(2,1)S(1)}, bf16[512,512]{1,0:T(8,128)(2,1)}, u32[]{:S(2)}, u32[]{:S(2)}) collective-permute-start(bf16[512,512]{1,0:T(8,128)(2,1)S(1)} %copy-done.5), channel_id=1, source_target_pairs={{0,192},{16,208},{32,224},{48,240},{64,0},{80,16},{96,32},{112,48}... | collective-permute-start | bytes 1572872 | tf_op jit(solution)/shard_map/ppermute | solution.py:522
  101.5 15.7 %collective-permute-start.13 = (bf16[512,512]{1,0:T(8,128)(2,1)}, bf16[512,512]{1,0:T(8,128)(2,1)}, u32[]{:S(2)}, u32[]{:S(2)}) collective-permute-start(bf16[512,512]{1,0:T(8,128)(2,1)} %slice.117.refs_3_), channel_id=1, source_target_pairs={{0,40},{1,41},{2,42},{3,43},{4,44},{5,45},{6,46},{7,47},{8,32},{9,... | collective-permute-start | bytes 1572872 | tf_op jit(solution)/shard_map/ppermute | solution.py:523
  111.1 26.7 %all-to-all-start.2 = ((bf16[4,96,1536]{2,1,0:T(8,128)(2,1)}), bf16[4,96,1536]{2,1,0:T(8,128)(2,1)S(1)}, u32[]{:S(2)}, u32[]{:S(2)}) async-start(bf16[4,96,1536]{2,1,0:T(8,128)(2,1)} %add_convert_fusion.refs_8_), calls=%async_computation.2 | async-start | bytes 2359296 | tf_op jit(solution)/shard_map/all_to_all | solution.py:532
  115.7 39.5 %collective-permute-start.14 = (bf16[1,128,768]{2,1,0:T(8,128)(2,1)}, bf16[1,128,768]{2,1,0:T(8,128)(2,1)}, u32[]{:S(2)}, u32[]{:S(2)}) collective-permute-start(bf16[1,128,768]{2,1,0:T(8,128)(2,1)} %get-tuple-element.41), channel_id=1, source_target_pairs={{0,16},{16,0},{32,48},{48,32},{64,80},{80,64},{96,112},{112,96},{1... | collective-permute-start | bytes 589832 | tf_op jit(solution)/shard_map/ppermute | solution.py:514
  115.7 39.5 %collective-permute-start.15 = (bf16[2,128,768]{2,1,0:T(8,128)(2,1)}, bf16[2,128,768]{2,1,0:T(8,128)(2,1)S(1)}, u32[]{:S(2)}, u32[]{:S(2)}) collective-permute-start(bf16[2,128,768]{2,1,0:T(8,128)(2,1)} %get-tuple-element.42), channel_id=1, source_target_pairs={{0,16},{16,0},{32,48},{48,32},{64,80},{80,64},{96,112},{112,96},{1... | collective-permute-start | bytes 1179656 | tf_op jit(solution)/shard_map/ppermute | solution.py:516
  116.2 39.0 %collective-permute-start.16 = (bf16[1,128,768]{2,1,0:T(8,128)(2,1)}, bf16[1,128,768]{2,1,0:T(8,128)(2,1)}, u32[]{:S(2)}, u32[]{:S(2)}) collective-permute-start(bf16[1,128,768]{2,1,0:T(8,128)(2,1)} %get-tuple-element.43), channel_id=1, source_target_pairs={{0,16},{16,0},{32,48},{48,32},{64,80},{80,64},{96,112},{112,96},{1... | collective-permute-start | bytes 589832 | tf_op jit(solution)/shard_map/ppermute | solution.py:515
  136.1 19.1 %collective-permute-start.17 = (bf16[4,128,768]{2,1,0:T(8,128)(2,1)}, bf16[4,128,768]{2,1,0:T(8,128)(2,1)}, u32[]{:S(2)}, u32[]{:S(2)}) collective-permute-start(bf16[4,128,768]{2,1,0:T(8,128)(2,1)} %get-tuple-element.44), channel_id=1, source_target_pairs={{0,16},{16,0},{32,48},{48,32},{64,80},{80,64},{96,112},{112,96},{1... | collective-permute-start | bytes 2359304 | tf_op jit(solution)/shard_map/ppermute | solution.py:549
  137.8 1.0 copy-start.3
  138.8 5.4 %copy-start.7 = (bf16[1,1,96,1536]{3,2,1,0:T(8,128)(2,1)S(1)}, bf16[1,1,96,1536]{3,2,1,0:T(8,128)(2,1)}, u32[]{:S(2)}) copy-start(bf16[1,1,96,1536]{3,2,1,0:T(8,128)(2,1)} %param.20) | copy-start | bytes 884740
  138.8 14.7 %copy-start.1 = (f32[288,512]{1,0:T(8,128)S(1)}, f32[288,512]{1,0:T(8,128)}, u32[]{:S(2)}) copy-start(f32[288,512]{1,0:T(8,128)} %shard_map.161) | copy-start | bytes 1769476
  139.8 13.8 %collective-permute-start.18 = (f32[32,576]{1,0:T(8,128)S(1)}, f32[32,576]{1,0:T(8,128)S(1)}, u32[]{:S(2)}, u32[]{:S(2)}) collective-permute-start(f32[32,576]{1,0:T(8,128)S(1)} %pad_maximum_fusion.1), channel_id=1, source_target_pairs={{32,0},{48,16},{64,32},{80,48},{96,64},{112,80},{128,96},{144,112}... | collective-permute-start | bytes 221192 | tf_op jit(solution)/shard_map/ppermute | solution.py:554
  144.4 10.8 %copy-start.9 = (f32[96]{0:T(128)}, f32[96]{0:T(128)S(1)}, u32[]{:S(2)}) copy-start(f32[96]{0:T(128)S(1)} %fusion.4) | copy-start | bytes 1156
  145.1 16.8 %all-to-all-start.3 = ((f32[16,1,6]{2,1,0:T(1,128)}), f32[16,1,6]{2,1,0:T(1,128)S(1)}, u32[]{:S(2)}, u32[]{:S(2)}) async-start(f32[16,1,6]{2,1,0:T(1,128)} %bitcast.38), calls=%async_computation.3 | async-start | bytes 16384 | tf_op jit(solution)/shard_map/all_to_all | solution.py:564
  154.4 9.6 %collective-permute-start.19 = (f32[128,576]{1,0:T(8,128)}, f32[128,576]{1,0:T(8,128)}, u32[]{:S(2)}, u32[]{:S(2)}) collective-permute-start(f32[128,576]{1,0:T(8,128)} %fusion.7), channel_id=1, source_target_pairs={{0,16},{16,0},{32,48},{48,32},{64,80},{80,64},{96,112},{112,96},{1... | collective-permute-start | bytes 884744 | tf_op jit(solution)/shard_map/ppermute | solution.py:559
  155.2 0.8 copy-start.6

commit v4 on v3

--- a/solution.py
+++ b/solution.py
@@ -510,15 +510,16 @@
         slices, "ctx", split_axis=0, concat_axis=0, tiled=True, axis_index_groups=RING
     )
 
-    *sums, part_d, mark_d = attend(where, 4, *common, [both(beside)], sums, (sent,))
+    *sums, part_d, mark_d = attend(
+        where, 4, *common, [both(beside), both(opposite)], sums, (sent,)
+    )
     part_a = lax.ppermute(part_a, "ctx", TWIN)
     part_d = lax.ppermute(part_d, "ctx", TWIN)
     part_b = lax.ppermute(part_b, "ctx", TWIN)
 
     beside_after = tie(beside_after, mark_d)
-    opposite = tie(opposite, mark_d)
     key_half = beside_after[:LATENT]
-    value_half = opposite[LATENT:]
+    value_half = tie(opposite[LATENT:], mark_d)
     last_key = lax.ppermute(key_half, "ctx", LEFT)
     last_value = lax.ppermute(value_half, ("ctx", "exp"), ACROSS)
 
@@ -535,10 +536,9 @@
 
     *sums, part_c, mark_c = attend(
         where,
-        5,
+        6,
         *common,
         [
-            both(opposite),
             both(beside_before),
             both(beside_after),
             ((last_key, 0), (last_value, 0)),

time: 168 us -> 163 us (0.970)
  waiting for transfers between devices: 15.8 us -> 11.7 us
    all_to_all x1, waiting for transfers between devices: 5.32 us -> 1.14 us  [local(): lax.all_to_all(slices, 'ctx', split_axis=0, concat_axis=0, tiled=True, ax...]
  transfers between devices with their start and end apart: 24 -> 24, of which waited for: 5 -> 5; matrix products, arithmetic and copies ran while one was open for 19% -> 19% of each run, Pallas kernels for 34% -> 35%
where the time goes in v4:
time: 163 us; the launch traced here: 162 us
  Pallas kernels  62.3 us (38%)
  starting transfers between devices  49.1 us (30%)
  local copies, waits for them, and re-layouts  22.6 us (14%)
  other arithmetic  13.6 us (8%)
  waiting for transfers between devices  11.7 us (7%)
  matrix products  1.67 us (1%)
    pallas_call x4, Pallas kernels, attend(): pl.pallas_call(functools.partial(attend_body, count, base, len(skipped)),...  43.7 us
    pallas_call x2, Pallas kernels, terms(): pl.pallas_call(terms_body, grid_spec=pltpu.PrefetchScalarGridSpec(num_sca...  9.74 us
    all_to_all x1, starting transfers between devices, local(): lax.all_to_all(outbound, 'exp', split_axis=0, concat_axis=0, tiled=True)  8.62 us
    all_to_all x1, starting transfers between devices, local(): lax.all_to_all(gate_part.reshape(EXP, CAP), 'exp', split_axis=0, concat_a...  8.09 us
    unnamed x27, local copies, waits for them, and re-layouts  5.68 us
    all_to_all x1, starting transfers between devices, local(): lax.all_to_all(slices, 'ctx', split_axis=0, concat_axis=0, tiled=True, ax...  4.84 us
    ppermute x1, waiting for transfers between devices, local(): lax.ppermute(jnp.where(core == 0, twin_rows[TOK - WIN:], mine[TOK - WIN:]...  4.79 us
    all_to_all x1, starting transfers between devices, local(): lax.all_to_all(keep, 'ctx', split_axis=0, concat_axis=0, tiled=True, axis...  4.65 us
  transfers between devices with their start and end apart: 24, of which 5 were waited for; matrix products, arithmetic and copies ran while one was open for 19% of the time, Pallas kernels for 35%

profile of v4, /device:TPU:2, one launch (start us, length us, event | category | flops | bytes accessed | tf_op | source)
XLA Modules:
  0.0 162.1 jit_solution(12519315380757195710)
XLA Ops:
  1.3 2.3 %shard_map.148.refs_7_.refs_8_.refs_1_.refs_2_ = bf16[1024,512]{1,0:T(8,128)(2,1)} custom-call(bf16[512,512]{1,0:T(8,128)(2,1)} %key_ref.1, bf16[512,512]{1,0:T(8,128)(2,1)} %value_ref.1), custom_call_target="tpu_custom_call" | custom-call | flops 1000000 | bytes 1000000 | tf_op jit(solution)/shard_map/pallas_call | solution.py:78
  3.5 1.5 collective-permute-start.4
  5.8 2.8 %collective-permute-start.7 = (bf16[1024,512]{1,0:T(8,128)(2,1)}, bf16[1024,512]{1,0:T(8,128)(2,1)}, u32[]{:S(2)}, u32[]{:S(2)}) collective-permute-start(bf16[1024,512]{1,0:T(8,128)(2,1)} %shard_map.148.refs_7_.refs_8_.refs_1_.refs_2_), channel_id=1, source_target_pairs={{0,40},{1,41},{2,42},{3,43},{4,44},{5,45},{6,46},{7,47},{8,32},{9,... | collective-permute-start | bytes 3145736 | tf_op jit(solution)/shard_map/ppermute | solution.py:460
  9.3 1.4 slice_reduce_fusion.5
  11.2 1.4 convolution_convert_fusion
  12.5 2.4 %reshape.123 = bf16[16,240,128]{2,1,0:T(8,128)(2,1)} reshape(bf16[96,5120]{1,0:T(8,128)(2,1)} %convolution_convert_fusion) | data formatting | bytes 1966080 | tf_op jit(solution)/shard_map/reshape | solution.py:485
  14.9 2.2 %fusion.3.refs_0_ = bf16[16,248,128]{2,1,0:T(8,128)(2,1)} fusion(bf16[16,1,6]{2,1,0:T(2,128)(2,1)S(1)} %convert_element_type.102, bf16[16,240,128]{2,1,0:T(8,128)(2,1)} %reshape.123), kind=kLoop, calls=%fused_computation.11 | loop fusion | flops 3047424 | bytes 1999040 | tf_op jit(solution)/shard_map/concatenate | solution.py:483
  17.1 8.6 %all-to-all-start = ((bf16[16,248,128]{2,1,0:T(8,128)(2,1)}), bf16[16,248,128]{2,1,0:T(8,128)(2,1)}, u32[]{:S(2)}, u32[]{:S(2)}) async-start(bf16[16,248,128]{2,1,0:T(8,128)(2,1)} %shard_map.152), calls=%async_computation | async-start | bytes 2031616 | tf_op jit(solution)/shard_map/all_to_all | solution.py:491
  25.7 1.7 %shard_map.146.mine_ref = bf16[128,640]{1,0:T(8,128)(2,1)} custom-call(bf16[128,512]{1,0:T(8,128)(2,1)} %bitcast.88, bf16[64,128]{1,0:T(8,128)(2,1)} %bitcast.89), custom_call_target="tpu_custom_call" | custom-call | flops 1000000 | bytes 1000000 | tf_op jit(solution)/shard_map/pallas_call | solution.py:93
  27.4 1.7 %collective-permute-done.twin_ref = bf16[128,640]{1,0:T(8,128)(2,1)} collective-permute-done((bf16[128,640]{1,0:T(8,128)(2,1)}, bf16[128,640]{1,0:T(8,128)(2,1)}, u32[]{:S(2)}, u32[]{:S(2)}) %collective-permute-start) | collective-permute-done | bytes 163872 | tf_op jit(solution)/shard_map/ppermute | solution.py:453
  29.1 0.8 slice_select_fusion
  30.0 3.0 %collective-permute-start.1 = (bf16[32,640]{1,0:T(8,128)(2,1)S(1)}, bf16[32,640]{1,0:T(8,128)(2,1)S(1)}, u32[]{:S(2)}, u32[]{:S(2)}) collective-permute-start(bf16[32,640]{1,0:T(8,128)(2,1)S(1)} %slice_select_fusion), channel_id=1, source_target_pairs={{0,32},{16,48},{32,64},{48,80},{64,96},{80,112},{96,128},{112,144}... | collective-permute-start | bytes 122888 | tf_op jit(solution)/shard_map/ppermute | solution.py:454
  33.7 4.8 %collective-permute-done.1.halo_ref = bf16[32,640]{1,0:T(8,128)(2,1)S(1)} collective-permute-done((bf16[32,640]{1,0:T(8,128)(2,1)S(1)}, bf16[32,640]{1,0:T(8,128)(2,1)S(1)}, u32[]{:S(2)}, u32[]{:S(2)}) %collective-permute-start.1) | collective-permute-done | bytes 40992 | tf_op jit(solution)/shard_map/ppermute | solution.py:454
  38.5 0.8 collective-permute-start.6
  39.3 1.9 %shard_map.147 = (bf16[288,512]{1,0:T(8,128)(2,1)}, bf16[288,128]{1,0:T(8,128)(2,1)}, f32[288,128]{1,0:T(8,128)}) custom-call(s32[11]{0:T(128)} %stack.68.where_ref, bf16[128,640]{1,0:T(8,128)(2,1)} %shard_map.146.mine_ref, bf16[128,640]{1,0:T(8,128)(2,1)} %collective-permute-done.twin_ref, bf16[32,640]{1,0:T(8,128)(2,1)} %copy-done.8), custom_call_target="tpu_custom_call" | custom-call | flops 1000000 | bytes 1000000 | tf_op jit(solution)/shard_map/pallas_call | solution.py:121
  41.2 1.5 collective-permute-start.8
  42.7 3.6 %collective-permute-start.9 = (bf16[1024,512]{1,0:T(8,128)(2,1)}, bf16[1024,512]{1,0:T(8,128)(2,1)}, u32[]{:S(2)}, u32[]{:S(2)}) collective-permute-start(bf16[1024,512]{1,0:T(8,128)(2,1)} %collective-permute-done.4.refs_8_.refs_9_), channel_id=1, source_target_pairs={{0,40},{1,41},{2,42},{3,43},{4,44},{5,45},{6,46},{7,47},{8,32},{9,... | collective-permute-start | bytes 3145736 | tf_op jit(solution)/shard_map/ppermute | solution.py:500
  46.9 0.8 copy-done.2
  47.7 6.8 %shard_map.149 = (bf16[128,12288]{1,0:T(8,128)(2,1)}, bf16[1,128,768]{2,1,0:T(8,128)(2,1)}, f32[288,512]{1,0:T(8,128)}, f32[288,128]{1,0:T(8,128)}, f32[8,128]{1,0:T(8,128)}) custom-call(s32[11]{0:T(128)} %stack.68.where_ref, bf16[288,512]{1,0:T(8,128)(2,1)} %get-tuple-element.26.refs_0_, bf16[288,128]{1,0:T(8,128)(2,1)} %get-tuple-element.27.refs_1_, ...), custom_call_target="tpu_custom_call" | custom-call | flops 500000000 | bytes 500000 | tf_op jit(solution)/shard_map/pallas_call | solution.py:333
  54.6 11.0 %shard_map.150 = (bf16[128,12288]{1,0:T(8,128)(2,1)}, bf16[2,128,768]{2,1,0:T(8,128)(2,1)}, f32[288,512]{1,0:T(8,128)}, f32[288,128]{1,0:T(8,128)}, f32[8,128]{1,0:T(8,128)}) custom-call(s32[11]{0:T(128)} %stack.68.where_ref, bf16[288,512]{1,0:T(8,128)(2,1)} %get-tuple-element.26.refs_0_, ...), custom_call_target="tpu_custom_call", output_to_operand_aliasing={{0}: (8, {})} | custom-call | flops 10000000000 | bytes 1000000 | tf_op jit(solution)/shard_map/pallas_call | solution.py:333
  65.5 1.0 collective-permute-done.6.refs_2_.other_ref
  66.6 2.2 %slice.115 = bf16[16,240,128]{2,1,0:T(8,128)(2,1)} slice(bf16[16,248,128]{2,1,0:T(8,128)(2,1)} %shard_map.153), slice={[0:16], [0:240], [0:128]} | slice | bytes 1966080 | tf_op jit(solution)/shard_map/slice | solution.py:506
  68.8 3.2 %reshape.124 = bf16[96,4,2,2,320]{4,3,2,1,0:T(2,128)(2,1)S(1)} reshape(bf16[16,240,128]{2,1,0:T(8,128)(2,1)} %slice.115) | data formatting | bytes 1966080 | tf_op jit(solution)/shard_map/reshape | solution.py:506
  72.0 1.3 copy.38
  73.3 4.8 %all-to-all-start.1 = ((bf16[8,192,320]{2,1,0:T(8,128)(2,1)}), bf16[8,192,320]{2,1,0:T(8,128)(2,1)S(1)}, u32[]{:S(2)}, u32[]{:S(2)}) async-start(bf16[8,192,320]{2,1,0:T(8,128)(2,1)} %bitcast.82), calls=%async_computation.1 | async-start | bytes 2359296 | tf_op jit(solution)/shard_map/all_to_all | solution.py:509
  78.1 1.9 %slice.117.refs_0_ = bf16[512,512]{1,0:T(8,128)(2,1)} slice(bf16[1024,512]{1,0:T(8,128)(2,1)} %collective-permute-done.8.refs_11_.refs_12_), slice={[512:1024], [0:512]} | slice | bytes 1048576 | tf_op jit(solution)/shard_map/slice | solution.py:522
  80.0 11.0 %shard_map.154 = (bf16[128,12288]{1,0:T(8,128)(2,1)}, bf16[2,128,768]{2,1,0:T(8,128)(2,1)}, f32[288,512]{1,0:T(8,128)}, f32[288,128]{1,0:T(8,128)}, f32[8,128]{1,0:T(8,128)}) custom-call(s32[11]{0:T(128)} %stack.68.where_ref, bf16[288,512]{1,0:T(8,128)(2,1)} %get-tuple-element.26.refs_0_, ...), custom_call_target="tpu_custom_call", output_to_operand_aliasing={{0}: (8, {})} | custom-call | flops 1000000000 | bytes 1000000 | tf_op jit(solution)/shard_map/pallas_call | solution.py:333
  91.0 1.9 %slice.116.refs_2_ = bf16[512,512]{1,0:T(8,128)(2,1)} slice(bf16[1024,512]{1,0:T(8,128)(2,1)} %shard_map.155.refs_11_.refs_12_), slice={[0:512], [0:512]} | slice | bytes 1048576 | tf_op jit(solution)/shard_map/slice | solution.py:521
  92.9 1.1 all-to-all-done.1
  94.0 1.0 copy-done.4
  95.1 4.9 %shard_map.157.refs_0_ = bf16[4,96,1536]{2,1,0:T(8,128)(2,1)} custom-call(s32[11]{0:T(128)} %stack.68.where_ref, bf16[4,2,192,320]{3,2,1,0:T(8,128)(2,1)} %bitcast.80, bf16[320,1536]{1,0:T(8,128)(2,1)} %bitcast.86, bf16[320,1536]{1,0:T(8,128)(2,1)} %collective-permute-done.6.refs_2_.other_ref, f32[8,128]{1,0:T(8,128)} %get-tuple-element.33.refs_1_.refs_0_, ...), custom_call_target="tpu_custom_call" | custom-call | flops 100000000 | bytes 100000 | tf_op jit(solution)/shard_map/pallas_call | solution.py:390
  100.0 1.5 collective-permute-start.12
  101.5 2.3 %collective-permute-start.13 = (bf16[512,512]{1,0:T(8,128)(2,1)S(1)}, bf16[512,512]{1,0:T(8,128)(2,1)}, u32[]{:S(2)}, u32[]{:S(2)}) collective-permute-start(bf16[512,512]{1,0:T(8,128)(2,1)S(1)} %copy-done.5), channel_id=1, source_target_pairs={{0,40},{1,41},{2,42},{3,43},{4,44},{5,45},{6,46},{7,47},{8,32},{9,... | collective-permute-start | bytes 1572872 | tf_op jit(solution)/shard_map/ppermute | solution.py:524
  103.7 4.8 %shard_map.158 = bf16[4,96,1536]{2,1,0:T(8,128)(2,1)} custom-call(s32[11]{0:T(128)} %stack.68.where_ref, bf16[4,2,192,320]{3,2,1,0:T(8,128)(2,1)} %bitcast.81, bf16[320,1536]{1,0:T(8,128)(2,1)} %bitcast.87, bf16[320,1536]{1,0:T(8,128)(2,1)} %collective-permute-done.6.refs_2_.other_ref, bf16[4,96,1536]{2,1,0:T(8,128)(2,1)} %shard_map.157.refs_0_), custom_call_target="tpu_custom_call" | custom-call | flops 100000000 | bytes 100000 | tf_op jit(solution)/shard_map/pallas_call | solution.py:390
  108.6 2.7 %add_convert_fusion.refs_8_ = bf16[4,96,1536]{2,1,0:T(8,128)(2,1)} fusion(bf16[4,96,1536]{2,1,0:T(8,128)(2,1)S(1)} %collective-permute-done.11, bf16[4,96,1536]{2,1,0:T(8,128)(2,1)} %shard_map.158), kind=kLoop, calls=%fused_computation.2 | loop fusion | flops 2359296 | bytes 3538944 | tf_op jit(solution)/shard_map/convert_element_type | solution.py:532
  111.2 4.6 %all-to-all-start.2 = ((bf16[4,96,1536]{2,1,0:T(8,128)(2,1)}), bf16[4,96,1536]{2,1,0:T(8,128)(2,1)S(1)}, u32[]{:S(2)}, u32[]{:S(2)}) async-start(bf16[4,96,1536]{2,1,0:T(8,128)(2,1)} %add_convert_fusion.refs_8_), calls=%async_computation.2 | async-start | bytes 2359296 | tf_op jit(solution)/shard_map/all_to_all | solution.py:533
  117.3 14.9 %shard_map.159 = (bf16[128,12288]{1,0:T(8,128)(2,1)}, bf16[3,128,768]{2,1,0:T(8,128)(2,1)}, f32[288,512]{1,0:T(8,128)}, f32[288,128]{1,0:T(8,128)}, f32[8,128]{1,0:T(8,128)}) custom-call(s32[11]{0:T(128)} %stack.68.where_ref, bf16[288,512]{1,0:T(8,128)(2,1)} %get-tuple-element.26.refs_0_, ...), custom_call_target="tpu_custom_call", output_to_operand_aliasing={{0}: (8, {})} | custom-call | flops 1500000000 | bytes 1500000 | tf_op jit(solution)/shard_map/pallas_call | solution.py:333
  132.8 1.1 slice_add_fusion
  133.9 1.0 copy-done.3
  134.9 0.9 pad_maximum_fusion.1
  135.8 3.0 %collective-permute-start.18 = (f32[32,576]{1,0:T(8,128)S(1)}, f32[32,576]{1,0:T(8,128)S(1)}, u32[]{:S(2)}, u32[]{:S(2)}) collective-permute-start(f32[32,576]{1,0:T(8,128)S(1)} %pad_maximum_fusion.1), channel_id=1, source_target_pairs={{32,0},{48,16},{64,32},{80,48},{96,64},{112,80},{128,96},{144,112}... | collective-permute-start | bytes 221192 | tf_op jit(solution)/shard_map/ppermute | solution.py:554
  138.8 1.5 convert_reduce_fusion
  141.2 8.1 %all-to-all-start.3 = ((f32[16,1,6]{2,1,0:T(1,128)}), f32[16,1,6]{2,1,0:T(1,128)S(1)}, u32[]{:S(2)}, u32[]{:S(2)}) async-start(f32[16,1,6]{2,1,0:T(1,128)} %bitcast.38), calls=%async_computation.3 | async-start | bytes 16384 | tf_op jit(solution)/shard_map/all_to_all | solution.py:564
  149.3 0.8 fusion.7
  150.1 0.8 fusion.5
  151.7 3.0 %shard_map.160 = bf16[128,12288]{1,0:T(8,128)(2,1)} custom-call(s32[11]{0:T(128)} %stack.68.where_ref, bf16[128,12288]{1,0:T(8,128)(2,1)} %get-tuple-element.40.grid_ref, f32[1,96]{1,0:T(1,128)} %bitcast.91, bf16[1,128,768]{2,1,0:T(8,128)(2,1)} %collective-permute-done.14.refs_0_, bf16[2,128,768]{2,1,0:T(8,128)(2,1)} %copy-done.6, ...), custom_call_target="tpu_custom_call", output_to_operand_aliasing={{}: (1, {})} | custom-call | flops 1000000 | bytes 1000000 | tf_op jit(solution)/shard_map/pallas_call | solution.py:163
  154.7 3.0 %all-to-all-done.3 = f32[16,1,6]{2,1,0:T(1,128)S(1)} async-done(((f32[16,1,6]{2,1,0:T(1,128)}), f32[16,1,6]{2,1,0:T(1,128)S(1)}, u32[]{:S(2)}, u32[]{:S(2)}) %all-to-all-start.3) | async-done | bytes 416 | tf_op jit(solution)/shard_map/all_to_all | solution.py:564
  159.7 1.0 add_convert_fusion.1
  (78 shorter events, 10.7 us)
Async XLA Ops:
  0.6 10.5 %copy-start = (bf16[1,128,5120]{2,1,0:T(8,128)(2,1)S(1)}, bf16[1,128,5120]{2,1,0:T(8,128)(2,1)}, u32[]{:S(2)}) copy-start(bf16[1,128,5120]{2,1,0:T(8,128)(2,1)} %param.17) | copy-start | bytes 3932164
  0.6 7.9 %copy-start.11 = (s32[1,128,6]{1,0,2:T(1,128)S(1)}, s32[1,128,6]{1,0,2:T(1,128)}, u32[]{:S(2)}) copy-start(s32[1,128,6]{1,0,2:T(1,128)} %param.18) | copy-start | bytes 9220
  0.7 10.1 %copy-start.10 = (bf16[1,128,6]{1,2,0:T(8,128)(2,1)S(1)}, bf16[1,128,6]{1,2,0:T(8,128)(2,1)}, u32[]{:S(2)}) copy-start(bf16[1,128,6]{1,2,0:T(8,128)(2,1)} %param.19) | copy-start | bytes 4612
  0.7 16.4 %collective-permute-start.2 = (bf16[128,12288]{1,0:T(8,128)(2,1)}, bf16[128,12288]{1,0:T(8,128)(2,1)}, u32[]{:S(2)}, u32[]{:S(2)}) collective-permute-start(bf16[128,12288]{1,0:T(8,128)(2,1)} %bitcast.69), channel_id=1, source_target_pairs={{0,16},{16,0},{32,48},{48,32},{64,80},{80,64},{96,112},{112,96},{1... | collective-permute-start | bytes 9437192 | tf_op jit(solution)/shard_map/ppermute | solution.py:461
  0.8 45.6 %collective-permute-start.3 = (bf16[128,8192]{1,0:T(8,128)(2,1)}, bf16[128,8192]{1,0:T(8,128)(2,1)S(1)}, u32[]{:S(2)}, u32[]{:S(2)}) collective-permute-start(bf16[128,8192]{1,0:T(8,128)(2,1)} %bitcast.75), channel_id=1, source_target_pairs={{0,16},{16,0},{32,48},{48,32},{64,80},{80,64},{96,112},{112,96},{1... | collective-permute-start | bytes 6291464 | tf_op jit(solution)/shard_map/ppermute | solution.py:462
  3.5 37.7 %collective-permute-start.4 = (bf16[1024,512]{1,0:T(8,128)(2,1)}, bf16[1024,512]{1,0:T(8,128)(2,1)}, u32[]{:S(2)}, u32[]{:S(2)}) collective-permute-start(bf16[1024,512]{1,0:T(8,128)(2,1)} %shard_map.148.refs_7_.refs_8_.refs_1_.refs_2_), channel_id=1, source_target_pairs={{0,64},{16,80},{32,96},{48,112},{64,128},{80,144},{96,160},{112,17... | collective-permute-start | bytes 3145736 | tf_op jit(solution)/shard_map/ppermute | solution.py:458
  5.0 49.5 %collective-permute-start.5 = (bf16[1024,512]{1,0:T(8,128)(2,1)}, bf16[1024,512]{1,0:T(8,128)(2,1)}, u32[]{:S(2)}, u32[]{:S(2)}) collective-permute-start(bf16[1024,512]{1,0:T(8,128)(2,1)} %shard_map.148.refs_7_.refs_8_.refs_1_.refs_2_), channel_id=1, source_target_pairs={{0,192},{16,208},{32,224},{48,240},{64,0},{80,16},{96,32},{112,48}... | collective-permute-start | bytes 3145736 | tf_op jit(solution)/shard_map/ppermute | solution.py:459
  5.8 36.9 %collective-permute-start.7 = (bf16[1024,512]{1,0:T(8,128)(2,1)}, bf16[1024,512]{1,0:T(8,128)(2,1)}, u32[]{:S(2)}, u32[]{:S(2)}) collective-permute-start(bf16[1024,512]{1,0:T(8,128)(2,1)} %shard_map.148.refs_7_.refs_8_.refs_1_.refs_2_), channel_id=1, source_target_pairs={{0,40},{1,41},{2,42},{3,43},{4,44},{5,45},{6,46},{7,47},{8,32},{9,... | collective-permute-start | bytes 3145736 | tf_op jit(solution)/shard_map/ppermute | solution.py:460
  17.1 49.5 %all-to-all-start = ((bf16[16,248,128]{2,1,0:T(8,128)(2,1)}), bf16[16,248,128]{2,1,0:T(8,128)(2,1)}, u32[]{:S(2)}, u32[]{:S(2)}) async-start(bf16[16,248,128]{2,1,0:T(8,128)(2,1)} %shard_map.152), calls=%async_computation | async-start | bytes 2031616 | tf_op jit(solution)/shard_map/all_to_all | solution.py:491
  27.4 1.7 %collective-permute-start = (bf16[128,640]{1,0:T(8,128)(2,1)}, bf16[128,640]{1,0:T(8,128)(2,1)}, u32[]{:S(2)}, u32[]{:S(2)}) collective-permute-start(bf16[128,640]{1,0:T(8,128)(2,1)} %shard_map.146.mine_ref), channel_id=1, source_target_pairs={{0,16},{16,0},{32,48},{48,32},{64,80},{80,64},{96,112},{112,96},{1... | collective-permute-start | bytes 491528 | tf_op jit(solution)/shard_map/ppermute | solution.py:453
  30.0 8.5 %collective-permute-start.1 = (bf16[32,640]{1,0:T(8,128)(2,1)S(1)}, bf16[32,640]{1,0:T(8,128)(2,1)S(1)}, u32[]{:S(2)}, u32[]{:S(2)}) collective-permute-start(bf16[32,640]{1,0:T(8,128)(2,1)S(1)} %slice_select_fusion), channel_id=1, source_target_pairs={{0,32},{16,48},{32,64},{48,80},{64,96},{80,112},{96,128},{112,144}... | collective-permute-start | bytes 122888 | tf_op jit(solution)/shard_map/ppermute | solution.py:454
  38.5 0.8 copy-start.8
  38.5 28.1 %collective-permute-start.6 = (bf16[320,1536]{1,0:T(8,128)(2,1)}, bf16[320,1536]{1,0:T(8,128)(2,1)}, u32[]{:S(2)}, u32[]{:S(2)}) collective-permute-start(bf16[320,1536]{1,0:T(8,128)(2,1)} %bitcast.85), channel_id=1, source_target_pairs={{0,32},{16,48},{32,0},{48,16},{64,96},{80,112},{96,64},{112,80},{1... | collective-permute-start | bytes 2949128 | tf_op jit(solution)/shard_map/ppermute | solution.py:464
  41.2 36.9 %collective-permute-start.8 = (bf16[1024,512]{1,0:T(8,128)(2,1)}, bf16[1024,512]{1,0:T(8,128)(2,1)}, u32[]{:S(2)}, u32[]{:S(2)}) collective-permute-start(bf16[1024,512]{1,0:T(8,128)(2,1)} %collective-permute-done.4.refs_8_.refs_9_), channel_id=1, source_target_pairs={{0,64},{16,80},{32,96},{48,112},{64,128},{80,144},{96,160},{112,17... | collective-permute-start | bytes 3145736 | tf_op jit(solution)/shard_map/ppermute | solution.py:498
  42.7 50.2 %collective-permute-start.9 = (bf16[1024,512]{1,0:T(8,128)(2,1)}, bf16[1024,512]{1,0:T(8,128)(2,1)}, u32[]{:S(2)}, u32[]{:S(2)}) collective-permute-start(bf16[1024,512]{1,0:T(8,128)(2,1)} %collective-permute-done.4.refs_8_.refs_9_), channel_id=1, source_target_pairs={{0,40},{1,41},{2,42},{3,43},{4,44},{5,45},{6,46},{7,47},{8,32},{9,... | collective-permute-start | bytes 3145736 | tf_op jit(solution)/shard_map/ppermute | solution.py:500
  46.3 1.4 copy-start.2
  46.3 44.7 %collective-permute-start.10 = (bf16[1024,512]{1,0:T(8,128)(2,1)}, bf16[1024,512]{1,0:T(8,128)(2,1)}, u32[]{:S(2)}, u32[]{:S(2)}) collective-permute-start(bf16[1024,512]{1,0:T(8,128)(2,1)} %collective-permute-done.7.refs_9_.refs_10_), channel_id=1, source_target_pairs={{0,192},{16,208},{32,224},{48,240},{64,0},{80,16},{96,32},{112,48}... | collective-permute-start | bytes 3145736 | tf_op jit(solution)/shard_map/ppermute | solution.py:499
  73.3 20.8 %all-to-all-start.1 = ((bf16[8,192,320]{2,1,0:T(8,128)(2,1)}), bf16[8,192,320]{2,1,0:T(8,128)(2,1)S(1)}, u32[]{:S(2)}, u32[]{:S(2)}) async-start(bf16[8,192,320]{2,1,0:T(8,128)(2,1)} %bitcast.82), calls=%async_computation.1 | async-start | bytes 2359296 | tf_op jit(solution)/shard_map/all_to_all | solution.py:509
  94.0 1.1 copy-start.4
  95.1 6.4 %copy-start.5 = (bf16[512,512]{1,0:T(8,128)(2,1)S(1)}, bf16[512,512]{1,0:T(8,128)(2,1)}, u32[]{:S(2)}) copy-start(bf16[512,512]{1,0:T(8,128)(2,1)} %shard_map.156.refs_3_) | copy-start | bytes 1572868
  100.0 8.6 %collective-permute-start.11 = (bf16[4,96,1536]{2,1,0:T(8,128)(2,1)}, bf16[4,96,1536]{2,1,0:T(8,128)(2,1)S(1)}, u32[]{:S(2)}, u32[]{:S(2)}) collective-permute-start(bf16[4,96,1536]{2,1,0:T(8,128)(2,1)} %shard_map.157.refs_0_), channel_id=1, source_target_pairs={{0,16},{16,0},{32,48},{48,32},{64,80},{80,64},{96,112},{112,96},{1... | collective-permute-start | bytes 3538952 | tf_op jit(solution)/shard_map/ppermute | solution.py:530
  100.0 17.2 %collective-permute-start.12 = (bf16[512,512]{1,0:T(8,128)(2,1)}, bf16[512,512]{1,0:T(8,128)(2,1)}, u32[]{:S(2)}, u32[]{:S(2)}) collective-permute-start(bf16[512,512]{1,0:T(8,128)(2,1)} %slice.116.refs_2_), channel_id=1, source_target_pairs={{0,192},{16,208},{32,224},{48,240},{64,0},{80,16},{96,32},{112,48}... | collective-permute-start | bytes 1572872 | tf_op jit(solution)/shard_map/ppermute | solution.py:523
  101.5 15.8 %collective-permute-start.13 = (bf16[512,512]{1,0:T(8,128)(2,1)S(1)}, bf16[512,512]{1,0:T(8,128)(2,1)}, u32[]{:S(2)}, u32[]{:S(2)}) collective-permute-start(bf16[512,512]{1,0:T(8,128)(2,1)S(1)} %copy-done.5), channel_id=1, source_target_pairs={{0,40},{1,41},{2,42},{3,43},{4,44},{5,45},{6,46},{7,47},{8,32},{9,... | collective-permute-start | bytes 1572872 | tf_op jit(solution)/shard_map/ppermute | solution.py:524
  111.2 22.7 %all-to-all-start.2 = ((bf16[4,96,1536]{2,1,0:T(8,128)(2,1)}), bf16[4,96,1536]{2,1,0:T(8,128)(2,1)S(1)}, u32[]{:S(2)}, u32[]{:S(2)}) async-start(bf16[4,96,1536]{2,1,0:T(8,128)(2,1)} %add_convert_fusion.refs_8_), calls=%async_computation.2 | async-start | bytes 2359296 | tf_op jit(solution)/shard_map/all_to_all | solution.py:533
  115.9 35.1 %collective-permute-start.14 = (bf16[1,128,768]{2,1,0:T(8,128)(2,1)}, bf16[1,128,768]{2,1,0:T(8,128)(2,1)}, u32[]{:S(2)}, u32[]{:S(2)}) collective-permute-start(bf16[1,128,768]{2,1,0:T(8,128)(2,1)} %get-tuple-element.41), channel_id=1, source_target_pairs={{0,16},{16,0},{32,48},{48,32},{64,80},{80,64},{96,112},{112,96},{1... | collective-permute-start | bytes 589832 | tf_op jit(solution)/shard_map/ppermute | solution.py:516
  115.9 35.1 %collective-permute-start.15 = (bf16[2,128,768]{2,1,0:T(8,128)(2,1)}, bf16[2,128,768]{2,1,0:T(8,128)(2,1)S(1)}, u32[]{:S(2)}, u32[]{:S(2)}) collective-permute-start(bf16[2,128,768]{2,1,0:T(8,128)(2,1)} %get-tuple-element.42), channel_id=1, source_target_pairs={{0,16},{16,0},{32,48},{48,32},{64,80},{80,64},{96,112},{112,96},{1... | collective-permute-start | bytes 1179656 | tf_op jit(solution)/shard_map/ppermute | solution.py:518
  116.4 34.6 %collective-permute-start.16 = (bf16[2,128,768]{2,1,0:T(8,128)(2,1)}, bf16[2,128,768]{2,1,0:T(8,128)(2,1)}, u32[]{:S(2)}, u32[]{:S(2)}) collective-permute-start(bf16[2,128,768]{2,1,0:T(8,128)(2,1)} %get-tuple-element.43), channel_id=1, source_target_pairs={{0,16},{16,0},{32,48},{48,32},{64,80},{80,64},{96,112},{112,96},{1... | collective-permute-start | bytes 1179656 | tf_op jit(solution)/shard_map/ppermute | solution.py:517
  132.2 18.8 %collective-permute-start.17 = (bf16[3,128,768]{2,1,0:T(8,128)(2,1)}, bf16[3,128,768]{2,1,0:T(8,128)(2,1)}, u32[]{:S(2)}, u32[]{:S(2)}) collective-permute-start(bf16[3,128,768]{2,1,0:T(8,128)(2,1)} %get-tuple-element.44), channel_id=1, source_target_pairs={{0,16},{16,0},{32,48},{48,32},{64,80},{80,64},{96,112},{112,96},{1... | collective-permute-start | bytes 1769480 | tf_op jit(solution)/shard_map/ppermute | solution.py:549
  133.9 1.0 copy-start.3
  134.9 5.4 %copy-start.7 = (bf16[1,1,96,1536]{3,2,1,0:T(8,128)(2,1)S(1)}, bf16[1,1,96,1536]{3,2,1,0:T(8,128)(2,1)}, u32[]{:S(2)}) copy-start(bf16[1,1,96,1536]{3,2,1,0:T(8,128)(2,1)} %param.20) | copy-start | bytes 884740
  134.9 14.4 %copy-start.1 = (f32[288,512]{1,0:T(8,128)S(1)}, f32[288,512]{1,0:T(8,128)}, u32[]{:S(2)}) copy-start(f32[288,512]{1,0:T(8,128)} %shard_map.161) | copy-start | bytes 1769476
  135.8 13.5 %collective-permute-start.18 = (f32[32,576]{1,0:T(8,128)S(1)}, f32[32,576]{1,0:T(8,128)S(1)}, u32[]{:S(2)}, u32[]{:S(2)}) collective-permute-start(f32[32,576]{1,0:T(8,128)S(1)} %pad_maximum_fusion.1), channel_id=1, source_target_pairs={{32,0},{48,16},{64,32},{80,48},{96,64},{112,80},{128,96},{144,112}... | collective-permute-start | bytes 221192 | tf_op jit(solution)/shard_map/ppermute | solution.py:554
  140.5 10.5 %copy-start.9 = (f32[96]{0:T(128)}, f32[96]{0:T(128)S(1)}, u32[]{:S(2)}) copy-start(f32[96]{0:T(128)S(1)} %fusion.4) | copy-start | bytes 1156
  141.2 16.5 %all-to-all-start.3 = ((f32[16,1,6]{2,1,0:T(1,128)}), f32[16,1,6]{2,1,0:T(1,128)S(1)}, u32[]{:S(2)}, u32[]{:S(2)}) async-start(f32[16,1,6]{2,1,0:T(1,128)} %bitcast.38), calls=%async_computation.3 | async-start | bytes 16384 | tf_op jit(solution)/shard_map/all_to_all | solution.py:564
  150.1 9.5 %collective-permute-start.19 = (f32[128,576]{1,0:T(8,128)}, f32[128,576]{1,0:T(8,128)}, u32[]{:S(2)}, u32[]{:S(2)}) collective-permute-start(f32[128,576]{1,0:T(8,128)} %fusion.7), channel_id=1, source_target_pairs={{0,16},{16,0},{32,48},{48,32},{64,80},{80,64},{96,112},{112,96},{1... | collective-permute-start | bytes 884744 | tf_op jit(solution)/shard_map/ppermute | solution.py:559
  151.0 0.8 copy-start.6

commit v5 on v4

--- a/solution.py
+++ b/solution.py
@@ -493,13 +493,11 @@
     shared = prepare(where, mine, twin_rows, halo)
     common = (shared, query, out_grad, twin_query, twin_grad)
 
-    *sums, part_a, mark_a = attend(where, 1, *common, [both(own)])
-
     opposite = lax.ppermute(before, "ctx", RIGHT)
     beside_after = lax.ppermute(beside, "ctx", LEFT)
     beside_before = lax.ppermute(before, ("ctx", "exp"), ACROSS)
     *sums, part_b, mark_b = attend(
-        where, 2, *common, [both(before), both(after)], sums, heavy=10
+        where, 1, *common, [both(own), both(before), both(after)], heavy=10
     )
     routed = tie(routed, mark_b, other_down)
     row_gate = routed[:, CAP * tiles, :CAP].reshape(EXP * CAP, 1)
@@ -513,7 +511,6 @@
     *sums, part_d, mark_d = attend(
         where, 4, *common, [both(beside), both(opposite)], sums, (sent,)
     )
-    part_a = lax.ppermute(part_a, "ctx", TWIN)
     part_d = lax.ppermute(part_d, "ctx", TWIN)
     part_b = lax.ppermute(part_b, "ctx", TWIN)
 
@@ -564,7 +561,7 @@
     returned = lax.all_to_all(
         gate_part.reshape(EXP, CAP), "exp", split_axis=0, concat_axis=0, tiled=True
     )
-    query_grad = place(where, query_grad, (part_a, part_b, part_d, part_c), gate_part[None])
+    query_grad = place(where, query_grad, (part_b, part_d, part_c), gate_part[None])
     found = token_hot.astype(jnp.float32) * returned.reshape(1, -1)
     gate_grad = jnp.stack(
         [jnp.sum(jnp.where(match[k], found, 0.0), axis=1) for k in range(TOPK)], axis=1

time: 163 us -> 163 us (level)
  Pallas kernels: 62.3 us -> 59 us
  other arithmetic: 13.6 us -> 15.3 us
    ppermute x1, waiting for transfers between devices: 1.04 us -> 5.09 us  [local(): other_down = lax.ppermute(down, 'ctx', [(i, i ^ 2) for i in range(CTX)])]
    pallas_call x4 -> x3, Pallas kernels: 43.7 us -> 40.6 us  [attend(): pl.pallas_call(functools.partial(attend_body, count, base, len(skipped)),...]
    unnamed x27 -> x61, local copies, waits for them, and re-layouts: 5.68 us -> 7.72 us
    reshape x1, local copies, waits for them, and re-layouts: 2.36 us -> 0.45 us  [local(): outbound.reshape(EXP, CAP * tiles, NOPE)]
  transfers between devices with their start and end apart: 24 -> 23, of which waited for: 5 -> 5; matrix products, arithmetic and copies ran while one was open for 19% -> 19% of each run, Pallas kernels for 35% -> 34%
where the time goes in v5:
time: 163 us; the launch traced here: 162 us
  Pallas kernels  59 us (36%)
  starting transfers between devices  49.4 us (30%)
  local copies, waits for them, and re-layouts  23.4 us (14%)
  other arithmetic  15.3 us (9%)
  waiting for transfers between devices  12.9 us (8%)
    pallas_call x3, Pallas kernels, attend(): pl.pallas_call(functools.partial(attend_body, count, base, len(skipped)),...  40.6 us
    pallas_call x2, Pallas kernels, terms(): pl.pallas_call(terms_body, grid_spec=pltpu.PrefetchScalarGridSpec(num_sca...  9.59 us
    all_to_all x1, starting transfers between devices, local(): lax.all_to_all(outbound, 'exp', split_axis=0, concat_axis=0, tiled=True)  8.56 us
    all_to_all x1, starting transfers between devices, local(): lax.all_to_all(gate_part.reshape(EXP, CAP), 'exp', split_axis=0, concat_a...  8.01 us
    unnamed x61, local copies, waits for them, and re-layouts  7.72 us
    all_to_all x1, starting transfers between devices, local(): lax.all_to_all(keep, 'ctx', split_axis=0, concat_axis=0, tiled=True, axis...  5.33 us
    ppermute x1, waiting for transfers between devices, local(): other_down = lax.ppermute(down, 'ctx', [(i, i ^ 2) for i in range(CTX)])  5.09 us
    all_to_all x1, starting transfers between devices, local(): lax.all_to_all(slices, 'ctx', split_axis=0, concat_axis=0, tiled=True, ax...  4.83 us
  transfers between devices with their start and end apart: 23, of which 5 were waited for; matrix products, arithmetic and copies ran while one was open for 19% of the time, Pallas kernels for 34%

profile of v5, /device:TPU:2, one launch (start us, length us, event | category | flops | bytes accessed | tf_op | source)
XLA Modules:
  0.0 161.9 jit_solution(3031243289009251334)
XLA Ops:
  1.3 2.3 %shard_map.148.refs_7_.refs_8_.refs_1_.refs_2_ = bf16[1024,512]{1,0:T(8,128)(2,1)} custom-call(bf16[512,512]{1,0:T(8,128)(2,1)} %key_ref.1, bf16[512,512]{1,0:T(8,128)(2,1)} %value_ref.1), custom_call_target="tpu_custom_call" | custom-call | flops 1000000 | bytes 1000000 | tf_op jit(solution)/shard_map/pallas_call | solution.py:78
  3.5 1.5 collective-permute-start.4
  5.8 2.8 %collective-permute-start.7 = (bf16[1024,512]{1,0:T(8,128)(2,1)}, bf16[1024,512]{1,0:T(8,128)(2,1)}, u32[]{:S(2)}, u32[]{:S(2)}) collective-permute-start(bf16[1024,512]{1,0:T(8,128)(2,1)} %shard_map.148.refs_7_.refs_8_.refs_1_.refs_2_), channel_id=1, source_target_pairs={{0,40},{1,41},{2,42},{3,43},{4,44},{5,45},{6,46},{7,47},{8,32},{9,... | collective-permute-start | bytes 3145736 | tf_op jit(solution)/shard_map/ppermute | solution.py:460
  9.4 1.4 slice_reduce_fusion.5
  12.9 1.1 fusion.3.refs_0_
  13.9 8.6 %all-to-all-start = ((bf16[16,248,128]{2,1,0:T(8,128)(2,1)}), bf16[16,248,128]{2,1,0:T(8,128)(2,1)S(1)}, u32[]{:S(2)}, u32[]{:S(2)}) async-start(bf16[16,248,128]{2,1,0:T(8,128)(2,1)} %shard_map.151), calls=%async_computation | async-start | bytes 2031616 | tf_op jit(solution)/shard_map/all_to_all | solution.py:491
  22.5 1.7 %shard_map.146.mine_ref = bf16[128,640]{1,0:T(8,128)(2,1)} custom-call(bf16[128,512]{1,0:T(8,128)(2,1)} %bitcast.83, bf16[64,128]{1,0:T(8,128)(2,1)} %bitcast.84), custom_call_target="tpu_custom_call" | custom-call | flops 1000000 | bytes 1000000 | tf_op jit(solution)/shard_map/pallas_call | solution.py:93
  24.2 1.6 collective-permute-done.twin_ref
  25.8 0.8 slice_select_fusion
  26.6 3.0 %collective-permute-start.1 = (bf16[32,640]{1,0:T(8,128)(2,1)S(1)}, bf16[32,640]{1,0:T(8,128)(2,1)S(1)}, u32[]{:S(2)}, u32[]{:S(2)}) collective-permute-start(bf16[32,640]{1,0:T(8,128)(2,1)S(1)} %slice_select_fusion), channel_id=1, source_target_pairs={{0,32},{16,48},{32,64},{48,80},{64,96},{80,112},{96,128},{112,144}... | collective-permute-start | bytes 122888 | tf_op jit(solution)/shard_map/ppermute | solution.py:454
  30.4 4.7 %collective-permute-done.1.halo_ref = bf16[32,640]{1,0:T(8,128)(2,1)S(1)} collective-permute-done((bf16[32,640]{1,0:T(8,128)(2,1)S(1)}, bf16[32,640]{1,0:T(8,128)(2,1)S(1)}, u32[]{:S(2)}, u32[]{:S(2)}) %collective-permute-start.1) | collective-permute-done | bytes 40992 | tf_op jit(solution)/shard_map/ppermute | solution.py:454
  35.1 0.8 collective-permute-start.6
  35.9 1.9 %shard_map.147 = (bf16[288,512]{1,0:T(8,128)(2,1)}, bf16[288,128]{1,0:T(8,128)(2,1)}, f32[288,128]{1,0:T(8,128)}) custom-call(s32[11]{0:T(128)} %stack.68.where_ref, bf16[128,640]{1,0:T(8,128)(2,1)} %shard_map.146.mine_ref, bf16[128,640]{1,0:T(8,128)(2,1)} %copy-done.8, bf16[32,640]{1,0:T(8,128)(2,1)} %copy-done.11), custom_call_target="tpu_custom_call" | custom-call | flops 1000000 | bytes 1000000 | tf_op jit(solution)/shard_map/pallas_call | solution.py:121
  37.8 1.5 collective-permute-start.8
  39.3 3.7 %collective-permute-start.9 = (bf16[1024,512]{1,0:T(8,128)(2,1)}, bf16[1024,512]{1,0:T(8,128)(2,1)}, u32[]{:S(2)}, u32[]{:S(2)}) collective-permute-start(bf16[1024,512]{1,0:T(8,128)(2,1)} %collective-permute-done.4.refs_9_.refs_10_), channel_id=1, source_target_pairs={{0,40},{1,41},{2,42},{3,43},{4,44},{5,45},{6,46},{7,47},{8,32},{9,... | collective-permute-start | bytes 3145736 | tf_op jit(solution)/shard_map/ppermute | solution.py:498
  43.6 14.7 %shard_map.149 = (bf16[128,12288]{1,0:T(8,128)(2,1)}, bf16[3,128,768]{2,1,0:T(8,128)(2,1)}, f32[288,512]{1,0:T(8,128)}, f32[288,128]{1,0:T(8,128)}, f32[8,128]{1,0:T(8,128)}) custom-call(s32[11]{0:T(128)} %stack.68.where_ref, bf16[288,512]{1,0:T(8,128)(2,1)} %get-tuple-element.22.refs_0_, bf16[288,128]{1,0:T(8,128)(2,1)} %get-tuple-element.23.refs_1_, ...), custom_call_target="tpu_custom_call" | custom-call | flops 15000000512 | bytes 1500000 | tf_op jit(solution)/shard_map/pallas_call | solution.py:333
  58.2 5.1 %collective-permute-done.6.refs_2_.other_ref = bf16[320,1536]{1,0:T(8,128)(2,1)} collective-permute-done((bf16[320,1536]{1,0:T(8,128)(2,1)}, bf16[320,1536]{1,0:T(8,128)(2,1)}, u32[]{:S(2)}, u32[]{:S(2)}) %collective-permute-start.6) | collective-permute-done | bytes 983072 | tf_op jit(solution)/shard_map/ppermute | solution.py:464
  63.3 1.0 copy-done.5
  64.3 2.2 %slice.115 = bf16[16,240,128]{2,1,0:T(8,128)(2,1)} slice(bf16[16,248,128]{2,1,0:T(8,128)(2,1)} %shard_map.152), slice={[0:16], [0:240], [0:128]} | slice | bytes 1966080 | tf_op jit(solution)/shard_map/slice | solution.py:504
  66.6 3.2 %reshape.124 = bf16[96,4,2,2,320]{4,3,2,1,0:T(2,128)(2,1)S(1)} reshape(bf16[16,240,128]{2,1,0:T(8,128)(2,1)} %slice.115) | data formatting | bytes 1966080 | tf_op jit(solution)/shard_map/reshape | solution.py:504
  69.7 1.3 copy.37
  71.1 4.8 %all-to-all-start.1 = ((bf16[8,192,320]{2,1,0:T(8,128)(2,1)}), bf16[8,192,320]{2,1,0:T(8,128)(2,1)S(1)}, u32[]{:S(2)}, u32[]{:S(2)}) async-start(bf16[8,192,320]{2,1,0:T(8,128)(2,1)} %bitcast.76), calls=%async_computation.1 | async-start | bytes 2359296 | tf_op jit(solution)/shard_map/all_to_all | solution.py:507
  75.9 1.9 %slice.117.refs_0_ = bf16[512,512]{1,0:T(8,128)(2,1)} slice(bf16[1024,512]{1,0:T(8,128)(2,1)} %collective-permute-done.8.refs_11_.refs_12_), slice={[512:1024], [0:512]} | slice | bytes 1048576 | tf_op jit(solution)/shard_map/slice | solution.py:519
  77.8 11.0 %shard_map.153 = (bf16[128,12288]{1,0:T(8,128)(2,1)}, bf16[2,128,768]{2,1,0:T(8,128)(2,1)}, f32[288,512]{1,0:T(8,128)}, f32[288,128]{1,0:T(8,128)}, f32[8,128]{1,0:T(8,128)}) custom-call(s32[11]{0:T(128)} %stack.68.where_ref, bf16[288,512]{1,0:T(8,128)(2,1)} %get-tuple-element.22.refs_0_, ...), custom_call_target="tpu_custom_call", output_to_operand_aliasing={{0}: (8, {})} | custom-call | flops 1000000000 | bytes 1000000 | tf_op jit(solution)/shard_map/pallas_call | solution.py:333
  88.8 1.0 copy-done.2
  89.8 1.9 %slice.116.refs_2_ = bf16[512,512]{1,0:T(8,128)(2,1)} slice(bf16[1024,512]{1,0:T(8,128)(2,1)} %shard_map.154.refs_11_.refs_12_), slice={[0:512], [0:512]} | slice | bytes 1048576 | tf_op jit(solution)/shard_map/slice | solution.py:518
  91.8 1.1 copy-done.4
  92.9 4.7 %shard_map.156.refs_0_ = bf16[4,96,1536]{2,1,0:T(8,128)(2,1)} custom-call(s32[11]{0:T(128)} %stack.68.where_ref, bf16[4,2,192,320]{3,2,1,0:T(8,128)(2,1)} %bitcast.74, bf16[320,1536]{1,0:T(8,128)(2,1)} %bitcast.26.own_ref, bf16[320,1536]{1,0:T(8,128)(2,1)} %collective-permute-done.6.refs_2_.other_ref, f32[8,128]{1,0:T(8,128)} %get-tuple-element.26.refs_1_.refs_0_, ...), custom_call_target="tpu_custom_call" | custom-call | flops 100000000 | bytes 100000 | tf_op jit(solution)/shard_map/pallas_call | solution.py:390
  97.7 1.4 collective-permute-start.12
  99.1 2.2 %collective-permute-start.13 = (bf16[512,512]{1,0:T(8,128)(2,1)}, bf16[512,512]{1,0:T(8,128)(2,1)}, u32[]{:S(2)}, u32[]{:S(2)}) collective-permute-start(bf16[512,512]{1,0:T(8,128)(2,1)} %shard_map.155.refs_3_), channel_id=1, source_target_pairs={{0,40},{1,41},{2,42},{3,43},{4,44},{5,45},{6,46},{7,47},{8,32},{9,... | collective-permute-start | bytes 1572872 | tf_op jit(solution)/shard_map/ppermute | solution.py:521
  101.2 4.8 %shard_map.157 = bf16[4,96,1536]{2,1,0:T(8,128)(2,1)} custom-call(s32[11]{0:T(128)} %stack.68.where_ref, bf16[4,2,192,320]{3,2,1,0:T(8,128)(2,1)} %bitcast.75, bf16[320,1536]{1,0:T(8,128)(2,1)} %bitcast.26.own_ref, bf16[320,1536]{1,0:T(8,128)(2,1)} %collective-permute-done.6.refs_2_.other_ref, bf16[4,96,1536]{2,1,0:T(8,128)(2,1)} %shard_map.156.refs_0_), custom_call_target="tpu_custom_call" | custom-call | flops 100000000 | bytes 100000 | tf_op jit(solution)/shard_map/pallas_call | solution.py:390
  106.1 2.7 %add_convert_fusion.refs_8_ = bf16[4,96,1536]{2,1,0:T(8,128)(2,1)} fusion(bf16[4,96,1536]{2,1,0:T(8,128)(2,1)S(1)} %collective-permute-done.11, bf16[4,96,1536]{2,1,0:T(8,128)(2,1)} %shard_map.157), kind=kLoop, calls=%fused_computation.2 | loop fusion | flops 2359296 | bytes 3538944 | tf_op jit(solution)/shard_map/convert_element_type | solution.py:529
  108.7 5.3 %all-to-all-start.2 = ((bf16[4,96,1536]{2,1,0:T(8,128)(2,1)}), bf16[4,96,1536]{2,1,0:T(8,128)(2,1)S(1)}, u32[]{:S(2)}, u32[]{:S(2)}) async-start(bf16[4,96,1536]{2,1,0:T(8,128)(2,1)} %add_convert_fusion.refs_8_), calls=%async_computation.2 | async-start | bytes 2359296 | tf_op jit(solution)/shard_map/all_to_all | solution.py:530
  114.6 0.8 fusion.30
  116.0 14.9 %shard_map.158 = (bf16[128,12288]{1,0:T(8,128)(2,1)}, bf16[3,128,768]{2,1,0:T(8,128)(2,1)}, f32[288,512]{1,0:T(8,128)}, f32[288,128]{1,0:T(8,128)}, f32[8,128]{1,0:T(8,128)}) custom-call(s32[11]{0:T(128)} %stack.68.where_ref, bf16[288,512]{1,0:T(8,128)(2,1)} %get-tuple-element.22.refs_0_, ...), custom_call_target="tpu_custom_call", output_to_operand_aliasing={{0}: (8, {})} | custom-call | flops 1500000000 | bytes 1500000 | tf_op jit(solution)/shard_map/pallas_call | solution.py:333
  131.0 1.1 slice_add_fusion
  132.1 1.0 copy-done.3
  133.1 1.6 pad_maximum_fusion.1
  134.7 3.3 %collective-permute-start.17 = (f32[32,576]{1,0:T(8,128)}, f32[32,576]{1,0:T(8,128)}, u32[]{:S(2)}, u32[]{:S(2)}) collective-permute-start(f32[32,576]{1,0:T(8,128)} %pad_maximum_fusion.1), channel_id=1, source_target_pairs={{32,0},{48,16},{64,32},{80,48},{96,64},{112,80},{128,96},{144,112}... | collective-permute-start | bytes 221192 | tf_op jit(solution)/shard_map/ppermute | solution.py:551
  138.0 1.5 convert_reduce_fusion
  140.4 8.0 %all-to-all-start.3 = ((f32[16,1,6]{2,1,0:T(1,128)}), f32[16,1,6]{2,1,0:T(1,128)}, u32[]{:S(2)}, u32[]{:S(2)}) async-start(f32[16,1,6]{2,1,0:T(1,128)} %bitcast.38), calls=%async_computation.3 | async-start | bytes 16384 | tf_op jit(solution)/shard_map/all_to_all | solution.py:561
  148.4 0.9 fusion.10
  150.1 1.4 fusion.5
  151.6 0.8 copy-done.6
  152.4 3.0 %shard_map.159 = bf16[128,12288]{1,0:T(8,128)(2,1)} custom-call(s32[11]{0:T(128)} %stack.68.where_ref, bf16[128,12288]{1,0:T(8,128)(2,1)} %get-tuple-element.33.grid_ref, f32[1,96]{1,0:T(1,128)} %bitcast.86, bf16[3,128,768]{2,1,0:T(8,128)(2,1)} %copy-done.6, bf16[2,128,768]{2,1,0:T(8,128)(2,1)} %collective-permute-done.15.refs_1_, ...), custom_call_target="tpu_custom_call", output_to_operand_aliasing={{}: (1, {})} | custom-call | flops 1000000 | bytes 1000000 | tf_op jit(solution)/shard_map/pallas_call | solution.py:163
  155.4 1.3 all-to-all-done.3
  157.2 1.4 reduce.19
  159.5 1.0 add_convert_fusion.1
  (109 shorter events, 11.1 us)
Async XLA Ops:
  0.6 11.3 %copy-start = (bf16[1,128,5120]{2,1,0:T(8,128)(2,1)S(1)}, bf16[1,128,5120]{2,1,0:T(8,128)(2,1)}, u32[]{:S(2)}) copy-start(bf16[1,128,5120]{2,1,0:T(8,128)(2,1)} %param.17) | copy-start | bytes 3932164
  0.6 7.9 %copy-start.14 = (s32[1,128,6]{1,0,2:T(1,128)S(1)}, s32[1,128,6]{1,0,2:T(1,128)}, u32[]{:S(2)}) copy-start(s32[1,128,6]{1,0,2:T(1,128)} %param.18) | copy-start | bytes 9220
  0.7 10.1 %copy-start.13 = (bf16[1,128,6]{1,2,0:T(8,128)(2,1)S(1)}, bf16[1,128,6]{1,2,0:T(8,128)(2,1)}, u32[]{:S(2)}) copy-start(bf16[1,128,6]{1,2,0:T(8,128)(2,1)} %param.19) | copy-start | bytes 4612
  0.7 13.3 %collective-permute-start.2 = (bf16[128,12288]{1,0:T(8,128)(2,1)}, bf16[128,12288]{1,0:T(8,128)(2,1)}, u32[]{:S(2)}, u32[]{:S(2)}) collective-permute-start(bf16[128,12288]{1,0:T(8,128)(2,1)} %bitcast.70), channel_id=1, source_target_pairs={{0,16},{16,0},{32,48},{48,32},{64,80},{80,64},{96,112},{112,96},{1... | collective-permute-start | bytes 9437192 | tf_op jit(solution)/shard_map/ppermute | solution.py:461
  0.8 42.8 %collective-permute-start.3 = (bf16[128,8192]{1,0:T(8,128)(2,1)}, bf16[128,8192]{1,0:T(8,128)(2,1)}, u32[]{:S(2)}, u32[]{:S(2)}) collective-permute-start(bf16[128,8192]{1,0:T(8,128)(2,1)} %bitcast.78), channel_id=1, source_target_pairs={{0,16},{16,0},{32,48},{48,32},{64,80},{80,64},{96,112},{112,96},{1... | collective-permute-start | bytes 6291464 | tf_op jit(solution)/shard_map/ppermute | solution.py:462
  3.5 34.3 %collective-permute-start.4 = (bf16[1024,512]{1,0:T(8,128)(2,1)}, bf16[1024,512]{1,0:T(8,128)(2,1)}, u32[]{:S(2)}, u32[]{:S(2)}) collective-permute-start(bf16[1024,512]{1,0:T(8,128)(2,1)} %shard_map.148.refs_7_.refs_8_.refs_1_.refs_2_), channel_id=1, source_target_pairs={{0,64},{16,80},{32,96},{48,112},{64,128},{80,144},{96,160},{112,17... | collective-permute-start | bytes 3145736 | tf_op jit(solution)/shard_map/ppermute | solution.py:458
  5.0 34.3 %collective-permute-start.5 = (bf16[1024,512]{1,0:T(8,128)(2,1)}, bf16[1024,512]{1,0:T(8,128)(2,1)}, u32[]{:S(2)}, u32[]{:S(2)}) collective-permute-start(bf16[1024,512]{1,0:T(8,128)(2,1)} %shard_map.148.refs_7_.refs_8_.refs_1_.refs_2_), channel_id=1, source_target_pairs={{0,192},{16,208},{32,224},{48,240},{64,0},{80,16},{96,32},{112,48}... | collective-permute-start | bytes 3145736 | tf_op jit(solution)/shard_map/ppermute | solution.py:459
  5.8 37.2 %collective-permute-start.7 = (bf16[1024,512]{1,0:T(8,128)(2,1)}, bf16[1024,512]{1,0:T(8,128)(2,1)}, u32[]{:S(2)}, u32[]{:S(2)}) collective-permute-start(bf16[1024,512]{1,0:T(8,128)(2,1)} %shard_map.148.refs_7_.refs_8_.refs_1_.refs_2_), channel_id=1, source_target_pairs={{0,40},{1,41},{2,42},{3,43},{4,44},{5,45},{6,46},{7,47},{8,32},{9,... | collective-permute-start | bytes 3145736 | tf_op jit(solution)/shard_map/ppermute | solution.py:460
  9.3 1.8 %copy-start.27 = (s32[96]{0:T(128)}, s32[96]{0:T(128)S(1)}, u32[]{:S(2)}) copy-start(s32[96]{0:T(128)S(1)} %get-tuple-element.75) | copy-start | bytes 1156
  10.8 0.6 copy-start.21
  10.8 0.6 copy-start.23
  11.4 0.6 copy-start.9
  13.9 49.4 %all-to-all-start = ((bf16[16,248,128]{2,1,0:T(8,128)(2,1)}), bf16[16,248,128]{2,1,0:T(8,128)(2,1)S(1)}, u32[]{:S(2)}, u32[]{:S(2)}) async-start(bf16[16,248,128]{2,1,0:T(8,128)(2,1)} %shard_map.151), calls=%async_computation | async-start | bytes 2031616 | tf_op jit(solution)/shard_map/all_to_all | solution.py:491
  24.2 1.6 collective-permute-start
  25.8 10.1 %copy-start.8 = (bf16[128,640]{1,0:T(8,128)(2,1)}, bf16[128,640]{1,0:T(8,128)(2,1)S(1)}, u32[]{:S(2)}) copy-start(bf16[128,640]{1,0:T(8,128)(2,1)S(1)} %collective-permute-done.twin_ref) | copy-start | bytes 491524
  26.6 8.5 %collective-permute-start.1 = (bf16[32,640]{1,0:T(8,128)(2,1)S(1)}, bf16[32,640]{1,0:T(8,128)(2,1)S(1)}, u32[]{:S(2)}, u32[]{:S(2)}) collective-permute-start(bf16[32,640]{1,0:T(8,128)(2,1)S(1)} %slice_select_fusion), channel_id=1, source_target_pairs={{0,32},{16,48},{32,64},{48,80},{64,96},{80,112},{96,128},{112,144}... | collective-permute-start | bytes 122888 | tf_op jit(solution)/shard_map/ppermute | solution.py:454
  35.1 0.8 copy-start.11
  35.1 28.2 %collective-permute-start.6 = (bf16[320,1536]{1,0:T(8,128)(2,1)}, bf16[320,1536]{1,0:T(8,128)(2,1)}, u32[]{:S(2)}, u32[]{:S(2)}) collective-permute-start(bf16[320,1536]{1,0:T(8,128)(2,1)} %bitcast.26.own_ref), channel_id=1, source_target_pairs={{0,32},{16,48},{32,0},{48,16},{64,96},{80,112},{96,64},{112,80},{1... | collective-permute-start | bytes 2949128 | tf_op jit(solution)/shard_map/ppermute | solution.py:464
  37.8 38.1 %collective-permute-start.8 = (bf16[1024,512]{1,0:T(8,128)(2,1)}, bf16[1024,512]{1,0:T(8,128)(2,1)}, u32[]{:S(2)}, u32[]{:S(2)}) collective-permute-start(bf16[1024,512]{1,0:T(8,128)(2,1)} %collective-permute-done.4.refs_9_.refs_10_), channel_id=1, source_target_pairs={{0,64},{16,80},{32,96},{48,112},{64,128},{80,144},{96,160},{112,17... | collective-permute-start | bytes 3145736 | tf_op jit(solution)/shard_map/ppermute | solution.py:496
  39.3 52.4 %collective-permute-start.9 = (bf16[1024,512]{1,0:T(8,128)(2,1)}, bf16[1024,512]{1,0:T(8,128)(2,1)}, u32[]{:S(2)}, u32[]{:S(2)}) collective-permute-start(bf16[1024,512]{1,0:T(8,128)(2,1)} %collective-permute-done.4.refs_9_.refs_10_), channel_id=1, source_target_pairs={{0,40},{1,41},{2,42},{3,43},{4,44},{5,45},{6,46},{7,47},{8,32},{9,... | collective-permute-start | bytes 3145736 | tf_op jit(solution)/shard_map/ppermute | solution.py:498
  43.0 45.8 %collective-permute-start.10 = (bf16[1024,512]{1,0:T(8,128)(2,1)}, bf16[1024,512]{1,0:T(8,128)(2,1)S(1)}, u32[]{:S(2)}, u32[]{:S(2)}) collective-permute-start(bf16[1024,512]{1,0:T(8,128)(2,1)} %collective-permute-done.7.refs_9_.refs_10_), channel_id=1, source_target_pairs={{0,192},{16,208},{32,224},{48,240},{64,0},{80,16},{96,32},{112,48}... | collective-permute-start | bytes 3145736 | tf_op jit(solution)/shard_map/ppermute | solution.py:497
  63.3 1.0 copy-start.5
  71.1 20.7 %all-to-all-start.1 = ((bf16[8,192,320]{2,1,0:T(8,128)(2,1)}), bf16[8,192,320]{2,1,0:T(8,128)(2,1)S(1)}, u32[]{:S(2)}, u32[]{:S(2)}) async-start(bf16[8,192,320]{2,1,0:T(8,128)(2,1)} %bitcast.76), calls=%async_computation.1 | async-start | bytes 2359296 | tf_op jit(solution)/shard_map/all_to_all | solution.py:507
  88.8 1.0 copy-start.2
  91.8 1.1 copy-start.4
  97.6 8.5 %collective-permute-start.11 = (bf16[4,96,1536]{2,1,0:T(8,128)(2,1)}, bf16[4,96,1536]{2,1,0:T(8,128)(2,1)S(1)}, u32[]{:S(2)}, u32[]{:S(2)}) collective-permute-start(bf16[4,96,1536]{2,1,0:T(8,128)(2,1)} %shard_map.156.refs_0_), channel_id=1, source_target_pairs={{0,16},{16,0},{32,48},{48,32},{64,80},{80,64},{96,112},{112,96},{1... | collective-permute-start | bytes 3538952 | tf_op jit(solution)/shard_map/ppermute | solution.py:527
  97.7 18.3 %collective-permute-start.12 = (bf16[512,512]{1,0:T(8,128)(2,1)}, bf16[512,512]{1,0:T(8,128)(2,1)}, u32[]{:S(2)}, u32[]{:S(2)}) collective-permute-start(bf16[512,512]{1,0:T(8,128)(2,1)} %slice.116.refs_2_), channel_id=1, source_target_pairs={{0,192},{16,208},{32,224},{48,240},{64,0},{80,16},{96,32},{112,48}... | collective-permute-start | bytes 1572872 | tf_op jit(solution)/shard_map/ppermute | solution.py:520
  99.1 16.9 %collective-permute-start.13 = (bf16[512,512]{1,0:T(8,128)(2,1)}, bf16[512,512]{1,0:T(8,128)(2,1)}, u32[]{:S(2)}, u32[]{:S(2)}) collective-permute-start(bf16[512,512]{1,0:T(8,128)(2,1)} %shard_map.155.refs_3_), channel_id=1, source_target_pairs={{0,40},{1,41},{2,42},{3,43},{4,44},{5,45},{6,46},{7,47},{8,32},{9,... | collective-permute-start | bytes 1572872 | tf_op jit(solution)/shard_map/ppermute | solution.py:521
  108.7 23.4 %all-to-all-start.2 = ((bf16[4,96,1536]{2,1,0:T(8,128)(2,1)}), bf16[4,96,1536]{2,1,0:T(8,128)(2,1)S(1)}, u32[]{:S(2)}, u32[]{:S(2)}) async-start(bf16[4,96,1536]{2,1,0:T(8,128)(2,1)} %add_convert_fusion.refs_8_), calls=%async_computation.2 | async-start | bytes 2359296 | tf_op jit(solution)/shard_map/all_to_all | solution.py:530
  114.1 37.5 %collective-permute-start.14 = (bf16[3,128,768]{2,1,0:T(8,128)(2,1)}, bf16[3,128,768]{2,1,0:T(8,128)(2,1)S(1)}, u32[]{:S(2)}, u32[]{:S(2)}) collective-permute-start(bf16[3,128,768]{2,1,0:T(8,128)(2,1)} %get-tuple-element.34), channel_id=1, source_target_pairs={{0,16},{16,0},{32,48},{48,32},{64,80},{80,64},{96,112},{112,96},{1... | collective-permute-start | bytes 1769480 | tf_op jit(solution)/shard_map/ppermute | solution.py:515
  114.1 37.5 %collective-permute-start.15 = (bf16[2,128,768]{2,1,0:T(8,128)(2,1)}, bf16[2,128,768]{2,1,0:T(8,128)(2,1)}, u32[]{:S(2)}, u32[]{:S(2)}) collective-permute-start(bf16[2,128,768]{2,1,0:T(8,128)(2,1)} %get-tuple-element.35), channel_id=1, source_target_pairs={{0,16},{16,0},{32,48},{48,32},{64,80},{80,64},{96,112},{112,96},{1... | collective-permute-start | bytes 1179656 | tf_op jit(solution)/shard_map/ppermute | solution.py:514
  130.9 20.7 %collective-permute-start.16 = (bf16[3,128,768]{2,1,0:T(8,128)(2,1)}, bf16[3,128,768]{2,1,0:T(8,128)(2,1)}, u32[]{:S(2)}, u32[]{:S(2)}) collective-permute-start(bf16[3,128,768]{2,1,0:T(8,128)(2,1)} %get-tuple-element.36), channel_id=1, source_target_pairs={{0,16},{16,0},{32,48},{48,32},{64,80},{80,64},{96,112},{112,96},{1... | collective-permute-start | bytes 1769480 | tf_op jit(solution)/shard_map/ppermute | solution.py:546
  132.1 1.0 copy-start.3
  133.1 6.4 %copy-start.7 = (bf16[1,1,96,1536]{3,2,1,0:T(8,128)(2,1)S(1)}, bf16[1,1,96,1536]{3,2,1,0:T(8,128)(2,1)}, u32[]{:S(2)}) copy-start(bf16[1,1,96,1536]{3,2,1,0:T(8,128)(2,1)} %param.20) | copy-start | bytes 884740
  133.1 15.2 %copy-start.1 = (f32[288,512]{1,0:T(8,128)S(1)}, f32[288,512]{1,0:T(8,128)}, u32[]{:S(2)}) copy-start(f32[288,512]{1,0:T(8,128)} %shard_map.160) | copy-start | bytes 1769476
  134.7 13.7 %collective-permute-start.17 = (f32[32,576]{1,0:T(8,128)}, f32[32,576]{1,0:T(8,128)}, u32[]{:S(2)}, u32[]{:S(2)}) collective-permute-start(f32[32,576]{1,0:T(8,128)} %pad_maximum_fusion.1), channel_id=1, source_target_pairs={{32,0},{48,16},{64,32},{80,48},{96,64},{112,80},{128,96},{144,112}... | collective-permute-start | bytes 221192 | tf_op jit(solution)/shard_map/ppermute | solution.py:551
  139.7 8.8 %copy-start.12 = (f32[96]{0:T(128)}, f32[96]{0:T(128)S(1)}, u32[]{:S(2)}) copy-start(f32[96]{0:T(128)S(1)} %fusion.4) | copy-start | bytes 1156
  140.4 16.4 %all-to-all-start.3 = ((f32[16,1,6]{2,1,0:T(1,128)}), f32[16,1,6]{2,1,0:T(1,128)}, u32[]{:S(2)}, u32[]{:S(2)}) async-start(f32[16,1,6]{2,1,0:T(1,128)} %bitcast.38), calls=%async_computation.3 | async-start | bytes 16384 | tf_op jit(solution)/shard_map/all_to_all | solution.py:561
  150.1 9.4 %collective-permute-start.18 = (f32[128,576]{1,0:T(8,128)}, f32[128,576]{1,0:T(8,128)}, u32[]{:S(2)}, u32[]{:S(2)}) collective-permute-start(f32[128,576]{1,0:T(8,128)} %fusion.7), channel_id=1, source_target_pairs={{0,16},{16,0},{32,48},{48,32},{64,80},{80,64},{96,112},{112,96},{1... | collective-permute-start | bytes 884744 | tf_op jit(solution)/shard_map/ppermute | solution.py:556
  151.5 0.8 copy-start.6
  152.4 6.3 %copy-start.10 = (pred[128,96]{0,1:T(32,128)(4,1)S(1)}, pred[128,96]{0,1:T(32,128)(4,1)}, u32[]{:S(2)}) copy-start(pred[128,96]{0,1:T(32,128)(4,1)} %copy-done.9) | copy-start | bytes 36868
  152.4 6.3 %copy-start.16 = (s32[128]{0:T(128)S(1)}, s32[128]{0:T(128)}, u32[]{:S(2)}) copy-start(s32[128]{0:T(128)} %copy-done.15) | copy-start | bytes 1540
  152.4 6.4 %copy-start.18 = (s32[128]{0:T(128)S(1)}, s32[128]{0:T(128)}, u32[]{:S(2)}) copy-start(s32[128]{0:T(128)} %copy-done.17) | copy-start | bytes 1540
  152.4 6.4 %copy-start.20 = (s32[128]{0:T(128)S(1)}, s32[128]{0:T(128)}, u32[]{:S(2)}) copy-start(s32[128]{0:T(128)} %copy-done.19) | copy-start | bytes 1540
  152.4 6.4 %copy-start.22 = (s32[128]{0:T(128)S(1)}, s32[128]{0:T(128)}, u32[]{:S(2)}) copy-start(s32[128]{0:T(128)} %copy-done.21) | copy-start | bytes 1540
  152.4 6.4 %copy-start.24 = (s32[128]{0:T(128)S(1)}, s32[128]{0:T(128)}, u32[]{:S(2)}) copy-start(s32[128]{0:T(128)} %copy-done.23) | copy-start | bytes 1540
  152.4 6.4 %copy-start.26 = (s32[128]{0:T(128)S(1)}, s32[128]{0:T(128)}, u32[]{:S(2)}) copy-start(s32[128]{0:T(128)} %copy-done.25) | copy-start | bytes 1540
  152.4 6.4 %copy-start.28 = (s32[96]{0:T(128)S(1)}, s32[96]{0:T(128)}, u32[]{:S(2)}) copy-start(s32[96]{0:T(128)} %copy-done.27) | copy-start | bytes 1156
  (4 other events, 2.2 us)
